TPU v7x, 512 devices: a whole 4x4x16 slice. The times are simulated.
512 devices in a mesh: mem: 64 (over z, y_lo, core), tile: 8 (over y_hi, x).
Axes of the slice: x: 4, y: 4 (y_hi: 2, y_lo: 2; y = y_hi * 2 + y_lo), z: 16, core: 2. Of those that a mesh axis runs over, the one named last changes fastest.
Arguments:
- background: float32 [2, 256, 1024], P(None, 'tile'), may hold values from -6 to 6
- anomalies: float32 [64, 2, 256, 1024], P('mem', None, 'tile'), may hold values from -6 to 6
- courant_lon: float32 [2, 256, 1024], P(None, 'tile'), may hold values from -0.12 to 0.12
- courant_lat: float32 [2, 256, 1024], P(None, 'tile'), may hold values from -0.85 to 0.85
- obs_value: float32 [32768], P('tile'), may hold values from -12 to 12
- obs_weight: float32 [32768], P('tile'), may hold values from 0.015 to 0.15
- obs_column: int32 [32768], P('tile'), may hold values from 0 to 32767
- obs_level: int32 [32768], P('tile'), may hold values from 0 to 1
Outputs:
- increment: float32 [2, 256, 1024], P(None, 'tile')
All inputs are finite; a program needn't handle non-finite values.
Results may differ from a plain program's by a relative error of at most 0.00026.
Values sent between devices are 32-bit elements; how exact they have to be, the bound alone decides.
No kernel may reach another device: no remote copies, remote signals or barrier semaphores. Data moves between devices by JAX's collectives and lax.ppermute only.
A program may use at most 64 MiB of HBM per device.

v0:
```python
import jax
import jax.numpy as jnp
from jax import lax
from jax.sharding import PartitionSpec as P

NSTEP = 8
ITERS = 2


bundle_scale = 0.5
quad_coef = 0.25
speed_base = 0.85
speed_gain = 0.15


def padded_2(block, sides, width):
    for axis, dim in sides:
        count = lax.axis_size(axis)
        forward = [(i, i + 1) for i in range(count - 1)]
        backward = [(target, source) for source, target in forward]
        low = lax.ppermute(
            lax.slice_in_dim(block, block.shape[dim] - width, None, axis=dim), axis, forward
        )
        high = lax.ppermute(lax.slice_in_dim(block, 0, width, axis=dim), axis, backward)
        block = jnp.concatenate([low, block, high], axis=dim)
    return block


def advance(field, south, north, courants):
    west = jnp.roll(field, 1, axis=2)
    east = jnp.roll(field, -1, axis=2)
    factor = speed_base + speed_gain * jnp.tanh(field)
    along_lon = factor * courants[0]
    along_lat = factor * courants[1]
    zonal_flux = jnp.maximum(along_lon, 0.0) * (field - west) + jnp.minimum(along_lon, 0.0) * (
        east - field
    )
    merid_flux = jnp.maximum(along_lat, 0.0) * (field - south) + jnp.minimum(along_lat, 0.0) * (
        north - field
    )
    return field - zonal_flux - merid_flux


def propagate(field, courants):
    for sweep_index in range(NSTEP):
        padded = padded_2(field, (("tile", 1),), 1)
        field = advance(field, padded[:, :-2, :], padded[:, 2:, :], courants)
    return field


def sample(state, flat_index):
    return state.reshape(-1)[flat_index]


def apply_obs(sampled):
    return sampled + quad_coef * sampled * sampled


def normal_terms(observed, obs_value, obs_weight):
    center = jnp.mean(observed, axis=0)
    spread = (observed - center[None, :]) / bundle_scale * obs_weight[None, :]
    misfit = (obs_value - center) * obs_weight
    gram_mat = jnp.dot(spread, spread.T, precision=lax.Precision.HIGHEST)
    project = jnp.dot(spread, misfit, precision=lax.Precision.HIGHEST)
    return (gram_mat, project)


def newton_update(weights, gram_mat, project):
    members = weights.shape[0]
    hessian = gram_mat + (members - 1) * jnp.eye(members, dtype=jnp.float32)
    gradient = (members - 1) * weights - project
    chol_low = jnp.linalg.cholesky(hessian)
    forward_sol = lax.linalg.triangular_solve(
        chol_low, gradient[:, None], left_side=True, lower=True
    )
    solved = lax.linalg.triangular_solve(
        chol_low, forward_sol, left_side=True, lower=True, transpose_a=True
    )
    return weights - solved[:, 0]


def member_sum(weights, own, member_index):
    return lax.psum(weights[member_index] * own, "mem")


def local(
    background, anomalies, courant_lon, courant_lat, obs_value, obs_weight, obs_column, obs_level
):
    own = anomalies[0]
    members = lax.axis_size("mem")
    member_index = lax.axis_index("mem")
    cells = background.shape[1] * background.shape[2]
    courants = jnp.stack([courant_lon, courant_lat])
    flat_index = obs_level * cells + obs_column
    weights = jnp.zeros((members,), jnp.float32)
    for iteration in range(ITERS):
        state = background + bundle_scale * own
        if iteration > 0:
            state = state + member_sum(weights, own, member_index)
        own_obs = apply_obs(sample(propagate(state, courants), flat_index))
        observed = lax.all_gather(own_obs[None, :], "mem", axis=0, tiled=True)
        gram_mat, project = normal_terms(observed, obs_value, obs_weight)
        gram_mat, project = lax.psum((gram_mat, project), "tile")
        weights = newton_update(weights, gram_mat, project)
    return member_sum(weights, own, member_index)


def solution(mesh):
    return jax.shard_map(
        local,
        mesh=mesh,
        in_specs=(
            P(None, "tile", None),
            P("mem", None, "tile", None),
            P(None, "tile", None),
            P(None, "tile", None),
            P("tile"),
            P("tile"),
            P("tile"),
            P("tile"),
        ),
        out_specs=P(None, "tile", None),
        check_vma=False,
    )
```

profile of v0, /device:TPU:1, one launch (start us, length us, event | category | flops | bytes accessed | tf_op | source)
XLA Modules:
  0.0 1405.6 jit_solution(1391592101823370460)
XLA Ops:
  25.2 7.0 collective-permute-start.4
  37.0 5.5 collective-permute-start.6
  47.3 5.5 collective-permute-start.8
  57.7 5.5 collective-permute-start.10
  68.0 5.5 collective-permute-start.12
  78.4 5.5 collective-permute-start.14
  88.6 23.0 %gather_fusion = f32[4096]{0:T(1024)S(1)} fusion(f32[65536]{0:T(1024)S(1)} %bitcast.100, s32[4096]{0:T(1024)S(1)} %fusion.188), kind=kCustom, calls=%fused_computation | custom fusion | bytes 49152 | tf_op jit(solution)/shard_map/gather | solution.py:52
  112.4 137.6 %all-gather.5.cloned.1.call-done = f32[64,1,4096]{2,1,0:T(1,128)} async-done(((f32[1,1,4096]{2,1,0:T(1,128)}), f32[64,1,4096]{2,1,0:T(1,128)}) %all-gather.5.cloned.1.call-update) | async-done | bytes 1048592 | tf_op jit(solution)/shard_map/all_gather | solution.py:101
  255.7 34.6 %all-reduce.1 = (f32[64,64]{0,1:T(8,128)S(1)}, f32[64]{0:T(128)S(1)}) all-reduce(f32[64,64]{0,1:T(8,128)S(1)} %fusion.5, f32[64]{0:T(128)S(1)} %convolution_bitcast_fusion.1), channel_id=1, replica_groups=mesh['mem'=64,'tile'=8] {'tile'}, use_global_device_ids=true, to_apply=%region_1.2 | all-reduce | flops 4160 | bytes 33280 | tf_op jit(solution)/shard_map/psum | solution.py:103
  290.4 5.8 cholesky.44
  297.6 4.9 custom-call.11
  304.8 402.5 %all-reduce.5.cloned.1.call-done = f32[2,32,1024]{2,1,0:T(8,128)} async-done(((f32[2,32,1024]{2,1,0:T(8,128)}), f32[2,32,1024]{2,1,0:T(8,128)}) %all-reduce.5.cloned.1.call-update) | async-done | bytes 262160 | tf_op jit(solution)/shard_map/psum | solution.py:83
  724.7 7.0 collective-permute-start.20
  736.5 5.5 collective-permute-start.22
  746.8 5.5 collective-permute-start.24
  757.2 5.5 collective-permute-start.26
  767.6 5.5 collective-permute-start.28
  777.9 5.5 collective-permute-start.30
  788.2 23.0 %gather_fusion.1 = f32[4096]{0:T(1024)S(1)} fusion(f32[65536]{0:T(1024)S(1)} %bitcast.99, s32[4096]{0:T(1024)S(1)} %fusion.188), kind=kCustom, calls=%fused_computation.1 | custom fusion | bytes 49152 | tf_op jit(solution)/shard_map/gather | solution.py:52
  811.9 128.3 %all-gather.7.cloned.1.call-done = f32[64,1,4096]{2,1,0:T(1,128)} async-done(((f32[1,1,4096]{2,1,0:T(1,128)}), f32[64,1,4096]{2,1,0:T(1,128)}) %all-gather.7.cloned.1.call-update) | async-done | bytes 1048592 | tf_op jit(solution)/shard_map/all_gather | solution.py:101
  945.9 34.4 %all-reduce = (f32[64,64]{0,1:T(8,128)S(1)}, f32[64]{0:T(128)S(1)}) all-reduce(f32[64,64]{0,1:T(8,128)S(1)} %fusion.8, f32[64]{0:T(128)S(1)} %convolution_bitcast_fusion), channel_id=1, replica_groups=mesh['mem'=64,'tile'=8] {'tile'}, use_global_device_ids=true, to_apply=%region_7.0 | all-reduce | flops 4160 | bytes 33280 | tf_op jit(solution)/shard_map/psum | solution.py:103
  980.5 5.8 cholesky.55
  987.7 4.9 custom-call.13
  994.8 402.6 %all-reduce.7.cloned.1.call-done = f32[2,32,1024]{2,1,0:T(8,128)} async-done(((f32[2,32,1024]{2,1,0:T(8,128)}), f32[2,32,1024]{2,1,0:T(8,128)}) %all-reduce.7.cloned.1.call-update) | async-done | bytes 262160 | tf_op jit(solution)/shard_map/psum | solution.py:83
  (178 shorter events, 114.9 us)
Async XLA Ops:
  6.5 243.4 %all-gather.5.cloned.1.call-start = ((), (), s32[]{:S(2)}) async-start(), calls=%async_computation.2 | async-start | bytes 1064960 | tf_op jit(solution)/shard_map/all_gather | solution.py:101
  7.6 6.2 collective-permute-start
  16.4 4.5 collective-permute-start.2
  19.5 5.2 collective-permute-start.3
  25.2 8.4 collective-permute-start.4
  32.2 4.4 collective-permute-start.5
  37.0 6.9 collective-permute-start.6
  42.5 4.4 collective-permute-start.7
  47.3 6.9 collective-permute-start.8
  57.7 6.9 collective-permute-start.10
  68.0 6.9 collective-permute-start.12
  78.4 6.9 collective-permute-start.14
  112.3 595.0 %all-reduce.5.cloned.1.call-start = ((), (), s32[]{:S(2)}) async-start(), calls=%async_computation | async-start | bytes 524288 | tf_op jit(solution)/shard_map/psum | solution.py:83
  304.7 635.5 %all-gather.7.cloned.1.call-start = ((), (), s32[]{:S(2)}) async-start(), calls=%async_computation.3 | async-start | bytes 1064960 | tf_op jit(solution)/shard_map/all_gather | solution.py:101
  708.5 4.7 collective-permute-start.16
  716.4 4.5 collective-permute-start.18
  719.5 4.8 collective-permute-start.19
  724.7 8.4 collective-permute-start.20
  736.5 6.9 collective-permute-start.22
  746.8 6.9 collective-permute-start.24
  757.2 6.9 collective-permute-start.26
  767.6 6.9 collective-permute-start.28
  777.9 6.9 collective-permute-start.30
  811.9 585.5 %all-reduce.7.cloned.1.call-start = ((), (), s32[]{:S(2)}) async-start(), calls=%async_computation.1 | async-start | bytes 524288 | tf_op jit(solution)/shard_map/psum | solution.py:83
  (21 other events, 392.0 us)
Sparse Core Ops, SparseCore 0:
  112.5 137.4 all-gather.4
  304.9 402.4 all-reduce.4
  812.0 128.1 all-gather.6
  994.9 402.3 all-reduce.6
where the time goes:
time: 1410 us
  waiting for transfers between devices  1120 us (79%)
  starting transfers between devices  103 us (7%)
  blocking collectives  69 us (5%)
  local copies, waits for them, and re-layouts  53.4 us (4%)
  other arithmetic  38.5 us (3%)
    psum x2, waiting for transfers between devices, member_sum(): return lax.psum(weights[member_index] * own, 'mem')  805 us
    all_gather x2, waiting for transfers between devices, local(): observed = lax.all_gather(own_obs[None, :], 'mem', axis=0, tiled=True)  266 us
    ppermute x16, starting transfers between devices, padded_2(): lax.ppermute(lax.slice_in_dim(block, block.shape[dim] - width, None, axis...  82.5 us
    psum x2, blocking collectives, local(): gram_mat, project = lax.psum((gram_mat, project), 'tile')  69 us
    ppermute x16, waiting for transfers between devices, padded_2(): lax.ppermute(lax.slice_in_dim(block, 0, width, axis=dim), axis, backward)  48.5 us
    gather x2, local copies, waits for them, and re-layouts, sample(): return state.reshape(-1)[flat_index]  46.1 us
  transfers between devices with their start and end apart: 36, of which 20 were waited for; matrix products, arithmetic and copies ran while one was open for 0% of the time, Pallas kernels for 0%

commit v1 on v0

v1 whole, which is shorter than its diff:
```python
import functools

import jax
import jax.numpy as jnp
from jax import lax
from jax.experimental import pallas as pl
from jax.experimental.pallas import tpu as pltpu
from jax.sharding import Mesh, PartitionSpec as P

NSTEP = 8
MEMBERS = 64
PAIRS = 32
LEV = 2
CY = 32
NX = 1024
CHUNK = 16
HALO = 8
ROWS = CY + 2 * HALO
LANES = 128
HIGHEST = lax.Precision.HIGHEST

MEM = ("z", "yl", "core")
TILE = ("yh", "x")
PLANE = ("yl", "core", "yh", "x")
VMEM = pl.BlockSpec(memory_space=pltpu.VMEM)
SMEM = pl.BlockSpec(memory_space=pltpu.SMEM)


def lane_of(shape):
    return lax.broadcasted_iota(jnp.int32, shape, len(shape) - 1)


def call(body, out, scratch=(), in_specs=None, vmem=40 << 20):
    return pl.pallas_call(
        body,
        out_shape=out,
        in_specs=in_specs,
        out_specs=jax.tree.map(lambda _: VMEM, out),
        scratch_shapes=list(scratch),
        compiler_params=pltpu.CompilerParams(vmem_limit_bytes=vmem),
    )


def f32(*shape):
    return jax.ShapeDtypeStruct(shape, jnp.float32)


def pack_body(chunk_ref, own_ref, bg_ref, lon_ref, lat_ref, pieces_ref, fields_ref):
    lane = lane_of((16, LANES))
    shifted = []
    for group in range(4):
        half, lev = divmod(group, 2)
        rolled = [
            pltpu.roll(
                own_ref[lev, 16 * half : 16 * half + 16, LANES * b : LANES * b + LANES],
                HALO,
                axis=1,
            )
            for b in range(8)
        ]
        shifted.append([jnp.where(lane < HALO, rolled[b - 1], rolled[b]) for b in range(8)])
    for b in range(8):
        for k in range(8):
            out = None
            for group in range(4):
                amount = (32 * group - CHUNK * k) % LANES
                source = shifted[group][b]
                if k == 7:
                    source = jnp.where(lane < CHUNK, shifted[group][(b + 1) % 8], source)
                moved = pltpu.roll(source, amount, axis=1) if amount else source
                out = moved if out is None else jnp.where(lane >= 32 * group, moved, out)
            pieces_ref[8 * b + k] = out
    chunk = chunk_ref[0]
    b, k = chunk // 8, chunk % 8
    wide = lane_of((CY, LANES))

    def block(ref, lev, index):
        return ref[lev, :, pl.ds(pl.multiple_of(index * LANES, LANES), LANES)]

    for index, ref in enumerate((bg_ref, lon_ref, lat_ref)):
        out = None
        for lev in range(LEV):
            mid = block(ref, lev, b)
            low = block(ref, lev, (b + 7) % 8)
            high = block(ref, lev, (b + 1) % 8)
            mid = jnp.where((wide >= LANES - HALO) & (k == 0), low, mid)
            mid = jnp.where((wide < HALO) & (k == 7), high, mid)
            moved = pltpu.roll(mid, (32 * lev + HALO - CHUNK * k + LANES) % LANES, axis=1)
            out = moved if out is None else jnp.where(wide >= 32, moved, out)
        out = jnp.where(wide < 64, out, pltpu.roll(out, 64, axis=1))
        fields_ref[index] = out


def pair_body(x_ref, fields_ref, mid_ref, low_ref, high_ref):
    lane = lane_of((16, LANES))
    for p in range(PAIRS):
        first, second = x_ref[p], x_ref[p + PAIRS]
        upper = jnp.where(lane < 64, first, pltpu.roll(second, 64, axis=1))
        lower = jnp.where(lane < 64, pltpu.roll(first, 64, axis=1), second)
        mid_ref[p, 0:16] = upper
        mid_ref[p, 16:32] = lower
        low_ref[p] = upper[0:HALO]
        high_ref[p] = lower[HALO:16]
    for index in range(3):
        low_ref[PAIRS + index] = fields_ref[index, 0:HALO]
        high_ref[PAIRS + index] = fields_ref[index, CY - HALO : CY]


def cells_body(chunk_ref, value_ref, weight_ref, column_ref, level_ref, out_ref):
    chunk = chunk_ref[0]
    column = column_ref[...]
    row = column // NX
    offset = column % NX - CHUNK * chunk
    inside = (offset >= 0) & (offset < CHUNK)
    lane = jnp.where(inside, level_ref[...] * 32 + HALO + offset, -1)
    square = weight_ref[...] * weight_ref[...]
    nobs = column.shape[1]
    at_row = lax.broadcasted_iota(jnp.int32, (CY, nobs), 0) == row
    at_lane = (lax.broadcasted_iota(jnp.int32, (LANES, nobs), 0) == lane).astype(jnp.bfloat16)
    parts = []
    for value in (square, square * value_ref[...]):
        left = jnp.where(at_row, value, 0.0)
        for _ in range(3):
            part = left.astype(jnp.bfloat16)
            parts.append(part)
            left = left - part.astype(jnp.float32)
    sums = lax.dot_general(
        jnp.concatenate(parts, axis=0),
        at_lane,
        (((1,), (1,)), ((), ())),
        preferred_element_type=jnp.float32,
    )
    for index in range(2):
        base = 3 * CY * index
        total = sums[base : base + CY] + sums[base + CY : base + 2 * CY]
        total = total + sums[base + 2 * CY : base + 3 * CY]
        out_ref[index] = total


def transport(base, anoms_ref, coefs, count, first):
    state = base + 0.5 * anoms_ref[pl.ds(first, count)]
    west_c, east_c, south_c, north_c, own_c = coefs
    for _ in range(NSTEP):
        west = pltpu.roll(state, 1, axis=2)
        east = pltpu.roll(state, LANES - 1, axis=2)
        south = pltpu.roll(state, 1, axis=1)
        north = pltpu.roll(state, ROWS - 1, axis=1)
        speed = 0.85 + 0.15 * jnp.tanh(state)
        change = west_c[...] * west + east_c[...] * east
        change = change + (south_c[...] * south + north_c[...] * north)
        state = state + speed * (change - own_c[...] * state)
    return state


def observe_and_gram(base, anoms_ref, coefs, cells_ref, gram_ref, obs_ref, dev_ref, left_ref, right_ref):
    group = 4

    def one(index, total):
        first = index * group
        state = transport(base, anoms_ref, coefs, group, first)[:, HALO : HALO + CY]
        seen = state + 0.25 * state * state
        obs_ref[pl.ds(first, group)] = seen
        return total + jnp.sum(seen, axis=0)

    total = lax.fori_loop(0, PAIRS // group, one, jnp.zeros((CY, LANES), jnp.float32))
    center = (total + pltpu.roll(total, 64, axis=1)) * (1.0 / MEMBERS)
    lane = lane_of((16, LANES))
    for p in range(PAIRS):
        dev = obs_ref[p] - center
        upper, lower = dev[0:16], dev[16:32]
        dev_ref[16 * p : 16 * p + 16] = jnp.where(lane < 64, upper, pltpu.roll(lower, 64, axis=1))
        at = 16 * (p + PAIRS)
        dev_ref[at : at + 16] = jnp.where(lane < 64, pltpu.roll(upper, 64, axis=1), lower)
    weight, weighted = cells_ref[0], cells_ref[1]
    aim = 2.0 * (weighted - weight * center)
    aim = jnp.where(lane < 64, aim[0:16], pltpu.roll(aim[16:32], 64, axis=1))
    weight = 4.0 * weight
    weight = jnp.where(lane < 64, weight[0:16], pltpu.roll(weight[16:32], 64, axis=1))
    right_ref[MEMBERS:LANES, :] = jnp.zeros((LANES - MEMBERS, 16 * LANES), jnp.float32)
    for r in range(16):
        rows = dev_ref[pl.ds(r, MEMBERS, stride=16), :]
        left_ref[:, LANES * r : LANES * r + LANES] = rows
        right_ref[0:MEMBERS, LANES * r : LANES * r + LANES] = rows * weight[r : r + 1]
        right_ref[MEMBERS : MEMBERS + 1, LANES * r : LANES * r + LANES] = aim[r : r + 1]
    gram_ref[...] = lax.dot_general(
        left_ref[...],
        right_ref[...],
        (((1,), (1,)), ((), ())),
        precision=HIGHEST,
        preferred_element_type=jnp.float32,
    )


def fill_coefs(lon, lat, coefs):
    west_c, east_c, south_c, north_c, own_c = coefs
    west_c[...] = jnp.maximum(lon, 0.0)
    east_c[...] = jnp.maximum(-lon, 0.0)
    south_c[...] = jnp.maximum(lat, 0.0)
    north_c[...] = jnp.maximum(-lat, 0.0)
    own_c[...] = jnp.abs(lon) + jnp.abs(lat)


def first_body(mid_ref, low_ref, high_ref, fields_ref, cells_ref, gram_ref, anoms_ref, full_ref, *scratch):
    coefs, rest = scratch[:5], scratch[5:]
    anoms_ref[:, 0:HALO] = low_ref[0:PAIRS]
    anoms_ref[:, HALO : HALO + CY] = mid_ref[...]
    anoms_ref[:, HALO + CY : ROWS] = high_ref[0:PAIRS]
    for index in range(3):
        full_ref[index, 0:HALO] = low_ref[PAIRS + index]
        full_ref[index, HALO : HALO + CY] = fields_ref[index]
        full_ref[index, HALO + CY : ROWS] = high_ref[PAIRS + index]
    fill_coefs(full_ref[1], full_ref[2], coefs)
    observe_and_gram(full_ref[0], anoms_ref, coefs, cells_ref, gram_ref, *rest)


def solve(sums, weights):
    shape = (MEMBERS, LANES)
    lane = lane_of(shape)
    sub = lax.broadcasted_iota(jnp.int32, shape, 0)
    left = MEMBERS - 1.0
    matrix = jnp.where(
        lane < MEMBERS,
        sums + jnp.where(lane == sub, left, 0.0),
        jnp.where(lane == MEMBERS, left * weights - sums, 0.0),
    )
    for k in range(MEMBERS):
        row = matrix[k : k + 1]
        column = jnp.broadcast_to(matrix[:, k : k + 1], shape)
        factor = column / column[k : k + 1]
        matrix = matrix - jnp.where(sub == k, 0.0, factor) * row
    diagonal = jnp.sum(jnp.where(lane == sub, matrix, 0.0), axis=1, keepdims=True)
    solved = matrix[:, MEMBERS : MEMBERS + 1] / diagonal
    return weights - jnp.broadcast_to(solved, shape)


def by_pair(weights):
    lane = lane_of((PAIRS, LANES))
    return jnp.where(lane < 64, weights[0:PAIRS], weights[PAIRS:MEMBERS])


def mix(pair_ref, anoms_ref, low, rows):
    total = jnp.zeros((rows, LANES), jnp.float32)
    for p in range(PAIRS):
        total = total + pair_ref[p : p + 1] * anoms_ref[p, low : low + rows]
    return total + pltpu.roll(total, 64, axis=1)


def second_body(sums_ref, anoms_ref, full_ref, cells_ref, gram_ref, weights_ref, *scratch):
    pair_ref, coefs, rest = scratch[0], scratch[1:6], scratch[6:]
    fill_coefs(full_ref[1], full_ref[2], coefs)
    weights = solve(sums_ref[...], jnp.zeros((MEMBERS, LANES), jnp.float32))
    weights_ref[...] = weights
    pair_ref[...] = by_pair(weights)
    base = full_ref[0] + mix(pair_ref, anoms_ref, 0, ROWS)
    observe_and_gram(base, anoms_ref, coefs, cells_ref, gram_ref, *rest)


def last_body(sums_ref, weights_ref, anoms_ref, out_ref, pair_ref):
    weights = solve(sums_ref[...], weights_ref[...])
    pair_ref[...] = by_pair(weights)
    total = mix(pair_ref, anoms_ref, HALO, CY)
    lane = lane_of((8, LANES))
    out = None
    for group in range(8):
        lev, part = divmod(group, 4)
        moved = pltpu.roll(
            total[8 * part : 8 * part + 8], (CHUNK * group - 32 * lev - HALO) % LANES, axis=1
        )
        out = moved if out is None else jnp.where(lane >= CHUNK * group, moved, out)
    out_ref[...] = out


def spread_body(x_ref, out_ref):
    lane = lane_of((8, LANES))
    for b in range(8):
        pieces = [x_ref[8 * b + k] for k in range(8)]
        for group in range(8):
            lev, part = divmod(group, 4)
            out = None
            for k in range(8):
                moved = pltpu.roll(pieces[k], (CHUNK * (k - group)) % LANES, axis=1)
                out = moved if out is None else jnp.where(lane >= CHUNK * k, moved, out)
            out_ref[lev, 8 * part : 8 * part + 8, LANES * b : LANES * b + LANES] = out


def exchange(array, axes):
    return lax.all_to_all(array, axes, 0, 0, tiled=True)


def to_all(array, axes, count):
    return exchange(jnp.broadcast_to(array[None], (count, *array.shape)), axes)


def sum_everywhere(gram):
    part = jnp.sum(exchange(gram.reshape(32, 2, LANES), PLANE), axis=0)
    part = jnp.sum(to_all(part, "z", 16), axis=0)
    return to_all(part, PLANE, 32).reshape(MEMBERS, LANES)


def local(
    background, anomalies, courant_lon, courant_lat, obs_value, obs_weight, obs_column, obs_level
):
    chunk = lax.axis_index(MEM).astype(jnp.int32).reshape(1)
    pieces, fields = call(
        pack_body,
        (f32(MEMBERS, 16, LANES), f32(3, CY, LANES)),
        in_specs=[SMEM] + [VMEM] * 4,
    )(chunk, anomalies[0], background, courant_lon, courant_lat)
    pieces = exchange(pieces, MEM)
    mid, low_edge, high_edge = call(
        pair_body,
        (f32(PAIRS, CY, LANES), f32(PAIRS + 3, HALO, LANES), f32(PAIRS + 3, HALO, LANES)),
        in_specs=[VMEM] * 2,
    )(pieces, fields)
    forward = [(i, i + 1) for i in range(7)]
    backward = [(i + 1, i) for i in range(7)]
    low = lax.ppermute(high_edge, TILE, forward)
    high = lax.ppermute(low_edge, TILE, backward)
    nobs = obs_value.shape[0]
    flat = [a.reshape(1, nobs) for a in (obs_value, obs_weight, obs_column, obs_level)]
    cells = call(cells_body, f32(2, CY, LANES), in_specs=[SMEM] + [VMEM] * 4)(chunk, *flat)
    coefs = [pltpu.VMEM((ROWS, LANES), jnp.float32)] * 5
    rest = [
        pltpu.VMEM((PAIRS, CY, LANES), jnp.float32),
        pltpu.VMEM((MEMBERS * 16, LANES), jnp.float32),
        pltpu.VMEM((MEMBERS, 16 * LANES), jnp.float32),
        pltpu.VMEM((LANES, 16 * LANES), jnp.float32),
    ]
    pair = pltpu.VMEM((PAIRS, LANES), jnp.float32)
    gram, anoms, full = call(
        first_body,
        (f32(MEMBERS, LANES), f32(PAIRS, ROWS, LANES), f32(3, ROWS, LANES)),
        coefs + rest,
        in_specs=[VMEM] * 5,
    )(mid, low, high, fields, cells)
    gram, weights = call(
        second_body,
        (f32(MEMBERS, LANES), f32(MEMBERS, LANES)),
        [pair] + coefs + rest,
        in_specs=[VMEM] * 4,
    )(sum_everywhere(gram), anoms, full, cells)
    part = call(last_body, f32(8, LANES), [pair], in_specs=[VMEM] * 3)(
        sum_everywhere(gram), weights, anoms
    )
    parts = to_all(part, MEM, MEMBERS)
    return call(spread_body, f32(LEV, CY, NX), in_specs=[VMEM])(parts)


def solution(mesh):
    fine = Mesh(mesh.devices.reshape(16, 2, 2, 2, 4), ("z", "yl", "core", "yh", "x"))
    return jax.shard_map(
        local,
        mesh=fine,
        in_specs=(
            P(None, TILE, None),
            P(MEM, None, TILE, None),
            P(None, TILE, None),
            P(None, TILE, None),
            P(TILE),
            P(TILE),
            P(TILE),
            P(TILE),
        ),
        out_specs=P(None, TILE, None),
        check_vma=False,
    )
```

time: 1410 us -> 208 us (0.15)
  waiting for transfers between devices: 1120 us -> 3.81 us
  starting transfers between devices: 103 us -> 4.42 us
  blocking collectives: 69 us -> 158 us
  local copies, waits for them, and re-layouts: 53.4 us -> 3.89 us
  other arithmetic: 38.5 us -> 0.14 us
  Pallas kernels: 0 us -> 36.8 us
    psum x2 -> x0, waiting for transfers between devices: 805 us -> none  [member_sum(): return lax.psum(weights[member_index] * own, 'mem')]
    all_gather x2 -> x0, waiting for transfers between devices: 266 us -> none  [local(): observed = lax.all_gather(own_obs[None, :], 'mem', axis=0, tiled=True)]
    all_to_all x0 -> x8, blocking collectives: none -> 158 us  [exchange(): return lax.all_to_all(array, axes, 0, 0, tiled=True)]
    ppermute x32 -> x2, starting transfers between devices: 103 us -> 4.42 us  [the longest x1 3.12 us: local(): low = lax.ppermute(high_edge, TILE, forward)]
    psum x2 -> x0, blocking collectives: 69 us -> none  [local(): gram_mat, project = lax.psum((gram_mat, project), 'tile')]
    gather x2 -> x0, local copies, waits for them, and re-layouts: 46.1 us -> none  [sample(): return state.reshape(-1)[flat_index]]
    ppermute x32 -> x2, waiting for transfers between devices: 48.6 us -> 3.81 us  [the longest x1 3.8 us: local(): high = lax.ppermute(low_edge, TILE, backward)]
    pallas_call x0 -> x7, Pallas kernels: none -> 36.8 us  [the longest x1 16.9 us: local(): call(second_body, (f32(MEMBERS, LANES), f32(MEMBERS, LANES)), [pair] + co...]
  transfers between devices with their start and end apart: 36 -> 2, of which waited for: 20 -> 1; matrix products, arithmetic and copies ran while one was open for 0% -> 0% of each run, Pallas kernels for 0% -> 0%
where the time goes in v1:
time: 208 us; the launch traced here: 207 us
  blocking collectives  158 us (76%)
  Pallas kernels  36.8 us (18%)
  starting transfers between devices  4.42 us (2%)
  local copies, waits for them, and re-layouts  3.89 us (2%)
  waiting for transfers between devices  3.81 us (2%)
    all_to_all x8, blocking collectives, exchange(): return lax.all_to_all(array, axes, 0, 0, tiled=True)  158 us
    pallas_call x1, Pallas kernels, local(): call(second_body, (f32(MEMBERS, LANES), f32(MEMBERS, LANES)), [pair] + co...  16.9 us
    pallas_call x1, Pallas kernels, local(): call(last_body, f32(8, LANES), [pair], in_specs=[VMEM] * 3)  8.81 us
    pallas_call x1, Pallas kernels, local(): call(first_body, (f32(MEMBERS, LANES), f32(PAIRS, ROWS, LANES), f32(3, RO...  8.19 us
  transfers between devices with their start and end apart: 2, of which 1 were waited for; matrix products, arithmetic and copies ran while one was open for 0% of the time, Pallas kernels for 0%

profile of v1, /device:TPU:1, one launch (start us, length us, event | category | flops | bytes accessed | tf_op | source)
XLA Modules:
  0.0 207.5 jit_solution(6289037307255303834)
XLA Ops:
  0.0 0.9 copy-done
  1.0 0.9 copy-done.1
  1.9 0.9 copy-done.2
  2.9 0.9 copy-done.3
  3.8 0.7 shard_map.82
  4.5 50.5 %all_to_all.40.x_ref = f32[64,16,128]{2,1,0:T(8,128)S(1)} all-to-all(f32[64,16,128]{2,1,0:T(8,128)S(1)} %get-tuple-element.15), channel_id=1, replica_groups=mesh['z'=16,'yl'=2,'core'=2,'yh'=2,'x'=4] {'z','yl','core'}, dimensions={0} | all-to-all | bytes 1048576 | tf_op jit(solution)/shard_map/all_to_all | solution.py:287
  55.0 0.2 shard_map.83
  55.2 3.1 %collective-permute-start = (f32[35,8,128]{2,1,0:T(8,128)S(1)}, f32[35,8,128]{2,1,0:T(8,128)S(1)}, u32[]{:S(2)}, u32[]{:S(2)}) collective-permute-start(f32[35,8,128]{2,1,0:T(8,128)S(1)} %get-tuple-element.18), channel_id=1, source_target_pairs={{0,1},{1,2},{2,3},{3,4},{4,5},{5,6},{6,7},{8,9},{9,10},{10,11},{11... | collective-permute-start | bytes 430088 | tf_op jit(solution)/shard_map/ppermute | solution.py:317
  58.4 1.3 collective-permute-start.1
  59.7 0.0 copy-done.4
  59.7 0.7 shard_map.84.cells_ref
  60.4 0.0 collective-permute-done.low_ref
  60.4 3.8 %collective-permute-done.1.high_ref = f32[35,8,128]{2,1,0:T(8,128)S(1)} collective-permute-done((f32[35,8,128]{2,1,0:T(8,128)S(1)}, f32[35,8,128]{2,1,0:T(8,128)S(1)}, u32[]{:S(2)}, u32[]{:S(2)}) %collective-permute-start.1) | collective-permute-done | bytes 143392 | tf_op jit(solution)/shard_map/ppermute | solution.py:318
  64.2 8.2 %shard_map.85 = (f32[64,128]{1,0:T(8,128)S(1)}, f32[32,48,128]{2,1,0:T(8,128)S(1)}, f32[3,48,128]{2,1,0:T(8,128)S(1)}) custom-call(f32[32,32,128]{2,1,0:T(8,128)S(1)} %get-tuple-element.17.mid_ref, f32[35,8,128]{2,1,0:T(8,128)S(1)} %collective-permute-done.low_ref, f32[35,8,128]{2,1,0:T(8,128)S(1)} %collective-permute-done.1.high_ref, ...), custom_call_target="tpu_custom_call" | custom-call | tf_op jit(solution)/shard_map/pallas_call | solution.py:330
  72.4 19.3 %all_to_all.41 = f32[32,2,128]{2,1,0:T(2,128)S(1)} all-to-all(f32[32,2,128]{2,1,0:T(2,128)S(1)} %bitcast.13), channel_id=1, replica_groups=mesh['z'=16,'yl'=2,'core'=2,'yh'=2,'x'=4] {'yl','core','yh','x'}, dimensions={0} | all-to-all | bytes 65536 | tf_op jit(solution)/shard_map/all_to_all | solution.py:287
  91.8 13.8 %all_to_all.42 = f32[16,2,128]{2,1,0:T(2,128)S(1)} all-to-all(f32[16,2,128]{2,1,0:T(2,128)S(1)} %broadcast_in_dim.10), channel_id=1, replica_groups=mesh['z'=16,'yl'=2,'core'=2,'yh'=2,'x'=4] {'z'}, dimensions={0} | all-to-all | bytes 32768 | tf_op jit(solution)/shard_map/all_to_all | solution.py:287
  105.6 12.0 %all_to_all.43 = f32[32,2,128]{2,1,0:T(2,128)S(1)} all-to-all(f32[32,2,128]{2,1,0:T(2,128)S(1)} %broadcast_in_dim.11), channel_id=1, replica_groups=mesh['z'=16,'yl'=2,'core'=2,'yh'=2,'x'=4] {'yl','core','yh','x'}, dimensions={0} | all-to-all | bytes 65536 | tf_op jit(solution)/shard_map/all_to_all | solution.py:287
  117.6 16.9 %shard_map.86 = (f32[64,128]{1,0:T(8,128)S(1)}, f32[64,128]{1,0:T(8,128)S(1)}) custom-call(f32[64,128]{1,0:T(8,128)S(1)} %bitcast.11, f32[32,48,128]{2,1,0:T(8,128)S(1)} %get-tuple-element.21.anoms_ref, f32[3,48,128]{2,1,0:T(8,128)S(1)} %get-tuple-element.22.full_ref, f32[2,32,128]{2,1,0:T(8,128)S(1)} %shard_map.84.cells_ref), custom_call_target="tpu_custom_call" | custom-call | tf_op jit(solution)/shard_map/pallas_call | solution.py:336
  134.5 10.8 %all_to_all.44 = f32[32,2,128]{2,1,0:T(2,128)S(1)} all-to-all(f32[32,2,128]{2,1,0:T(2,128)S(1)} %bitcast.14), channel_id=1, replica_groups=mesh['z'=16,'yl'=2,'core'=2,'yh'=2,'x'=4] {'yl','core','yh','x'}, dimensions={0} | all-to-all | bytes 65536 | tf_op jit(solution)/shard_map/all_to_all | solution.py:287
  145.3 13.8 %all_to_all.45 = f32[16,2,128]{2,1,0:T(2,128)S(1)} all-to-all(f32[16,2,128]{2,1,0:T(2,128)S(1)} %broadcast_in_dim.12), channel_id=1, replica_groups=mesh['z'=16,'yl'=2,'core'=2,'yh'=2,'x'=4] {'z'}, dimensions={0} | all-to-all | bytes 32768 | tf_op jit(solution)/shard_map/all_to_all | solution.py:287
  159.2 12.0 %all_to_all.46 = f32[32,2,128]{2,1,0:T(2,128)S(1)} all-to-all(f32[32,2,128]{2,1,0:T(2,128)S(1)} %broadcast_in_dim.13), channel_id=1, replica_groups=mesh['z'=16,'yl'=2,'core'=2,'yh'=2,'x'=4] {'yl','core','yh','x'}, dimensions={0} | all-to-all | bytes 65536 | tf_op jit(solution)/shard_map/all_to_all | solution.py:287
  171.1 8.8 %shard_map.87 = f32[8,128]{1,0:T(8,128)S(1)} custom-call(f32[64,128]{1,0:T(8,128)S(1)} %bitcast.12, f32[64,128]{1,0:T(8,128)S(1)} %get-tuple-element.24.weights_ref, f32[32,48,128]{2,1,0:T(8,128)S(1)} %get-tuple-element.21.anoms_ref), custom_call_target="tpu_custom_call" | custom-call | tf_op jit(solution)/shard_map/pallas_call | solution.py:342
  180.0 26.3 %all_to_all.47.x_ref = f32[64,8,128]{2,1,0:T(8,128)S(1)} all-to-all(f32[64,8,128]{2,1,0:T(8,128)S(1)} %broadcast_in_dim.14), channel_id=1, replica_groups=mesh['z'=16,'yl'=2,'core'=2,'yh'=2,'x'=4] {'z','yl','core'}, dimensions={0} | all-to-all | bytes 524288 | tf_op jit(solution)/shard_map/all_to_all | solution.py:287
  206.2 1.2 shard_map.88
  (20 shorter events, 0.2 us)
Async XLA Ops:
  0.0 0.9 copy-start
  1.0 0.9 copy-start.1
  1.9 0.9 copy-start.2
  2.9 0.9 copy-start.3
  55.0 4.7 %copy-start.4 = (f32[4096]{0:T(1024)S(1)}, f32[4096]{0:T(1024)}, u32[]{:S(2)}) copy-start(f32[4096]{0:T(1024)} %param.12) | copy-start | bytes 49156
  55.0 4.7 %copy-start.5 = (f32[4096]{0:T(1024)S(1)}, f32[4096]{0:T(1024)}, u32[]{:S(2)}) copy-start(f32[4096]{0:T(1024)} %param.13) | copy-start | bytes 49156
  55.0 4.7 %copy-start.6 = (s32[4096]{0:T(1024)S(1)}, s32[4096]{0:T(1024)}, u32[]{:S(2)}) copy-start(s32[4096]{0:T(1024)} %param.14) | copy-start | bytes 49156
  55.0 4.7 %copy-start.7 = (s32[4096]{0:T(1024)S(1)}, s32[4096]{0:T(1024)}, u32[]{:S(2)}) copy-start(s32[4096]{0:T(1024)} %param.15) | copy-start | bytes 49156
  55.2 5.2 %collective-permute-start = (f32[35,8,128]{2,1,0:T(8,128)S(1)}, f32[35,8,128]{2,1,0:T(8,128)S(1)}, u32[]{:S(2)}, u32[]{:S(2)}) collective-permute-start(f32[35,8,128]{2,1,0:T(8,128)S(1)} %get-tuple-element.18), channel_id=1, source_target_pairs={{0,1},{1,2},{2,3},{3,4},{4,5},{5,6},{6,7},{8,9},{9,10},{10,11},{11... | collective-permute-start | bytes 430088 | tf_op jit(solution)/shard_map/ppermute | solution.py:317
  58.4 5.8 %collective-permute-start.1 = (f32[35,8,128]{2,1,0:T(8,128)S(1)}, f32[35,8,128]{2,1,0:T(8,128)S(1)}, u32[]{:S(2)}, u32[]{:S(2)}) collective-permute-start(f32[35,8,128]{2,1,0:T(8,128)S(1)} %get-tuple-element.19), channel_id=1, source_target_pairs={{1,0},{2,1},{3,2},{4,3},{5,4},{6,5},{7,6},{9,8},{10,9},{11,10},{12... | collective-permute-start | bytes 430088 | tf_op jit(solution)/shard_map/ppermute | solution.py:318

commit v2 on v1

--- a/solution.py
+++ b/solution.py
@@ -10,6 +10,7 @@
 NSTEP = 8
 MEMBERS = 64
 PAIRS = 32
+GROUP = 8
 LEV = 2
 CY = 32
 NX = 1024
@@ -45,7 +46,7 @@
     return jax.ShapeDtypeStruct(shape, jnp.float32)
 
 
-def pack_body(chunk_ref, own_ref, bg_ref, lon_ref, lat_ref, pieces_ref, fields_ref):
+def pack_body(own_ref, pieces_ref):
     lane = lane_of((16, LANES))
     shifted = []
     for group in range(4):
@@ -70,6 +71,9 @@
                 moved = pltpu.roll(source, amount, axis=1) if amount else source
                 out = moved if out is None else jnp.where(lane >= 32 * group, moved, out)
             pieces_ref[8 * b + k] = out
+
+
+def own_fields(chunk_ref, refs, fields_ref):
     chunk = chunk_ref[0]
     b, k = chunk // 8, chunk % 8
     wide = lane_of((CY, LANES))
@@ -77,7 +81,7 @@
     def block(ref, lev, index):
         return ref[lev, :, pl.ds(pl.multiple_of(index * LANES, LANES), LANES)]
 
-    for index, ref in enumerate((bg_ref, lon_ref, lat_ref)):
+    for index, ref in enumerate(refs):
         out = None
         for lev in range(LEV):
             mid = block(ref, lev, b)
@@ -91,7 +95,8 @@
         fields_ref[index] = out
 
 
-def pair_body(x_ref, fields_ref, mid_ref, low_ref, high_ref):
+def pair_body(chunk_ref, x_ref, bg_ref, lon_ref, lat_ref, fields_ref, mid_ref, low_ref, high_ref):
+    own_fields(chunk_ref, (bg_ref, lon_ref, lat_ref), fields_ref)
     lane = lane_of((16, LANES))
     for p in range(PAIRS):
         first, second = x_ref[p], x_ref[p + PAIRS]
@@ -137,32 +142,50 @@
         out_ref[index] = total
 
 
-def transport(base, anoms_ref, coefs, count, first):
-    state = base + 0.5 * anoms_ref[pl.ds(first, count)]
+def transport(base, anoms_ref, coefs, buf_ref, first, use):
     west_c, east_c, south_c, north_c, own_c = coefs
-    for _ in range(NSTEP):
-        west = pltpu.roll(state, 1, axis=2)
-        east = pltpu.roll(state, LANES - 1, axis=2)
-        south = pltpu.roll(state, 1, axis=1)
-        north = pltpu.roll(state, ROWS - 1, axis=1)
-        speed = 0.85 + 0.15 * jnp.tanh(state)
-        change = west_c[...] * west + east_c[...] * east
-        change = change + (south_c[...] * south + north_c[...] * north)
-        state = state + speed * (change - own_c[...] * state)
-    return state
-
-
-def observe_and_gram(base, anoms_ref, coefs, cells_ref, gram_ref, obs_ref, dev_ref, left_ref, right_ref):
-    group = 4
-
-    def one(index, total):
-        first = index * group
-        state = transport(base, anoms_ref, coefs, group, first)[:, HALO : HALO + CY]
+    for p in range(GROUP):
+        buf_ref[0, p, HALO : HALO + ROWS] = base + 0.5 * anoms_ref[first + p]
+    for step in range(NSTEP):
+        low, count = (0, ROWS) if step < NSTEP - 1 else (HALO, CY)
+        rows = slice(low, low + count)
+        at = HALO + low
+        for p in range(GROUP):
+            now = buf_ref.at[step % 2, p]
+            state = now[at : at + count]
+            south = now[at - 1 : at - 1 + count]
+            north = now[at + 1 : at + 1 + count]
+            west = pltpu.roll(state, 1, axis=1)
+            east = pltpu.roll(state, LANES - 1, axis=1)
+            speed = 0.85 + 0.15 * jnp.tanh(state)
+            change = west_c[rows] * west + east_c[rows] * east
+            change = change + (south_c[rows] * south + north_c[rows] * north)
+            state = state + speed * (change - own_c[rows] * state)
+            if step < NSTEP - 1:
+                buf_ref[(step + 1) % 2, p, at : at + count] = state
+            else:
+                use(first + p, state)
+
+
+def observe_and_gram(
+    base, anoms_ref, coefs, cells_ref, gram_ref, buf_ref, total_ref, obs_ref, dev_ref, left_ref, right_ref
+):
+    edge = jnp.zeros((2, GROUP, HALO, LANES), jnp.float32)
+    buf_ref[:, :, 0:HALO] = edge
+    buf_ref[:, :, HALO + ROWS :] = edge
+    total_ref[...] = jnp.zeros((CY, LANES), jnp.float32)
+
+    def use(p, state):
         seen = state + 0.25 * state * state
-        obs_ref[pl.ds(first, group)] = seen
-        return total + jnp.sum(seen, axis=0)
-
-    total = lax.fori_loop(0, PAIRS // group, one, jnp.zeros((CY, LANES), jnp.float32))
+        obs_ref[p] = seen
+        total_ref[...] += seen
+
+    def one(index, carry):
+        transport(base, anoms_ref, coefs, buf_ref, index * GROUP, use)
+        return carry
+
+    lax.fori_loop(0, PAIRS // GROUP, one, 0)
+    total = total_ref[...]
     center = (total + pltpu.roll(total, 64, axis=1)) * (1.0 / MEMBERS)
     lane = lane_of((16, LANES))
     for p in range(PAIRS):
@@ -182,13 +205,18 @@
         left_ref[:, LANES * r : LANES * r + LANES] = rows
         right_ref[0:MEMBERS, LANES * r : LANES * r + LANES] = rows * weight[r : r + 1]
         right_ref[MEMBERS : MEMBERS + 1, LANES * r : LANES * r + LANES] = aim[r : r + 1]
-    gram_ref[...] = lax.dot_general(
+    gram = lax.dot_general(
         left_ref[...],
         right_ref[...],
         (((1,), (1,)), ((), ())),
         precision=HIGHEST,
         preferred_element_type=jnp.float32,
     )
+    lane = lane_of((PAIRS, LANES))
+    top, bottom = gram[0:PAIRS], gram[PAIRS:MEMBERS]
+    ends = jnp.where(lane == 96, pltpu.roll(top, 32, axis=1), pltpu.roll(bottom, 33, axis=1))
+    ends = jnp.where(lane < 96, pltpu.roll(bottom, 32, axis=1), ends)
+    gram_ref[...] = jnp.where(lane < 64, top, ends)
 
 
 def fill_coefs(lon, lat, coefs):
@@ -213,21 +241,34 @@
     observe_and_gram(full_ref[0], anoms_ref, coefs, cells_ref, gram_ref, *rest)
 
 
-def solve(sums, weights):
+def solve(packed, weights):
     shape = (MEMBERS, LANES)
     lane = lane_of(shape)
     sub = lax.broadcasted_iota(jnp.int32, shape, 0)
     left = MEMBERS - 1.0
+    half = lane[0:PAIRS]
+    moved = pltpu.roll(packed, LANES - 32, axis=1)
+    whole = jnp.concatenate([packed, jnp.zeros((LANES - PAIRS, LANES), jnp.float32)], axis=0)
+    cross = jnp.transpose(whole)[32:64]
+    bottom = jnp.where(half < 64, moved, pltpu.roll(packed, LANES - 33, axis=1))
+    bottom = jnp.where(half < 32, cross, bottom)
+    sums = jnp.concatenate([jnp.where(half < 64, packed, moved), bottom], axis=0)
     matrix = jnp.where(
         lane < MEMBERS,
         sums + jnp.where(lane == sub, left, 0.0),
         jnp.where(lane == MEMBERS, left * weights - sums, 0.0),
     )
-    for k in range(MEMBERS):
-        row = matrix[k : k + 1]
-        column = jnp.broadcast_to(matrix[:, k : k + 1], shape)
-        factor = column / column[k : k + 1]
-        matrix = matrix - jnp.where(sub == k, 0.0, factor) * row
+    width = 8
+    for start in range(0, MEMBERS, width):
+        columns = [
+            jnp.broadcast_to(matrix[:, start + j : start + j + 1], shape) for j in range(width)
+        ]
+        for j in range(width):
+            k = start + j
+            factor = jnp.where(sub == k, 0.0, columns[j] * (1.0 / columns[j][k : k + 1]))
+            for later in range(j + 1, width):
+                columns[later] = columns[later] - factor * columns[later][k : k + 1]
+            matrix = matrix - factor * matrix[k : k + 1]
     diagonal = jnp.sum(jnp.where(lane == sub, matrix, 0.0), axis=1, keepdims=True)
     solved = matrix[:, MEMBERS : MEMBERS + 1] / diagonal
     return weights - jnp.broadcast_to(solved, shape)
@@ -291,27 +332,29 @@
     return exchange(jnp.broadcast_to(array[None], (count, *array.shape)), axes)
 
 
-def sum_everywhere(gram):
-    part = jnp.sum(exchange(gram.reshape(32, 2, LANES), PLANE), axis=0)
+def sum_everywhere(packed):
+    quarters = jnp.broadcast_to(packed.reshape(4, 1, 8, LANES), (4, 8, 8, LANES))
+    part = jnp.sum(exchange(quarters.reshape(32, 8, LANES), PLANE), axis=0)
     part = jnp.sum(to_all(part, "z", 16), axis=0)
-    return to_all(part, PLANE, 32).reshape(MEMBERS, LANES)
+    return to_all(part, ("yl", "core"), 4).reshape(PAIRS, LANES)
 
 
 def local(
     background, anomalies, courant_lon, courant_lat, obs_value, obs_weight, obs_column, obs_level
 ):
     chunk = lax.axis_index(MEM).astype(jnp.int32).reshape(1)
-    pieces, fields = call(
-        pack_body,
-        (f32(MEMBERS, 16, LANES), f32(3, CY, LANES)),
+    pieces = call(pack_body, f32(MEMBERS, 16, LANES), in_specs=[VMEM])(anomalies[0])
+    pieces = exchange(pieces, MEM)
+    fields, mid, low_edge, high_edge = call(
+        pair_body,
+        (
+            f32(3, CY, LANES),
+            f32(PAIRS, CY, LANES),
+            f32(PAIRS + 3, HALO, LANES),
+            f32(PAIRS + 3, HALO, LANES),
+        ),
         in_specs=[SMEM] + [VMEM] * 4,
-    )(chunk, anomalies[0], background, courant_lon, courant_lat)
-    pieces = exchange(pieces, MEM)
-    mid, low_edge, high_edge = call(
-        pair_body,
-        (f32(PAIRS, CY, LANES), f32(PAIRS + 3, HALO, LANES), f32(PAIRS + 3, HALO, LANES)),
-        in_specs=[VMEM] * 2,
-    )(pieces, fields)
+    )(chunk, pieces, background, courant_lon, courant_lat)
     forward = [(i, i + 1) for i in range(7)]
     backward = [(i + 1, i) for i in range(7)]
     low = lax.ppermute(high_edge, TILE, forward)
@@ -321,6 +364,8 @@
     cells = call(cells_body, f32(2, CY, LANES), in_specs=[SMEM] + [VMEM] * 4)(chunk, *flat)
     coefs = [pltpu.VMEM((ROWS, LANES), jnp.float32)] * 5
     rest = [
+        pltpu.VMEM((2, GROUP, ROWS + 2 * HALO, LANES), jnp.float32),
+        pltpu.VMEM((CY, LANES), jnp.float32),
         pltpu.VMEM((PAIRS, CY, LANES), jnp.float32),
         pltpu.VMEM((MEMBERS * 16, LANES), jnp.float32),
         pltpu.VMEM((MEMBERS, 16 * LANES), jnp.float32),
@@ -329,13 +374,13 @@
     pair = pltpu.VMEM((PAIRS, LANES), jnp.float32)
     gram, anoms, full = call(
         first_body,
-        (f32(MEMBERS, LANES), f32(PAIRS, ROWS, LANES), f32(3, ROWS, LANES)),
+        (f32(PAIRS, LANES), f32(PAIRS, ROWS, LANES), f32(3, ROWS, LANES)),
         coefs + rest,
         in_specs=[VMEM] * 5,
     )(mid, low, high, fields, cells)
     gram, weights = call(
         second_body,
-        (f32(MEMBERS, LANES), f32(MEMBERS, LANES)),
+        (f32(PAIRS, LANES), f32(MEMBERS, LANES)),
         [pair] + coefs + rest,
         in_specs=[VMEM] * 4,
     )(sum_everywhere(gram), anoms, full, cells)

time: 208 us -> 181 us (0.87)
  blocking collectives: 158 us -> 101 us
  waiting for transfers between devices: 3.81 us -> 36.3 us
  Pallas kernels: 36.8 us -> 18.4 us
  starting transfers between devices: 4.42 us -> 22.7 us
  local copies, waits for them, and re-layouts: 3.89 us -> 1.07 us
    all_to_all x8 -> x7, blocking collectives: 158 us -> 101 us  [exchange(): return lax.all_to_all(array, axes, 0, 0, tiled=True)]
    all_to_all x0 -> x1, waiting for transfers between devices: none -> 32.5 us  [exchange(): return lax.all_to_all(array, axes, 0, 0, tiled=True)]
    all_to_all x0 -> x1, starting transfers between devices: none -> 18.3 us  [exchange(): return lax.all_to_all(array, axes, 0, 0, tiled=True)]
    pallas_call x4, Pallas kernels: 26 us -> 14.2 us  [the longest x1 7.32 us: local(): call(second_body, (f32(PAIRS, LANES), f32(MEMBERS, LANES)), [pair] + coef...]
    pallas_call x1, Pallas kernels: 8.81 us -> 2.35 us  [local(): call(last_body, f32(8, LANES), [pair], in_specs=[VMEM] * 3)]
    unnamed x16, local copies, waits for them, and re-layouts: 3.81 us -> 0.99 us
  transfers between devices with their start and end apart: 2 -> 3, of which waited for: 1 -> 2; matrix products, arithmetic and copies ran while one was open for 0% -> 0% of each run, Pallas kernels for 0% -> 0%
where the time goes in v2:
time: 181 us; the launch traced here: 180 us
  blocking collectives  101 us (56%)
  waiting for transfers between devices  36.3 us (20%)
  starting transfers between devices  22.7 us (13%)
  Pallas kernels  18.4 us (10%)
    all_to_all x7, blocking collectives, exchange(): return lax.all_to_all(array, axes, 0, 0, tiled=True)  101 us
    all_to_all x1, waiting for transfers between devices, exchange(): return lax.all_to_all(array, axes, 0, 0, tiled=True)  32.5 us
    all_to_all x1, starting transfers between devices, exchange(): return lax.all_to_all(array, axes, 0, 0, tiled=True)  18.3 us
    pallas_call x1, Pallas kernels, local(): call(second_body, (f32(PAIRS, LANES), f32(MEMBERS, LANES)), [pair] + coef...  7.32 us
    pallas_call x1, Pallas kernels, local(): call(first_body, (f32(PAIRS, LANES), f32(PAIRS, ROWS, LANES), f32(3, ROWS...  5.13 us
    ppermute x1, waiting for transfers between devices, local(): high = lax.ppermute(low_edge, TILE, backward)  3.81 us
  transfers between devices with their start and end apart: 3, of which 2 were waited for; matrix products, arithmetic and copies ran while one was open for 0% of the time, Pallas kernels for 0%

profile of v2, /device:TPU:1, one launch (start us, length us, event | category | flops | bytes accessed | tf_op | source)
XLA Modules:
  0.0 180.1 jit_solution(3213507233180842955)
XLA Ops:
  0.0 0.9 copy-done
  1.0 1.5 shard_map.82
  2.4 18.3 %all-to-all-start = ((f32[64,16,128]{2,1,0:T(8,128)}), f32[64,16,128]{2,1,0:T(8,128)S(1)}, u32[]{:S(2)}, u32[]{:S(2)}) async-start(f32[64,16,128]{2,1,0:T(8,128)} %shard_map.82), calls=%async_computation | async-start | bytes 1048576 | tf_op jit(solution)/shard_map/all_to_all | solution.py:328
  20.7 32.5 %all-to-all-done.x_ref = f32[64,16,128]{2,1,0:T(8,128)S(1)} async-done(((f32[64,16,128]{2,1,0:T(8,128)}), f32[64,16,128]{2,1,0:T(8,128)S(1)}, u32[]{:S(2)}, u32[]{:S(2)}) %all-to-all-start) | async-done | bytes 524320 | tf_op jit(solution)/shard_map/all_to_all | solution.py:328
  53.3 0.0 copy-start.4
  53.3 0.0 copy-start.5
  53.3 0.0 copy-start.6
  53.3 0.0 copy-start.7
  53.3 0.3 shard_map.83
  53.6 3.1 %collective-permute-start = (f32[35,8,128]{2,1,0:T(8,128)S(1)}, f32[35,8,128]{2,1,0:T(8,128)S(1)}, u32[]{:S(2)}, u32[]{:S(2)}) collective-permute-start(f32[35,8,128]{2,1,0:T(8,128)S(1)} %get-tuple-element.15), channel_id=1, source_target_pairs={{0,1},{1,2},{2,3},{3,4},{4,5},{5,6},{6,7},{8,9},{9,10},{10,11},{11... | collective-permute-start | bytes 430088 | tf_op jit(solution)/shard_map/ppermute | solution.py:360
  56.7 1.3 collective-permute-start.1
  58.1 0.7 shard_map.84.cells_ref
  58.8 3.8 %collective-permute-done.1.high_ref = f32[35,8,128]{2,1,0:T(8,128)S(1)} collective-permute-done((f32[35,8,128]{2,1,0:T(8,128)S(1)}, f32[35,8,128]{2,1,0:T(8,128)S(1)}, u32[]{:S(2)}, u32[]{:S(2)}) %collective-permute-start.1) | collective-permute-done | bytes 143392 | tf_op jit(solution)/shard_map/ppermute | solution.py:361
  62.6 5.1 %shard_map.85 = (f32[32,128]{1,0:T(8,128)S(1)}, f32[32,48,128]{2,1,0:T(8,128)S(1)}, f32[3,48,128]{2,1,0:T(8,128)S(1)}) custom-call(f32[32,32,128]{2,1,0:T(8,128)S(1)} %get-tuple-element.14.mid_ref, f32[35,8,128]{2,1,0:T(8,128)S(1)} %collective-permute-done.low_ref, f32[35,8,128]{2,1,0:T(8,128)S(1)} %collective-permute-done.1.high_ref, ...), custom_call_target="tpu_custom_call" | custom-call | tf_op jit(solution)/shard_map/pallas_call | solution.py:375
  67.7 19.9 %all_to_all.40 = f32[32,8,128]{2,1,0:T(8,128)S(1)} all-to-all(f32[32,8,128]{2,1,0:T(8,128)S(1)} %bitcast.21), channel_id=1, replica_groups=mesh['z'=16,'yl'=2,'core'=2,'yh'=2,'x'=4] {'yl','core','yh','x'}, dimensions={0} | all-to-all | bytes 262144 | tf_op jit(solution)/shard_map/all_to_all | solution.py:328
  87.7 14.2 %all_to_all.41 = f32[16,8,128]{2,1,0:T(8,128)S(1)} all-to-all(f32[16,8,128]{2,1,0:T(8,128)S(1)} %broadcast_in_dim.20), channel_id=1, replica_groups=mesh['z'=16,'yl'=2,'core'=2,'yh'=2,'x'=4] {'z'}, dimensions={0} | all-to-all | bytes 131072 | tf_op jit(solution)/shard_map/all_to_all | solution.py:328
  102.0 7.5 %all_to_all.42 = f32[4,8,128]{2,1,0:T(8,128)S(1)} all-to-all(f32[4,8,128]{2,1,0:T(8,128)S(1)} %broadcast_in_dim.21), channel_id=1, replica_groups=mesh['z'=16,'yl'=2,'core'=2,'yh'=2,'x'=4] {'yl','core'}, dimensions={0} | all-to-all | bytes 32768 | tf_op jit(solution)/shard_map/all_to_all | solution.py:328
  109.4 7.3 %shard_map.86 = (f32[32,128]{1,0:T(8,128)S(1)}, f32[64,128]{1,0:T(8,128)S(1)}) custom-call(f32[32,128]{1,0:T(8,128)S(1)} %bitcast.13, f32[32,48,128]{2,1,0:T(8,128)S(1)} %get-tuple-element.19.anoms_ref, f32[3,48,128]{2,1,0:T(8,128)S(1)} %get-tuple-element.20.full_ref, f32[2,32,128]{2,1,0:T(8,128)S(1)} %shard_map.84.cells_ref), custom_call_target="tpu_custom_call" | custom-call | tf_op jit(solution)/shard_map/pallas_call | solution.py:381
  116.8 11.8 %all_to_all.43 = f32[32,8,128]{2,1,0:T(8,128)S(1)} all-to-all(f32[32,8,128]{2,1,0:T(8,128)S(1)} %bitcast.22), channel_id=1, replica_groups=mesh['z'=16,'yl'=2,'core'=2,'yh'=2,'x'=4] {'yl','core','yh','x'}, dimensions={0} | all-to-all | bytes 262144 | tf_op jit(solution)/shard_map/all_to_all | solution.py:328
  128.6 14.2 %all_to_all.44 = f32[16,8,128]{2,1,0:T(8,128)S(1)} all-to-all(f32[16,8,128]{2,1,0:T(8,128)S(1)} %broadcast_in_dim.24), channel_id=1, replica_groups=mesh['z'=16,'yl'=2,'core'=2,'yh'=2,'x'=4] {'z'}, dimensions={0} | all-to-all | bytes 131072 | tf_op jit(solution)/shard_map/all_to_all | solution.py:328
  142.8 7.4 %all_to_all.45 = f32[4,8,128]{2,1,0:T(8,128)S(1)} all-to-all(f32[4,8,128]{2,1,0:T(8,128)S(1)} %broadcast_in_dim.25), channel_id=1, replica_groups=mesh['z'=16,'yl'=2,'core'=2,'yh'=2,'x'=4] {'yl','core'}, dimensions={0} | all-to-all | bytes 32768 | tf_op jit(solution)/shard_map/all_to_all | solution.py:328
  150.2 2.4 %shard_map.87 = f32[8,128]{1,0:T(8,128)S(1)} custom-call(f32[32,128]{1,0:T(8,128)S(1)} %bitcast.14, f32[64,128]{1,0:T(8,128)S(1)} %get-tuple-element.22.weights_ref, f32[32,48,128]{2,1,0:T(8,128)S(1)} %get-tuple-element.19.anoms_ref), custom_call_target="tpu_custom_call" | custom-call | tf_op jit(solution)/shard_map/pallas_call | solution.py:387
  152.6 26.2 %all_to_all.46.x_ref = f32[64,8,128]{2,1,0:T(8,128)S(1)} all-to-all(f32[64,8,128]{2,1,0:T(8,128)S(1)} %broadcast_in_dim.52), channel_id=1, replica_groups=mesh['z'=16,'yl'=2,'core'=2,'yh'=2,'x'=4] {'z','yl','core'}, dimensions={0} | all-to-all | bytes 524288 | tf_op jit(solution)/shard_map/all_to_all | solution.py:328
  178.9 1.2 shard_map.88
  (23 shorter events, 0.2 us)
Async XLA Ops:
  0.0 0.9 copy-start
  2.4 50.8 %copy-start.1 = (f32[2,32,1024]{2,1,0:T(8,128)S(1)}, f32[2,32,1024]{2,1,0:T(8,128)}, u32[]{:S(2)}) copy-start(f32[2,32,1024]{2,1,0:T(8,128)} %bg_ref.1) | copy-start | bytes 786436
  2.4 50.9 %copy-start.2 = (f32[2,32,1024]{2,1,0:T(8,128)S(1)}, f32[2,32,1024]{2,1,0:T(8,128)}, u32[]{:S(2)}) copy-start(f32[2,32,1024]{2,1,0:T(8,128)} %lon_ref.1) | copy-start | bytes 786436
  2.4 50.9 %copy-start.3 = (f32[2,32,1024]{2,1,0:T(8,128)S(1)}, f32[2,32,1024]{2,1,0:T(8,128)}, u32[]{:S(2)}) copy-start(f32[2,32,1024]{2,1,0:T(8,128)} %lat_ref.1) | copy-start | bytes 786436
  2.4 50.8 %all-to-all-start = ((f32[64,16,128]{2,1,0:T(8,128)}), f32[64,16,128]{2,1,0:T(8,128)S(1)}, u32[]{:S(2)}, u32[]{:S(2)}) async-start(f32[64,16,128]{2,1,0:T(8,128)} %shard_map.82), calls=%async_computation | async-start | bytes 1048576 | tf_op jit(solution)/shard_map/all_to_all | solution.py:328
  53.3 4.8 %copy-start.4 = (f32[4096]{0:T(1024)S(1)}, f32[4096]{0:T(1024)}, u32[]{:S(2)}) copy-start(f32[4096]{0:T(1024)} %param.12) | copy-start | bytes 49156
  53.3 4.8 %copy-start.5 = (f32[4096]{0:T(1024)S(1)}, f32[4096]{0:T(1024)}, u32[]{:S(2)}) copy-start(f32[4096]{0:T(1024)} %param.13) | copy-start | bytes 49156
  53.3 4.8 %copy-start.6 = (s32[4096]{0:T(1024)S(1)}, s32[4096]{0:T(1024)}, u32[]{:S(2)}) copy-start(s32[4096]{0:T(1024)} %param.14) | copy-start | bytes 49156
  53.3 4.8 %copy-start.7 = (s32[4096]{0:T(1024)S(1)}, s32[4096]{0:T(1024)}, u32[]{:S(2)}) copy-start(s32[4096]{0:T(1024)} %param.15) | copy-start | bytes 49156
  53.6 5.2 %collective-permute-start = (f32[35,8,128]{2,1,0:T(8,128)S(1)}, f32[35,8,128]{2,1,0:T(8,128)S(1)}, u32[]{:S(2)}, u32[]{:S(2)}) collective-permute-start(f32[35,8,128]{2,1,0:T(8,128)S(1)} %get-tuple-element.15), channel_id=1, source_target_pairs={{0,1},{1,2},{2,3},{3,4},{4,5},{5,6},{6,7},{8,9},{9,10},{10,11},{11... | collective-permute-start | bytes 430088 | tf_op jit(solution)/shard_map/ppermute | solution.py:360
  56.7 5.8 %collective-permute-start.1 = (f32[35,8,128]{2,1,0:T(8,128)S(1)}, f32[35,8,128]{2,1,0:T(8,128)S(1)}, u32[]{:S(2)}, u32[]{:S(2)}) collective-permute-start(f32[35,8,128]{2,1,0:T(8,128)S(1)} %get-tuple-element.16), channel_id=1, source_target_pairs={{1,0},{2,1},{3,2},{4,3},{5,4},{6,5},{7,6},{9,8},{10,9},{11,10},{12... | collective-permute-start | bytes 430088 | tf_op jit(solution)/shard_map/ppermute | solution.py:361

commit v3 on v2

v3 whole, which is shorter than its diff:
```python
import functools

import jax
import jax.numpy as jnp
from jax import lax
from jax.experimental import pallas as pl
from jax.experimental.pallas import tpu as pltpu
from jax.sharding import Mesh, PartitionSpec as P

NSTEP = 8
MEMBERS = 64
PAIRS = 32
GROUP = 8
LEV = 2
CY = 32
NX = 1024
CHUNK = 32
HALO = 8
ROWS = CY + 2 * HALO
LANES = 128
PACKED = 20
HIGHEST = lax.Precision.HIGHEST

MEM = ("z", "yl", "core")
TILE = ("yh", "x")
PLANE = ("yl", "core", "yh", "x")
VMEM = pl.BlockSpec(memory_space=pltpu.VMEM)
SMEM = pl.BlockSpec(memory_space=pltpu.SMEM)


def lane_of(shape):
    return lax.broadcasted_iota(jnp.int32, shape, len(shape) - 1)


def call(body, out, scratch=(), in_specs=None, vmem=40 << 20):
    return pl.pallas_call(
        body,
        out_shape=out,
        in_specs=in_specs,
        out_specs=jax.tree.map(lambda _: VMEM, out),
        scratch_shapes=list(scratch),
        compiler_params=pltpu.CompilerParams(vmem_limit_bytes=vmem),
    )


def f32(*shape):
    return jax.ShapeDtypeStruct(shape, jnp.float32)


def pack_body(own_ref, pieces_ref):
    lane = lane_of((8, LANES))
    for lev in range(LEV):
        turned = []
        for q in range(4):
            rolled = [
                pltpu.roll(own_ref[lev, 8 * q : 8 * q + 8, LANES * b : LANES * b + LANES], HALO, axis=1)
                for b in range(8)
            ]
            shifted = [jnp.where(lane < HALO, rolled[b - 1], rolled[b]) for b in range(8)]
            turned.append(
                [
                    [pltpu.roll(block, 32 * n, axis=1) if n else block for n in range(4)]
                    for block in shifted
                ]
            )

        def gather(b, k):
            out = turned[0][b][(-k) % 4]
            for q in range(1, 4):
                out = jnp.where(lane >= 32 * q, turned[q][b][(q - k) % 4], out)
            return out

        for b in range(8):
            for k in range(4):
                at = 12 * (32 * lev + 4 * b + k)
                pieces_ref[at : at + 8] = gather(b, k)
                rest = gather(b, k + 1) if k < 3 else gather((b + 1) % 8, 0)
                other = pltpu.roll(rest, 16, axis=1)
                pieces_ref[at + 8 : at + 12] = jnp.where(
                    lane[0:4] % 32 < 16, rest[0:4], other[4:8]
                )


def own_fields(chunk_ref, refs, fields_ref):
    chunk = chunk_ref[0]
    lev, b, k = chunk // 32, chunk % 32 // 4, chunk % 4
    wide = lane_of((CY, LANES))

    def block(ref, index):
        return ref[lev, :, pl.ds(pl.multiple_of(index * LANES, LANES), LANES)]

    for index, ref in enumerate(refs):
        mid = block(ref, b)
        mid = jnp.where((wide >= LANES - HALO) & (k == 0), block(ref, (b + 7) % 8), mid)
        mid = jnp.where((wide < HALO) & (k == 3), block(ref, (b + 1) % 8), mid)
        mid = pltpu.roll(mid, (HALO - CHUNK * k + LANES) % LANES, axis=1)
        mid = jnp.where(wide < CHUNK + 2 * HALO, mid, 0.0)
        fields_ref[index] = jnp.where(wide < 64, mid, pltpu.roll(mid, 64, axis=1))


def pair_body(chunk_ref, x_ref, bg_ref, lon_ref, lat_ref, fields_ref, mid_ref, low_ref, high_ref):
    own_fields(chunk_ref, (bg_ref, lon_ref, lat_ref), fields_ref)
    lane = lane_of((8, LANES))
    place = lane % 64

    def one(p, carry):
        parts = []
        for member in (p, p + PAIRS):
            main = x_ref[pl.ds(12 * member, 8)]
            rest = x_ref[pl.ds(12 * member + 8, 4)]
            parts.append((main, jnp.concatenate([rest, pltpu.roll(rest, LANES - 16, axis=1)], axis=0)))
        for q in range(4):
            out = None
            for half, (main, rest) in enumerate(parts):
                moved = pltpu.roll(main, (64 * half - 32 * q) % LANES, axis=1)
                tail = pltpu.roll(rest, (64 * half + 32 - 32 * q) % LANES, axis=1)
                moved = jnp.where(place < 32, moved, tail)
                out = moved if out is None else jnp.where(lane < 64, out, moved)
            out = jnp.where(place < CHUNK + 2 * HALO, out, 0.0)
            mid_ref[p, 8 * q : 8 * q + 8] = out
            if q == 0:
                low_ref[p] = out
            if q == 3:
                high_ref[p] = out
        return carry

    lax.fori_loop(0, PAIRS, one, 0, unroll=4)
    for index in range(3):
        low_ref[PAIRS + index] = fields_ref[index, 0:HALO]
        high_ref[PAIRS + index] = fields_ref[index, CY - HALO : CY]


def cells_body(chunk_ref, value_ref, weight_ref, column_ref, level_ref, out_ref):
    chunk = chunk_ref[0]
    column = column_ref[...]
    row = column // NX
    offset = column % NX - CHUNK * (chunk % 32)
    inside = (offset >= 0) & (offset < CHUNK) & (level_ref[...] == chunk // 32)
    lane = jnp.where(inside, HALO + offset, -1)
    square = weight_ref[...] * weight_ref[...]
    nobs = column.shape[1]
    at_row = lax.broadcasted_iota(jnp.int32, (CY, nobs), 0) == row
    at_lane = (lax.broadcasted_iota(jnp.int32, (LANES, nobs), 0) == lane).astype(jnp.bfloat16)
    parts = []
    for value in (square, square * value_ref[...]):
        left = jnp.where(at_row, value, 0.0)
        for _ in range(3):
            part = left.astype(jnp.bfloat16)
            parts.append(part)
            left = left - part.astype(jnp.float32)
    sums = lax.dot_general(
        jnp.concatenate(parts, axis=0),
        at_lane,
        (((1,), (1,)), ((), ())),
        preferred_element_type=jnp.float32,
    )
    for index in range(2):
        base = 3 * CY * index
        total = sums[base : base + CY] + sums[base + CY : base + 2 * CY]
        total = total + sums[base + 2 * CY : base + 3 * CY]
        out_ref[index] = total


def transport(base, anoms_ref, coefs, buf_ref, first, use):
    west_c, east_c, south_c, north_c, own_c = coefs
    for p in range(GROUP):
        buf_ref[0, p, HALO : HALO + ROWS] = base + 0.5 * anoms_ref[first + p]
    for step in range(NSTEP):
        low, count = (0, ROWS) if step < NSTEP - 1 else (HALO, CY)
        rows = slice(low, low + count)
        at = HALO + low
        for p in range(GROUP):
            now = buf_ref.at[step % 2, p]
            state = now[at : at + count]
            south = now[at - 1 : at - 1 + count]
            north = now[at + 1 : at + 1 + count]
            west = pltpu.roll(state, 1, axis=1)
            east = pltpu.roll(state, LANES - 1, axis=1)
            speed = 0.85 + 0.15 * jnp.tanh(state)
            change = west_c[rows] * west + east_c[rows] * east
            change = change + (south_c[rows] * south + north_c[rows] * north)
            state = state + speed * (change - own_c[rows] * state)
            if step < NSTEP - 1:
                buf_ref[(step + 1) % 2, p, at : at + count] = state
            else:
                use(first + p, state)


def inner(rows, start):
    lane = lane_of((8, LANES))
    out = None
    for q in range(4):
        moved = pltpu.roll(rows[8 * q : 8 * q + 8], (32 * q - HALO - start) % LANES, axis=1)
        out = moved if out is None else jnp.where(lane >= 32 * q, moved, out)
    return out


def observe_and_gram(
    base, anoms_ref, coefs, cells_ref, gram_ref, buf_ref, total_ref, obs_ref, dev_ref, left_ref, right_ref
):
    edge = jnp.zeros((2, GROUP, HALO, LANES), jnp.float32)
    buf_ref[:, :, 0:HALO] = edge
    buf_ref[:, :, HALO + ROWS :] = edge
    total_ref[...] = jnp.zeros((CY, LANES), jnp.float32)

    def use(p, state):
        seen = state + 0.25 * state * state
        obs_ref[p] = seen
        total_ref[...] += seen

    def one(index, carry):
        transport(base, anoms_ref, coefs, buf_ref, index * GROUP, use)
        return carry

    lax.fori_loop(0, PAIRS // GROUP, one, 0)
    total = total_ref[...]
    center = (total + pltpu.roll(total, 64, axis=1)) * (1.0 / MEMBERS)
    for p in range(PAIRS):
        dev = obs_ref[p] - center
        for half in range(2):
            at = 8 * (p + PAIRS * half)
            dev_ref[at : at + 8] = inner(dev, 64 * half)
    weight, weighted = cells_ref[0], cells_ref[1]
    aim = inner(2.0 * (weighted - weight * center), 0)
    weight = inner(4.0 * weight, 0)
    right_ref[MEMBERS:LANES, :] = jnp.zeros((LANES - MEMBERS, 8 * LANES), jnp.float32)
    for r in range(8):
        rows = dev_ref[pl.ds(r, MEMBERS, stride=8), :]
        left_ref[:, LANES * r : LANES * r + LANES] = rows
        right_ref[0:MEMBERS, LANES * r : LANES * r + LANES] = rows * weight[r : r + 1]
        right_ref[MEMBERS : MEMBERS + 1, LANES * r : LANES * r + LANES] = aim[r : r + 1]
    gram = lax.dot_general(
        left_ref[...],
        right_ref[...],
        (((1,), (1,)), ((), ())),
        precision=HIGHEST,
        preferred_element_type=jnp.float32,
    )
    wide = lane_of((MEMBERS, LANES))
    sub = lax.broadcasted_iota(jnp.int32, (MEMBERS, LANES), 0)
    column = jnp.broadcast_to(gram[:, MEMBERS : MEMBERS + 1], (MEMBERS, LANES))
    project = jnp.sum(jnp.where(wide == sub, column, 0.0), axis=0, keepdims=True)
    top, bottom = gram[0:PAIRS], gram[PAIRS:MEMBERS]
    lane, sub = wide[0:PAIRS], sub[0:PAIRS]
    diagonal = jnp.sum(jnp.where(lane - 32 == sub, bottom, 0.0), axis=0, keepdims=True)
    square = jnp.where(lane - 32 >= sub, pltpu.roll(top, 32, axis=1), bottom)
    square = jnp.where(lane < 32, pltpu.roll(top, LANES - 32, axis=1), square)
    packed = jnp.where(lane[0:16] < 64, square[0:16], pltpu.roll(square[16:32], 64, axis=1))
    gram_ref[...] = jnp.zeros((PACKED, LANES), jnp.float32)
    gram_ref[0:8] = packed[0:8]
    gram_ref[8:9] = jnp.where(lane[0:1] < 64, project, pltpu.roll(diagonal, 32, axis=1))
    gram_ref[10:18] = packed[8:16]


def fill_coefs(lon, lat, coefs):
    west_c, east_c, south_c, north_c, own_c = coefs
    west_c[...] = jnp.maximum(lon, 0.0)
    east_c[...] = jnp.maximum(-lon, 0.0)
    south_c[...] = jnp.maximum(lat, 0.0)
    north_c[...] = jnp.maximum(-lat, 0.0)
    own_c[...] = jnp.abs(lon) + jnp.abs(lat)


def first_body(mid_ref, low_ref, high_ref, fields_ref, cells_ref, gram_ref, anoms_ref, full_ref, *scratch):
    coefs, rest = scratch[:5], scratch[5:]
    anoms_ref[:, 0:HALO] = low_ref[0:PAIRS]
    anoms_ref[:, HALO : HALO + CY] = mid_ref[...]
    anoms_ref[:, HALO + CY : ROWS] = high_ref[0:PAIRS]
    for index in range(3):
        full_ref[index, 0:HALO] = low_ref[PAIRS + index]
        full_ref[index, HALO : HALO + CY] = fields_ref[index]
        full_ref[index, HALO + CY : ROWS] = high_ref[PAIRS + index]
    fill_coefs(full_ref[1], full_ref[2], coefs)
    observe_and_gram(full_ref[0], anoms_ref, coefs, cells_ref, gram_ref, *rest)


def solve(core, own, other, weights):
    shape = (MEMBERS, LANES)
    wide = lane_of(shape)
    sub = lax.broadcasted_iota(jnp.int32, shape, 0)
    left = MEMBERS - 1.0
    low, high = jnp.where(core == 0, own, other), jnp.where(core == 0, other, own)
    packed = jnp.concatenate([low[0:8], high[0:8]], axis=0)
    ends = jnp.broadcast_to(low[8:9], shape)
    square = jnp.concatenate([packed, pltpu.roll(packed, 64, axis=1)], axis=0)
    padded = jnp.concatenate([square, jnp.zeros((LANES - PAIRS, LANES), jnp.float32)], axis=0)
    turned = jnp.transpose(padded)
    lane, row = wide[0:PAIRS], sub[0:PAIRS]
    top = jnp.where(lane >= row, pltpu.roll(square, LANES - 32, axis=1), turned[32:64])
    top = jnp.where(lane < 32, top, pltpu.roll(square, 32, axis=1))
    bottom = jnp.where(lane - 32 < row, square, pltpu.roll(turned[32:64], 32, axis=1))
    bottom = jnp.where(lane - 32 == row, pltpu.roll(ends, LANES - 32, axis=1)[0:PAIRS], bottom)
    bottom = jnp.where(lane < 32, turned[0:32], bottom)
    sums = jnp.concatenate([top, bottom], axis=0)
    project = jnp.sum(jnp.where(wide == sub, ends, 0.0), axis=1, keepdims=True)
    gradient = left * weights - jnp.broadcast_to(project, shape)
    lane = wide
    matrix = jnp.where(
        lane < MEMBERS,
        sums + jnp.where(lane == sub, left, 0.0),
        jnp.where(lane == MEMBERS, gradient, 0.0),
    )
    width = 8
    for start in range(0, MEMBERS, width):
        columns = [
            jnp.broadcast_to(matrix[:, start + j : start + j + 1], shape) for j in range(width)
        ]
        for j in range(width):
            k = start + j
            factor = jnp.where(sub == k, 0.0, columns[j] * (1.0 / columns[j][k : k + 1]))
            for later in range(j + 1, width):
                columns[later] = columns[later] - factor * columns[later][k : k + 1]
            matrix = matrix - factor * matrix[k : k + 1]
    diagonal = jnp.sum(jnp.where(lane == sub, matrix, 0.0), axis=1, keepdims=True)
    solved = matrix[:, MEMBERS : MEMBERS + 1] / diagonal
    return weights - jnp.broadcast_to(solved, shape)


def by_pair(weights):
    lane = lane_of((PAIRS, LANES))
    return jnp.where(lane < 64, weights[0:PAIRS], weights[PAIRS:MEMBERS])


def mix(pair_ref, anoms_ref, low, rows):
    total = jnp.zeros((rows, LANES), jnp.float32)
    for p in range(PAIRS):
        total = total + pair_ref[p : p + 1] * anoms_ref[p, low : low + rows]
    return total + pltpu.roll(total, 64, axis=1)


def second_body(core_ref, own_ref, other_ref, anoms_ref, full_ref, cells_ref, gram_ref, weights_ref, *scratch):
    pair_ref, coefs, rest = scratch[0], scratch[1:6], scratch[6:]
    fill_coefs(full_ref[1], full_ref[2], coefs)
    weights = solve(
        core_ref[0], own_ref[...], other_ref[...], jnp.zeros((MEMBERS, LANES), jnp.float32)
    )
    weights_ref[...] = weights
    pair_ref[...] = by_pair(weights)
    base = full_ref[0] + mix(pair_ref, anoms_ref, 0, ROWS)
    observe_and_gram(base, anoms_ref, coefs, cells_ref, gram_ref, *rest)


def last_body(core_ref, own_ref, other_ref, weights_ref, anoms_ref, out_ref, pair_ref):
    weights = solve(core_ref[0], own_ref[...], other_ref[...], weights_ref[...])
    pair_ref[...] = by_pair(weights)
    out_ref[...] = inner(mix(pair_ref, anoms_ref, HALO, CY), 0)


def spread_body(core_ref, own_ref, other_ref, out_ref):
    lane = lane_of((8, LANES))
    first = core_ref[0] == 0
    for lev in range(LEV):
        for b in range(8):
            pieces = []
            for k in range(4):
                at = 16 * lev + 2 * b + k // 2
                own, other = own_ref[at], other_ref[at]
                if k % 2:
                    own, other = other, own
                pieces.append(jnp.where(first, own, other))
            for q in range(4):
                out = None
                for k in range(4):
                    moved = pltpu.roll(pieces[k], (32 * (k - q)) % LANES, axis=1)
                    out = moved if out is None else jnp.where(lane >= 32 * k, moved, out)
                out_ref[lev, 8 * q : 8 * q + 8, LANES * b : LANES * b + LANES] = out


def exchange(array, axes):
    return lax.all_to_all(array, axes, 0, 0, tiled=True)


def to_all(array, axes, count):
    return exchange(jnp.broadcast_to(array[None], (count, *array.shape)), axes)


def swap_cores(array):
    return lax.ppermute(array, "core", [(0, 1), (1, 0)])


def sum_everywhere(packed):
    shape = (5, 2, LANES)
    halves = jnp.broadcast_to(packed.reshape(1, 2, 1, *shape), (2, 2, 8, *shape))
    part = jnp.sum(exchange(halves.reshape(32, *shape), PLANE), axis=0)
    part = jnp.sum(to_all(part, "z", 16), axis=0).reshape(10, LANES)
    return part, swap_cores(part)


def local(
    background, anomalies, courant_lon, courant_lat, obs_value, obs_weight, obs_column, obs_level
):
    chunk = lax.axis_index(MEM).astype(jnp.int32).reshape(1)
    core = lax.axis_index("core").astype(jnp.int32).reshape(1)
    pieces = call(pack_body, f32(MEMBERS * 12, LANES), in_specs=[VMEM])(anomalies[0])
    pieces = exchange(pieces.reshape(MEMBERS, 3, 4, LANES), MEM).reshape(MEMBERS * 12, LANES)
    fields, mid, low_edge, high_edge = call(
        pair_body,
        (
            f32(3, CY, LANES),
            f32(PAIRS, CY, LANES),
            f32(PAIRS + 3, HALO, LANES),
            f32(PAIRS + 3, HALO, LANES),
        ),
        in_specs=[SMEM] + [VMEM] * 4,
    )(chunk, pieces, background, courant_lon, courant_lat)
    forward = [(i, i + 1) for i in range(7)]
    backward = [(i + 1, i) for i in range(7)]
    low = lax.ppermute(high_edge, TILE, forward)
    high = lax.ppermute(low_edge, TILE, backward)
    nobs = obs_value.shape[0]
    flat = [a.reshape(1, nobs) for a in (obs_value, obs_weight, obs_column, obs_level)]
    cells = call(cells_body, f32(2, CY, LANES), in_specs=[SMEM] + [VMEM] * 4)(chunk, *flat)
    coefs = [pltpu.VMEM((ROWS, LANES), jnp.float32)] * 5
    rest = [
        pltpu.VMEM((2, GROUP, ROWS + 2 * HALO, LANES), jnp.float32),
        pltpu.VMEM((CY, LANES), jnp.float32),
        pltpu.VMEM((PAIRS, CY, LANES), jnp.float32),
        pltpu.VMEM((MEMBERS * 8, LANES), jnp.float32),
        pltpu.VMEM((MEMBERS, 8 * LANES), jnp.float32),
        pltpu.VMEM((LANES, 8 * LANES), jnp.float32),
    ]
    pair = pltpu.VMEM((PAIRS, LANES), jnp.float32)
    gram, anoms, full = call(
        first_body,
        (f32(PACKED, LANES), f32(PAIRS, ROWS, LANES), f32(3, ROWS, LANES)),
        coefs + rest,
        in_specs=[VMEM] * 5,
    )(mid, low, high, fields, cells)
    gram, weights = call(
        second_body,
        (f32(PACKED, LANES), f32(MEMBERS, LANES)),
        [pair] + coefs + rest,
        in_specs=[SMEM] + [VMEM] * 5,
    )(core, *sum_everywhere(gram), anoms, full, cells)
    part = call(last_body, f32(8, LANES), [pair], in_specs=[SMEM] + [VMEM] * 4)(
        core, *sum_everywhere(gram), weights, anoms
    )
    parts = to_all(part, ("z", "yl"), 32)
    return call(spread_body, f32(LEV, CY, NX), in_specs=[SMEM] + [VMEM] * 2)(
        core, parts, swap_cores(parts)
    )


def solution(mesh):
    fine = Mesh(mesh.devices.reshape(16, 2, 2, 2, 4), ("z", "yl", "core", "yh", "x"))
    return jax.shard_map(
        local,
        mesh=fine,
        in_specs=(
            P(None, TILE, None),
            P(MEM, None, TILE, None),
            P(None, TILE, None),
            P(None, TILE, None),
            P(TILE),
            P(TILE),
            P(TILE),
            P(TILE),
        ),
        out_specs=P(None, TILE, None),
        check_vma=False,
    )
```

time: 181 us -> 169 us (0.934)
  blocking collectives: 101 us -> 77.7 us
  starting transfers between devices: 22.7 us -> 35.2 us
    all_to_all x7 -> x5, blocking collectives: 101 us -> 77.7 us  [exchange(): return lax.all_to_all(array, axes, 0, 0, tiled=True)]
    ppermute x0 -> x3, starting transfers between devices: none -> 12.5 us  [swap_cores(): return lax.ppermute(array, 'core', [(0, 1), (1, 0)])]
    all_to_all x1, waiting for transfers between devices: 32.5 us -> 27.9 us  [exchange(): return lax.all_to_all(array, axes, 0, 0, tiled=True)]
    ppermute x0 -> x3, waiting for transfers between devices: none -> 2.58 us  [swap_cores(): return lax.ppermute(array, 'core', [(0, 1), (1, 0)])]
  transfers between devices with their start and end apart: 3 -> 6, of which waited for: 2 -> 6; matrix products, arithmetic and copies ran while one was open for 0% -> 0% of each run, Pallas kernels for 0% -> 0%
where the time goes in v3:
time: 169 us; the launch traced here: 168 us
  blocking collectives  77.7 us (46%)
  starting transfers between devices  35.2 us (21%)
  waiting for transfers between devices  34.7 us (21%)
  Pallas kernels  19.2 us (11%)
    all_to_all x5, blocking collectives, exchange(): return lax.all_to_all(array, axes, 0, 0, tiled=True)  77.7 us
    all_to_all x1, waiting for transfers between devices, exchange(): return lax.all_to_all(array, axes, 0, 0, tiled=True)  27.9 us
    all_to_all x1, starting transfers between devices, exchange(): return lax.all_to_all(array, axes, 0, 0, tiled=True)  18.3 us
    ppermute x3, starting transfers between devices, swap_cores(): return lax.ppermute(array, 'core', [(0, 1), (1, 0)])  12.5 us
    pallas_call x1, Pallas kernels, local(): call(second_body, (f32(PACKED, LANES), f32(MEMBERS, LANES)), [pair] + coe...  7.15 us
    pallas_call x1, Pallas kernels, local(): call(first_body, (f32(PACKED, LANES), f32(PAIRS, ROWS, LANES), f32(3, ROW...  4.74 us
    ppermute x1, waiting for transfers between devices, local(): high = lax.ppermute(low_edge, TILE, backward)  3.8 us
  transfers between devices with their start and end apart: 6, of which 6 were waited for; matrix products, arithmetic and copies ran while one was open for 0% of the time, Pallas kernels for 0%

profile of v3, /device:TPU:1, one launch (start us, length us, event | category | flops | bytes accessed | tf_op | source)
XLA Modules:
  0.0 168.3 jit_solution(2402709721684656306)
XLA Ops:
  0.0 0.9 copy-done
  1.0 1.6 shard_map.82
  2.6 18.3 %all-to-all-start = ((f32[64,3,4,128]{3,2,1,0:T(4,128)}), f32[64,3,4,128]{3,2,1,0:T(4,128)S(1)}, u32[]{:S(2)}, u32[]{:S(2)}) async-start(f32[64,3,4,128]{3,2,1,0:T(4,128)} %bitcast.3), calls=%async_computation | async-start | bytes 786432 | tf_op jit(solution)/shard_map/all_to_all | solution.py:370
  20.9 27.9 %all-to-all-done = f32[64,3,4,128]{3,2,1,0:T(4,128)S(1)} async-done(((f32[64,3,4,128]{3,2,1,0:T(4,128)}), f32[64,3,4,128]{3,2,1,0:T(4,128)S(1)}, u32[]{:S(2)}, u32[]{:S(2)}) %all-to-all-start) | async-done | bytes 393248 | tf_op jit(solution)/shard_map/all_to_all | solution.py:370
  48.8 1.5 shard_map.83
  50.4 3.1 %collective-permute-start = (f32[35,8,128]{2,1,0:T(8,128)S(1)}, f32[35,8,128]{2,1,0:T(8,128)S(1)}, u32[]{:S(2)}, u32[]{:S(2)}) collective-permute-start(f32[35,8,128]{2,1,0:T(8,128)S(1)} %get-tuple-element.15), channel_id=1, source_target_pairs={{0,1},{1,2},{2,3},{3,4},{4,5},{5,6},{6,7},{8,9},{9,10},{10,11},{11... | collective-permute-start | bytes 430088 | tf_op jit(solution)/shard_map/ppermute | solution.py:408
  53.5 1.3 collective-permute-start.1
  54.9 0.7 shard_map.84.cells_ref
  56.0 3.8 %collective-permute-done.1.high_ref = f32[35,8,128]{2,1,0:T(8,128)S(1)} collective-permute-done((f32[35,8,128]{2,1,0:T(8,128)S(1)}, f32[35,8,128]{2,1,0:T(8,128)S(1)}, u32[]{:S(2)}, u32[]{:S(2)}) %collective-permute-start.1) | collective-permute-done | bytes 143392 | tf_op jit(solution)/shard_map/ppermute | solution.py:409
  59.8 4.7 %shard_map.85 = (f32[20,128]{1,0:T(8,128)S(1)}, f32[32,48,128]{2,1,0:T(8,128)S(1)}, f32[3,48,128]{2,1,0:T(8,128)S(1)}) custom-call(f32[32,32,128]{2,1,0:T(8,128)S(1)} %get-tuple-element.14.mid_ref, f32[35,8,128]{2,1,0:T(8,128)S(1)} %collective-permute-done.low_ref, f32[35,8,128]{2,1,0:T(8,128)S(1)} %collective-permute-done.1.high_ref, ...), custom_call_target="tpu_custom_call" | custom-call | tf_op jit(solution)/shard_map/pallas_call | solution.py:423
  64.6 18.9 %all_to_all.30 = f32[32,5,2,128]{3,2,1,0:T(2,128)S(1)} all-to-all(f32[32,5,2,128]{3,2,1,0:T(2,128)S(1)} %bitcast.17), channel_id=1, replica_groups=mesh['z'=16,'yl'=2,'core'=2,'yh'=2,'x'=4] {'yl','core','yh','x'}, dimensions={0} | all-to-all | bytes 327680 | tf_op jit(solution)/shard_map/all_to_all | solution.py:370
  83.5 14.3 %all_to_all.31 = f32[16,5,2,128]{3,2,1,0:T(2,128)S(1)} all-to-all(f32[16,5,2,128]{3,2,1,0:T(2,128)S(1)} %broadcast_in_dim.16), channel_id=1, replica_groups=mesh['z'=16,'yl'=2,'core'=2,'yh'=2,'x'=4] {'z'}, dimensions={0} | all-to-all | bytes 163840 | tf_op jit(solution)/shard_map/all_to_all | solution.py:370
  97.8 4.2 %collective-permute-start.2 = (f32[10,128]{1,0:T(8,128)S(1)}, f32[10,128]{1,0:T(8,128)S(1)}, u32[]{:S(2)}, u32[]{:S(2)}) collective-permute-start(f32[10,128]{1,0:T(8,128)S(1)} %reshape.52.own_ref), channel_id=1, source_target_pairs={{0,8},{8,0},{1,9},{9,1},{2,10},{10,2},{3,11},{11,3},{4,12},{12,4},... | collective-permute-start | bytes 15368 | tf_op jit(solution)/shard_map/ppermute | solution.py:378
  102.1 0.8 collective-permute-done.2.other_ref
  102.9 7.1 %shard_map.86 = (f32[20,128]{1,0:T(8,128)S(1)}, f32[64,128]{1,0:T(8,128)S(1)}) custom-call(s32[1]{0:T(128)} %bitcast.core_ref, f32[10,128]{1,0:T(8,128)S(1)} %reshape.52.own_ref, f32[10,128]{1,0:T(8,128)S(1)} %collective-permute-done.2.other_ref, f32[32,48,128]{2,1,0:T(8,128)S(1)} %get-tuple-element.19.anoms_ref, ...), custom_call_target="tpu_custom_call" | custom-call | tf_op jit(solution)/shard_map/pallas_call | solution.py:429
  110.1 11.6 %all_to_all.32 = f32[32,5,2,128]{3,2,1,0:T(2,128)S(1)} all-to-all(f32[32,5,2,128]{3,2,1,0:T(2,128)S(1)} %bitcast.18), channel_id=1, replica_groups=mesh['z'=16,'yl'=2,'core'=2,'yh'=2,'x'=4] {'yl','core','yh','x'}, dimensions={0} | all-to-all | bytes 327680 | tf_op jit(solution)/shard_map/all_to_all | solution.py:370
  121.7 14.8 %all_to_all.33 = f32[16,5,2,128]{3,2,1,0:T(2,128)S(1)} all-to-all(f32[16,5,2,128]{3,2,1,0:T(2,128)S(1)} %broadcast_in_dim.37), channel_id=1, replica_groups=mesh['z'=16,'yl'=2,'core'=2,'yh'=2,'x'=4] {'z'}, dimensions={0} | all-to-all | bytes 163840 | tf_op jit(solution)/shard_map/all_to_all | solution.py:370
  136.6 4.2 %collective-permute-start.3 = (f32[10,128]{1,0:T(8,128)S(1)}, f32[10,128]{1,0:T(8,128)S(1)}, u32[]{:S(2)}, u32[]{:S(2)}) collective-permute-start(f32[10,128]{1,0:T(8,128)S(1)} %reshape.54.own_ref), channel_id=1, source_target_pairs={{0,8},{8,0},{1,9},{9,1},{2,10},{10,2},{3,11},{11,3},{4,12},{12,4},... | collective-permute-start | bytes 15368 | tf_op jit(solution)/shard_map/ppermute | solution.py:378
  140.8 0.8 collective-permute-done.3.other_ref
  141.6 2.5 %shard_map.87 = f32[8,128]{1,0:T(8,128)S(1)} custom-call(s32[1]{0:T(128)} %bitcast.core_ref, f32[10,128]{1,0:T(8,128)S(1)} %reshape.54.own_ref, f32[10,128]{1,0:T(8,128)S(1)} %collective-permute-done.3.other_ref, f32[64,128]{1,0:T(8,128)S(1)} %get-tuple-element.22.weights_ref, f32[32,48,128]{2,1,0:T(8,128)S(1)} %get-tuple-element.19.anoms_ref), custom_call_target="tpu_custom_call" | custom-call | tf_op jit(solution)/shard_map/pallas_call | solution.py:435
  144.1 18.2 %all_to_all.34.own_ref = f32[32,8,128]{2,1,0:T(8,128)S(1)} all-to-all(f32[32,8,128]{2,1,0:T(8,128)S(1)} %broadcast_in_dim.38), channel_id=1, replica_groups=mesh['z'=16,'yl'=2,'core'=2,'yh'=2,'x'=4] {'z','yl'}, dimensions={0} | all-to-all | bytes 262144 | tf_op jit(solution)/shard_map/all_to_all | solution.py:370
  162.3 4.0 %collective-permute-start.4 = (f32[32,8,128]{2,1,0:T(8,128)S(1)}, f32[32,8,128]{2,1,0:T(8,128)S(1)}, u32[]{:S(2)}, u32[]{:S(2)}) collective-permute-start(f32[32,8,128]{2,1,0:T(8,128)S(1)} %all_to_all.34.own_ref), channel_id=1, source_target_pairs={{0,8},{8,0},{1,9},{9,1},{2,10},{10,2},{3,11},{11,3},{4,12},{12,4},... | collective-permute-start | bytes 393224 | tf_op jit(solution)/shard_map/ppermute | solution.py:378
  166.4 1.0 collective-permute-done.4.other_ref
  167.3 1.0 shard_map.88
  (29 shorter events, 0.9 us)
Async XLA Ops:
  0.0 0.9 copy-start
  2.6 46.2 %copy-start.1 = (f32[2,32,1024]{2,1,0:T(8,128)S(1)}, f32[2,32,1024]{2,1,0:T(8,128)}, u32[]{:S(2)}) copy-start(f32[2,32,1024]{2,1,0:T(8,128)} %bg_ref.1) | copy-start | bytes 786436
  2.6 46.2 %copy-start.2 = (f32[2,32,1024]{2,1,0:T(8,128)S(1)}, f32[2,32,1024]{2,1,0:T(8,128)}, u32[]{:S(2)}) copy-start(f32[2,32,1024]{2,1,0:T(8,128)} %lon_ref.1) | copy-start | bytes 786436
  2.6 46.2 %copy-start.3 = (f32[2,32,1024]{2,1,0:T(8,128)S(1)}, f32[2,32,1024]{2,1,0:T(8,128)}, u32[]{:S(2)}) copy-start(f32[2,32,1024]{2,1,0:T(8,128)} %lat_ref.1) | copy-start | bytes 786436
  2.6 46.2 %all-to-all-start = ((f32[64,3,4,128]{3,2,1,0:T(4,128)}), f32[64,3,4,128]{3,2,1,0:T(4,128)S(1)}, u32[]{:S(2)}, u32[]{:S(2)}) async-start(f32[64,3,4,128]{3,2,1,0:T(4,128)} %bitcast.3), calls=%async_computation | async-start | bytes 786432 | tf_op jit(solution)/shard_map/all_to_all | solution.py:370
  48.8 6.0 %copy-start.4 = (f32[4096]{0:T(1024)S(1)}, f32[4096]{0:T(1024)}, u32[]{:S(2)}) copy-start(f32[4096]{0:T(1024)} %param.12) | copy-start | bytes 49156
  48.8 6.0 %copy-start.5 = (f32[4096]{0:T(1024)S(1)}, f32[4096]{0:T(1024)}, u32[]{:S(2)}) copy-start(f32[4096]{0:T(1024)} %param.13) | copy-start | bytes 49156
  48.8 6.0 %copy-start.6 = (s32[4096]{0:T(1024)S(1)}, s32[4096]{0:T(1024)}, u32[]{:S(2)}) copy-start(s32[4096]{0:T(1024)} %param.14) | copy-start | bytes 49156
  48.8 6.0 %copy-start.7 = (s32[4096]{0:T(1024)S(1)}, s32[4096]{0:T(1024)}, u32[]{:S(2)}) copy-start(s32[4096]{0:T(1024)} %param.15) | copy-start | bytes 49156
  50.4 5.6 %collective-permute-start = (f32[35,8,128]{2,1,0:T(8,128)S(1)}, f32[35,8,128]{2,1,0:T(8,128)S(1)}, u32[]{:S(2)}, u32[]{:S(2)}) collective-permute-start(f32[35,8,128]{2,1,0:T(8,128)S(1)} %get-tuple-element.15), channel_id=1, source_target_pairs={{0,1},{1,2},{2,3},{3,4},{4,5},{5,6},{6,7},{8,9},{9,10},{10,11},{11... | collective-permute-start | bytes 430088 | tf_op jit(solution)/shard_map/ppermute | solution.py:408
  53.5 6.3 %collective-permute-start.1 = (f32[35,8,128]{2,1,0:T(8,128)S(1)}, f32[35,8,128]{2,1,0:T(8,128)S(1)}, u32[]{:S(2)}, u32[]{:S(2)}) collective-permute-start(f32[35,8,128]{2,1,0:T(8,128)S(1)} %get-tuple-element.16), channel_id=1, source_target_pairs={{1,0},{2,1},{3,2},{4,3},{5,4},{6,5},{7,6},{9,8},{10,9},{11,10},{12... | collective-permute-start | bytes 430088 | tf_op jit(solution)/shard_map/ppermute | solution.py:409
  97.8 5.0 %collective-permute-start.2 = (f32[10,128]{1,0:T(8,128)S(1)}, f32[10,128]{1,0:T(8,128)S(1)}, u32[]{:S(2)}, u32[]{:S(2)}) collective-permute-start(f32[10,128]{1,0:T(8,128)S(1)} %reshape.52.own_ref), channel_id=1, source_target_pairs={{0,8},{8,0},{1,9},{9,1},{2,10},{10,2},{3,11},{11,3},{4,12},{12,4},... | collective-permute-start | bytes 15368 | tf_op jit(solution)/shard_map/ppermute | solution.py:378
  136.6 5.0 %collective-permute-start.3 = (f32[10,128]{1,0:T(8,128)S(1)}, f32[10,128]{1,0:T(8,128)S(1)}, u32[]{:S(2)}, u32[]{:S(2)}) collective-permute-start(f32[10,128]{1,0:T(8,128)S(1)} %reshape.54.own_ref), channel_id=1, source_target_pairs={{0,8},{8,0},{1,9},{9,1},{2,10},{10,2},{3,11},{11,3},{4,12},{12,4},... | collective-permute-start | bytes 15368 | tf_op jit(solution)/shard_map/ppermute | solution.py:378
  162.3 5.0 %collective-permute-start.4 = (f32[32,8,128]{2,1,0:T(8,128)S(1)}, f32[32,8,128]{2,1,0:T(8,128)S(1)}, u32[]{:S(2)}, u32[]{:S(2)}) collective-permute-start(f32[32,8,128]{2,1,0:T(8,128)S(1)} %all_to_all.34.own_ref), channel_id=1, source_target_pairs={{0,8},{8,0},{1,9},{9,1},{2,10},{10,2},{3,11},{11,3},{4,12},{12,4},... | collective-permute-start | bytes 393224 | tf_op jit(solution)/shard_map/ppermute | solution.py:378

commit v4 on v3

--- a/solution.py
+++ b/solution.py
@@ -17,6 +17,7 @@
 CHUNK = 32
 HALO = 8
 ROWS = CY + 2 * HALO
+EDGE = 12 * MEMBERS // 4 + 3 * HALO
 LANES = 128
 PACKED = 20
 HIGHEST = lax.Precision.HIGHEST
@@ -81,7 +82,7 @@
                 )
 
 
-def own_fields(chunk_ref, refs, fields_ref):
+def fields_body(chunk_ref, bg_ref, lon_ref, lat_ref, fields_ref):
     chunk = chunk_ref[0]
     lev, b, k = chunk // 32, chunk % 32 // 4, chunk % 4
     wide = lane_of((CY, LANES))
@@ -89,7 +90,7 @@
     def block(ref, index):
         return ref[lev, :, pl.ds(pl.multiple_of(index * LANES, LANES), LANES)]
 
-    for index, ref in enumerate(refs):
+    for index, ref in enumerate((bg_ref, lon_ref, lat_ref)):
         mid = block(ref, b)
         mid = jnp.where((wide >= LANES - HALO) & (k == 0), block(ref, (b + 7) % 8), mid)
         mid = jnp.where((wide < HALO) & (k == 3), block(ref, (b + 1) % 8), mid)
@@ -98,36 +99,87 @@
         fields_ref[index] = jnp.where(wide < 64, mid, pltpu.roll(mid, 64, axis=1))
 
 
-def pair_body(chunk_ref, x_ref, bg_ref, lon_ref, lat_ref, fields_ref, mid_ref, low_ref, high_ref):
-    own_fields(chunk_ref, (bg_ref, lon_ref, lat_ref), fields_ref)
+def edges_body(x_ref, fields_ref, low_ref, high_ref):
+    lane = lane_of((12, LANES))
+    for u in range(MEMBERS // 4):
+        low, high = None, None
+        for i in range(4):
+            at = 12 * (4 * u + i)
+            piece = x_ref[at : at + 12]
+            first = pltpu.roll(piece, 32 * i, axis=1) if i else piece
+            last = pltpu.roll(piece, (32 * i + 32) % LANES, axis=1) if i < 3 else piece
+            low = first if i == 0 else jnp.where(lane >= 32 * i, first, low)
+            high = last if i == 0 else jnp.where(lane >= 32 * i, last, high)
+        low_ref[12 * u : 12 * u + 12] = low
+        high_ref[12 * u : 12 * u + 12] = high
+    for index in range(3):
+        at = EDGE - 3 * HALO + HALO * index
+        low_ref[at : at + HALO] = fields_ref[index, 0:HALO]
+        high_ref[at : at + HALO] = fields_ref[index, CY - HALO : CY]
+
+
+def halves(ref, first, second):
+    parts = []
+    for at in (first, second):
+        rest = ref[pl.ds(at + 8, 4)]
+        rest = jnp.concatenate([rest, pltpu.roll(rest, LANES - 16, axis=1)], axis=0)
+        parts.append((ref[pl.ds(at, 8)], rest))
+    return parts
+
+
+def unpacked(parts, q):
     lane = lane_of((8, LANES))
     place = lane % 64
-
-    def one(p, carry):
-        parts = []
-        for member in (p, p + PAIRS):
-            main = x_ref[pl.ds(12 * member, 8)]
-            rest = x_ref[pl.ds(12 * member + 8, 4)]
-            parts.append((main, jnp.concatenate([rest, pltpu.roll(rest, LANES - 16, axis=1)], axis=0)))
-        for q in range(4):
-            out = None
-            for half, (main, rest) in enumerate(parts):
-                moved = pltpu.roll(main, (64 * half - 32 * q) % LANES, axis=1)
-                tail = pltpu.roll(rest, (64 * half + 32 - 32 * q) % LANES, axis=1)
-                moved = jnp.where(place < 32, moved, tail)
-                out = moved if out is None else jnp.where(lane < 64, out, moved)
-            out = jnp.where(place < CHUNK + 2 * HALO, out, 0.0)
-            mid_ref[p, 8 * q : 8 * q + 8] = out
-            if q == 0:
-                low_ref[p] = out
-            if q == 3:
-                high_ref[p] = out
+    out = None
+    for half, (main, rest) in enumerate(parts):
+        moved = pltpu.roll(main, (64 * half - 32 * q) % LANES, axis=1)
+        tail = pltpu.roll(rest, (64 * half + 32 - 32 * q) % LANES, axis=1)
+        moved = jnp.where(place < 32, moved, tail)
+        out = moved if out is None else jnp.where(lane < 64, out, moved)
+    return jnp.where(place < CHUNK + 2 * HALO, out, 0.0)
+
+
+def advance(state, south, north, coefs, at):
+    west_c, east_c, south_c, north_c, own_c = (ref[at : at + 8] for ref in coefs)
+    west = pltpu.roll(state, 1, axis=1)
+    east = pltpu.roll(state, LANES - 1, axis=1)
+    speed = 0.85 + 0.15 * jnp.tanh(state)
+    change = west_c * west + east_c * east
+    change = change + (south_c * south + north_c * north)
+    return state + speed * (change - own_c * state)
+
+
+def inside_body(x_ref, fields_ref, mid_ref, steps_ref, seen_ref, total_ref, *coefs):
+    fill_coefs(fields_ref[1], fields_ref[2], coefs)
+    total_ref[...] = jnp.zeros((CY - 2 * HALO, LANES), jnp.float32)
+
+    def one(index, carry):
+        pairs = [index * GROUP + p for p in range(GROUP)]
+        for p in pairs:
+            parts = halves(x_ref, 12 * p, 12 * (p + PAIRS))
+            for q in range(4):
+                rows = slice(8 * q, 8 * q + 8)
+                out = unpacked(parts, q)
+                mid_ref[p, rows] = out
+                steps_ref[0, p, rows] = fields_ref[0, rows] + 0.5 * out
+        for step in range(NSTEP):
+            for q in range(4) if step < NSTEP - 1 else (1, 2):
+                at = 8 * q
+                for p in pairs:
+                    now = steps_ref.at[step, p]
+                    state = now[at : at + 8]
+                    south = now[at - 1 : at + 7] if q else pltpu.roll(state, 1, axis=0)
+                    north = now[at + 1 : at + 9] if q < 3 else pltpu.roll(state, 7, axis=0)
+                    state = advance(state, south, north, coefs, at)
+                    if step < NSTEP - 1:
+                        steps_ref[step + 1, p, at : at + 8] = state
+                    else:
+                        seen = state + 0.25 * state * state
+                        seen_ref[p, at - 8 : at] = seen
+                        total_ref[at - 8 : at] += seen
         return carry
 
-    lax.fori_loop(0, PAIRS, one, 0, unroll=4)
-    for index in range(3):
-        low_ref[PAIRS + index] = fields_ref[index, 0:HALO]
-        high_ref[PAIRS + index] = fields_ref[index, CY - HALO : CY]
+    lax.fori_loop(0, PAIRS // GROUP, one, 0)
 
 
 def cells_body(chunk_ref, value_ref, weight_ref, column_ref, level_ref, out_ref):
@@ -161,68 +213,90 @@
         out_ref[index] = total
 
 
-def transport(base, anoms_ref, coefs, buf_ref, first, use):
-    west_c, east_c, south_c, north_c, own_c = coefs
+def transport(base, anoms, coefs, buf_ref, first, use):
     for p in range(GROUP):
-        buf_ref[0, p, HALO : HALO + ROWS] = base + 0.5 * anoms_ref[first + p]
+        at = HALO
+        for ref in anoms:
+            rows = ref.shape[1]
+            buf_ref[0, p, at : at + rows] = base[at - HALO : at - HALO + rows] + 0.5 * ref[first + p]
+            at += rows
     for step in range(NSTEP):
-        low, count = (0, ROWS) if step < NSTEP - 1 else (HALO, CY)
-        rows = slice(low, low + count)
-        at = HALO + low
-        for p in range(GROUP):
-            now = buf_ref.at[step % 2, p]
-            state = now[at : at + count]
-            south = now[at - 1 : at - 1 + count]
-            north = now[at + 1 : at + 1 + count]
-            west = pltpu.roll(state, 1, axis=1)
-            east = pltpu.roll(state, LANES - 1, axis=1)
-            speed = 0.85 + 0.15 * jnp.tanh(state)
-            change = west_c[rows] * west + east_c[rows] * east
-            change = change + (south_c[rows] * south + north_c[rows] * north)
-            state = state + speed * (change - own_c[rows] * state)
-            if step < NSTEP - 1:
-                buf_ref[(step + 1) % 2, p, at : at + count] = state
-            else:
-                use(first + p, state)
+        for low in range(0, ROWS, 8) if step < NSTEP - 1 else range(HALO, HALO + CY, 8):
+            at = HALO + low
+            for p in range(GROUP):
+                now = buf_ref.at[step % 2, p]
+                state = advance(
+                    now[at : at + 8], now[at - 1 : at + 7], now[at + 1 : at + 9], coefs, low
+                )
+                if step < NSTEP - 1:
+                    buf_ref[(step + 1) % 2, p, at : at + 8] = state
+                else:
+                    use(first + p, low - HALO, state)
+
+
+def edge_transport(base, low_ref, high_ref, coefs, steps_ref, buf_ref, use):
+    for p in range(PAIRS):
+        buf_ref[0, p, 0:HALO] = base[0:HALO] + 0.5 * low_ref[p]
+        buf_ref[1, p, 2 * HALO : 3 * HALO] = base[HALO + CY :] + 0.5 * high_ref[p]
+    for step in range(NSTEP):
+        for edge in range(2):
+            inside, put, at, low = (
+                (step, step + 8, step + 1, step + 1)
+                if edge == 0
+                else (CY - 8 - step, 8 - step, 15 - step, 39 - step)
+            )
+            for p in range(PAIRS):
+                now = buf_ref.at[edge, p]
+                now[put : put + 8] = steps_ref[step, p, inside : inside + 8]
+                state = advance(
+                    now[at : at + 8], now[at - 1 : at + 7], now[at + 1 : at + 9], coefs, low
+                )
+                if step < NSTEP - 1:
+                    now[at : at + 8] = state
+                else:
+                    use(p, (CY - HALO) * edge, state)
+
+
+def blocks(rows):
+    return [rows[8 * q : 8 * q + 8] for q in range(4)]
 
 
 def inner(rows, start):
     lane = lane_of((8, LANES))
     out = None
     for q in range(4):
-        moved = pltpu.roll(rows[8 * q : 8 * q + 8], (32 * q - HALO - start) % LANES, axis=1)
+        moved = pltpu.roll(rows[q], (32 * q - HALO - start) % LANES, axis=1)
         out = moved if out is None else jnp.where(lane >= 32 * q, moved, out)
     return out
 
 
-def observe_and_gram(
-    base, anoms_ref, coefs, cells_ref, gram_ref, buf_ref, total_ref, obs_ref, dev_ref, left_ref, right_ref
-):
-    edge = jnp.zeros((2, GROUP, HALO, LANES), jnp.float32)
-    buf_ref[:, :, 0:HALO] = edge
-    buf_ref[:, :, HALO + ROWS :] = edge
-    total_ref[...] = jnp.zeros((CY, LANES), jnp.float32)
-
-    def use(p, state):
+def observer(total_ref, obs_ref):
+    def use(p, row, state):
         seen = state + 0.25 * state * state
-        obs_ref[p] = seen
-        total_ref[...] += seen
-
+        obs_ref[p, row : row + 8] = seen
+        total_ref[row : row + 8] += seen
+
+    return use
+
+
+def for_groups(work):
     def one(index, carry):
-        transport(base, anoms_ref, coefs, buf_ref, index * GROUP, use)
+        work(index * GROUP)
         return carry
 
     lax.fori_loop(0, PAIRS // GROUP, one, 0)
-    total = total_ref[...]
+
+
+def normal_terms(rows_of, total, cells_ref, gram_ref, dev_ref, left_ref, right_ref):
     center = (total + pltpu.roll(total, 64, axis=1)) * (1.0 / MEMBERS)
     for p in range(PAIRS):
-        dev = obs_ref[p] - center
+        dev = [rows - center[8 * q : 8 * q + 8] for q, rows in enumerate(rows_of(p))]
         for half in range(2):
             at = 8 * (p + PAIRS * half)
             dev_ref[at : at + 8] = inner(dev, 64 * half)
     weight, weighted = cells_ref[0], cells_ref[1]
-    aim = inner(2.0 * (weighted - weight * center), 0)
-    weight = inner(4.0 * weight, 0)
+    aim = inner(blocks(2.0 * (weighted - weight * center)), 0)
+    weight = inner(blocks(4.0 * weight), 0)
     right_ref[MEMBERS:LANES, :] = jnp.zeros((LANES - MEMBERS, 8 * LANES), jnp.float32)
     for r in range(8):
         rows = dev_ref[pl.ds(r, MEMBERS, stride=8), :]
@@ -261,17 +335,34 @@
     own_c[...] = jnp.abs(lon) + jnp.abs(lat)
 
 
-def first_body(mid_ref, low_ref, high_ref, fields_ref, cells_ref, gram_ref, anoms_ref, full_ref, *scratch):
+def first_body(
+    low_ref, high_ref, fields_ref, steps_ref, seen_ref, total_ref, cells_ref,
+    gram_ref, south_ref, north_ref, full_ref, buf_ref, sum_ref, obs_ref, *scratch
+):
     coefs, rest = scratch[:5], scratch[5:]
-    anoms_ref[:, 0:HALO] = low_ref[0:PAIRS]
-    anoms_ref[:, HALO : HALO + CY] = mid_ref[...]
-    anoms_ref[:, HALO + CY : ROWS] = high_ref[0:PAIRS]
     for index in range(3):
-        full_ref[index, 0:HALO] = low_ref[PAIRS + index]
+        at = EDGE - 3 * HALO + HALO * index
+        full_ref[index, 0:HALO] = low_ref[at : at + HALO]
         full_ref[index, HALO : HALO + CY] = fields_ref[index]
-        full_ref[index, HALO + CY : ROWS] = high_ref[PAIRS + index]
+        full_ref[index, HALO + CY : ROWS] = high_ref[at : at + HALO]
     fill_coefs(full_ref[1], full_ref[2], coefs)
-    observe_and_gram(full_ref[0], anoms_ref, coefs, cells_ref, gram_ref, *rest)
+    sum_ref[0:HALO] = jnp.zeros((HALO, LANES), jnp.float32)
+    sum_ref[HALO : CY - HALO] = total_ref[...]
+    sum_ref[CY - HALO : CY] = jnp.zeros((HALO, LANES), jnp.float32)
+    use = observer(sum_ref, obs_ref)
+    base = full_ref[0]
+
+    for ref, out_ref in ((low_ref, south_ref), (high_ref, north_ref)):
+        for u in range(PAIRS // 4):
+            parts = halves(ref, 12 * u, 12 * (u + PAIRS // 4))
+            for i in range(4):
+                out_ref[4 * u + i] = unpacked(parts, i)
+    edge_transport(base, south_ref, north_ref, coefs, steps_ref, buf_ref, use)
+
+    def rows_of(p):
+        return [obs_ref[p, 0:8], seen_ref[p, 0:8], seen_ref[p, 8:16], obs_ref[p, 24:32]]
+
+    normal_terms(rows_of, sum_ref[...], cells_ref, gram_ref, *rest)
 
 
 def solve(core, own, other, weights):
@@ -321,29 +412,41 @@
     return jnp.where(lane < 64, weights[0:PAIRS], weights[PAIRS:MEMBERS])
 
 
-def mix(pair_ref, anoms_ref, low, rows):
-    total = jnp.zeros((rows, LANES), jnp.float32)
+def mix(pair_ref, anoms_ref):
+    total = jnp.zeros(anoms_ref.shape[1:], jnp.float32)
     for p in range(PAIRS):
-        total = total + pair_ref[p : p + 1] * anoms_ref[p, low : low + rows]
+        total = total + pair_ref[p : p + 1] * anoms_ref[p]
     return total + pltpu.roll(total, 64, axis=1)
 
 
-def second_body(core_ref, own_ref, other_ref, anoms_ref, full_ref, cells_ref, gram_ref, weights_ref, *scratch):
-    pair_ref, coefs, rest = scratch[0], scratch[1:6], scratch[6:]
+def second_body(
+    core_ref, own_ref, other_ref, south_ref, mid_ref, north_ref, full_ref, cells_ref,
+    gram_ref, weights_ref, pair_ref, buf_ref, sum_ref, obs_ref, *scratch
+):
+    coefs, rest = scratch[:5], scratch[5:]
     fill_coefs(full_ref[1], full_ref[2], coefs)
     weights = solve(
         core_ref[0], own_ref[...], other_ref[...], jnp.zeros((MEMBERS, LANES), jnp.float32)
     )
     weights_ref[...] = weights
     pair_ref[...] = by_pair(weights)
-    base = full_ref[0] + mix(pair_ref, anoms_ref, 0, ROWS)
-    observe_and_gram(base, anoms_ref, coefs, cells_ref, gram_ref, *rest)
-
-
-def last_body(core_ref, own_ref, other_ref, weights_ref, anoms_ref, out_ref, pair_ref):
+    anoms = (south_ref, mid_ref, north_ref)
+    base = full_ref[0] + jnp.concatenate([mix(pair_ref, ref) for ref in anoms], axis=0)
+    edge = jnp.zeros((2, GROUP, HALO, LANES), jnp.float32)
+    buf_ref[:, :, 0:HALO] = edge
+    buf_ref[:, :, HALO + ROWS :] = edge
+    sum_ref[...] = jnp.zeros((CY, LANES), jnp.float32)
+    use = observer(sum_ref, obs_ref)
+    for_groups(lambda first: transport(base, anoms, coefs, buf_ref, first, use))
+    normal_terms(
+        lambda p: blocks(obs_ref[p]), sum_ref[...], cells_ref, gram_ref, *rest
+    )
+
+
+def last_body(core_ref, own_ref, other_ref, weights_ref, mid_ref, out_ref, pair_ref):
     weights = solve(core_ref[0], own_ref[...], other_ref[...], weights_ref[...])
     pair_ref[...] = by_pair(weights)
-    out_ref[...] = inner(mix(pair_ref, anoms_ref, HALO, CY), 0)
+    out_ref[...] = inner(blocks(mix(pair_ref, mid_ref)), 0)
 
 
 def spread_body(core_ref, own_ref, other_ref, out_ref):
@@ -393,47 +496,54 @@
     core = lax.axis_index("core").astype(jnp.int32).reshape(1)
     pieces = call(pack_body, f32(MEMBERS * 12, LANES), in_specs=[VMEM])(anomalies[0])
     pieces = exchange(pieces.reshape(MEMBERS, 3, 4, LANES), MEM).reshape(MEMBERS * 12, LANES)
-    fields, mid, low_edge, high_edge = call(
-        pair_body,
-        (
-            f32(3, CY, LANES),
-            f32(PAIRS, CY, LANES),
-            f32(PAIRS + 3, HALO, LANES),
-            f32(PAIRS + 3, HALO, LANES),
-        ),
-        in_specs=[SMEM] + [VMEM] * 4,
-    )(chunk, pieces, background, courant_lon, courant_lat)
+    nobs = obs_value.shape[0]
+    flat = [a.reshape(1, nobs) for a in (obs_value, obs_weight, obs_column, obs_level)]
+    cells = call(cells_body, f32(2, CY, LANES), in_specs=[SMEM] + [VMEM] * 4)(chunk, *flat)
+    fields = call(fields_body, f32(3, CY, LANES), in_specs=[SMEM] + [VMEM] * 3)(
+        chunk, background, courant_lon, courant_lat
+    )
+    pieces, fields, cells = lax.optimization_barrier((pieces, fields, cells))
+    low_edge, high_edge = call(
+        edges_body, (f32(EDGE, LANES), f32(EDGE, LANES)), in_specs=[VMEM] * 2
+    )(pieces, fields)
     forward = [(i, i + 1) for i in range(7)]
     backward = [(i + 1, i) for i in range(7)]
     low = lax.ppermute(high_edge, TILE, forward)
     high = lax.ppermute(low_edge, TILE, backward)
-    nobs = obs_value.shape[0]
-    flat = [a.reshape(1, nobs) for a in (obs_value, obs_weight, obs_column, obs_level)]
-    cells = call(cells_body, f32(2, CY, LANES), in_specs=[SMEM] + [VMEM] * 4)(chunk, *flat)
-    coefs = [pltpu.VMEM((ROWS, LANES), jnp.float32)] * 5
+    mid, steps, seen, total = call(
+        inside_body,
+        (
+            f32(PAIRS, CY, LANES),
+            f32(NSTEP, PAIRS, CY, LANES),
+            f32(PAIRS, CY - 2 * HALO, LANES),
+            f32(CY - 2 * HALO, LANES),
+        ),
+        [pltpu.VMEM((CY, LANES), jnp.float32)] * 5,
+        in_specs=[VMEM] * 2,
+    )(pieces, fields)
     rest = [
-        pltpu.VMEM((2, GROUP, ROWS + 2 * HALO, LANES), jnp.float32),
         pltpu.VMEM((CY, LANES), jnp.float32),
         pltpu.VMEM((PAIRS, CY, LANES), jnp.float32),
+        *[pltpu.VMEM((ROWS, LANES), jnp.float32)] * 5,
         pltpu.VMEM((MEMBERS * 8, LANES), jnp.float32),
         pltpu.VMEM((MEMBERS, 8 * LANES), jnp.float32),
         pltpu.VMEM((LANES, 8 * LANES), jnp.float32),
     ]
     pair = pltpu.VMEM((PAIRS, LANES), jnp.float32)
-    gram, anoms, full = call(
+    gram, south, north, full = call(
         first_body,
-        (f32(PACKED, LANES), f32(PAIRS, ROWS, LANES), f32(3, ROWS, LANES)),
-        coefs + rest,
-        in_specs=[VMEM] * 5,
-    )(mid, low, high, fields, cells)
+        (f32(PACKED, LANES), *[f32(PAIRS, HALO, LANES)] * 2, f32(3, ROWS, LANES)),
+        [pltpu.VMEM((2, PAIRS, 3 * HALO, LANES), jnp.float32), *rest],
+        in_specs=[VMEM] * 7,
+    )(low, high, fields, steps, seen, total, cells)
     gram, weights = call(
         second_body,
         (f32(PACKED, LANES), f32(MEMBERS, LANES)),
-        [pair] + coefs + rest,
-        in_specs=[SMEM] + [VMEM] * 5,
-    )(core, *sum_everywhere(gram), anoms, full, cells)
+        [pair, pltpu.VMEM((2, GROUP, ROWS + 2 * HALO, LANES), jnp.float32), *rest],
+        in_specs=[SMEM] + [VMEM] * 7,
+    )(core, *sum_everywhere(gram), south, mid, north, full, cells)
     part = call(last_body, f32(8, LANES), [pair], in_specs=[SMEM] + [VMEM] * 4)(
-        core, *sum_everywhere(gram), weights, anoms
+        core, *sum_everywhere(gram), weights, mid
     )
     parts = to_all(part, ("z", "yl"), 32)
     return call(spread_body, f32(LEV, CY, NX), in_specs=[SMEM] + [VMEM] * 2)(

time: 169 us -> 166 us (0.982)
  waiting for transfers between devices: 34.7 us -> 23.9 us
  local copies, waits for them, and re-layouts: 1.19 us -> 6.86 us
  Pallas kernels: 19.2 us -> 21.5 us
    all_to_all x1, waiting for transfers between devices: 27.9 us -> 21.3 us  [exchange(): return lax.all_to_all(array, axes, 0, 0, tiled=True)]
    unnamed x16, local copies, waits for them, and re-layouts: 0.99 us -> 6.66 us
    ppermute x1, waiting for transfers between devices: 3.8 us -> 0.01 us  [local(): high = lax.ppermute(low_edge, TILE, backward)]
    pallas_call x3 -> x5, Pallas kernels: 13.4 us -> 15.7 us  [the longest x1 7.25 us: local(): call(second_body, (f32(PACKED, LANES), f32(MEMBERS, LANES)), [pair, pltpu...]
  transfers between devices with their start and end apart: 6 -> 6, of which waited for: 6 -> 4; matrix products, arithmetic and copies ran while one was open for 0% -> 0% of each run, Pallas kernels for 0% -> 3%
where the time goes in v4:
time: 166 us; the launch traced here: 165 us
  blocking collectives  77.8 us (47%)
  starting transfers between devices  35 us (21%)
  waiting for transfers between devices  23.9 us (14%)
  Pallas kernels  21.5 us (13%)
  local copies, waits for them, and re-layouts  6.86 us (4%)
    all_to_all x5, blocking collectives, exchange(): return lax.all_to_all(array, axes, 0, 0, tiled=True)  77.8 us
    all_to_all x1, waiting for transfers between devices, exchange(): return lax.all_to_all(array, axes, 0, 0, tiled=True)  21.3 us
    all_to_all x1, starting transfers between devices, exchange(): return lax.all_to_all(array, axes, 0, 0, tiled=True)  18.2 us
    ppermute x3, starting transfers between devices, swap_cores(): return lax.ppermute(array, 'core', [(0, 1), (1, 0)])  12.5 us
    pallas_call x1, Pallas kernels, local(): call(second_body, (f32(PACKED, LANES), f32(MEMBERS, LANES)), [pair, pltpu...  7.25 us
    unnamed x16, local copies, waits for them, and re-layouts  6.66 us
    pallas_call x1, Pallas kernels, local(): call(inside_body, (f32(PAIRS, CY, LANES), f32(NSTEP, PAIRS, CY, LANES), f...  4.39 us
    pallas_call x1, Pallas kernels, local(): call(first_body, (f32(PACKED, LANES), *[f32(PAIRS, HALO, LANES)] * 2, f32...  3.66 us
  transfers between devices with their start and end apart: 6, of which 4 were waited for; matrix products, arithmetic and copies ran while one was open for 0% of the time, Pallas kernels for 3%

profile of v4, /device:TPU:1, one launch (start us, length us, event | category | flops | bytes accessed | tf_op | source)
XLA Modules:
  0.0 165.5 jit_solution(1979159260376880262)
XLA Ops:
  0.0 0.9 copy-done.3
  1.0 1.6 shard_map.82
  2.6 18.2 %all-to-all-start = ((f32[64,3,4,128]{3,2,1,0:T(4,128)}), f32[64,3,4,128]{3,2,1,0:T(4,128)S(1)}, u32[]{:S(2)}, u32[]{:S(2)}) async-start(f32[64,3,4,128]{3,2,1,0:T(4,128)} %bitcast.2), calls=%async_computation | async-start | bytes 786432 | tf_op jit(solution)/shard_map/all_to_all | solution.py:473
  20.8 0.9 copy-done
  21.7 0.9 copy-done.1
  22.6 0.9 copy-done.2
  27.3 21.3 %all-to-all-done = f32[64,3,4,128]{3,2,1,0:T(4,128)S(1)} async-done(((f32[64,3,4,128]{3,2,1,0:T(4,128)}), f32[64,3,4,128]{3,2,1,0:T(4,128)S(1)}, u32[]{:S(2)}, u32[]{:S(2)}) %all-to-all-start) | async-done | bytes 393248 | tf_op jit(solution)/shard_map/all_to_all | solution.py:473
  48.9 3.1 %collective-permute-start = (f32[216,128]{1,0:T(8,128)S(1)}, f32[216,128]{1,0:T(8,128)S(1)}, u32[]{:S(2)}, u32[]{:S(2)}) collective-permute-start(f32[216,128]{1,0:T(8,128)S(1)} %get-tuple-element.22), channel_id=1, source_target_pairs={{0,1},{1,2},{2,3},{3,4},{4,5},{5,6},{6,7},{8,9},{9,10},{10,11},{11... | collective-permute-start | bytes 331784 | tf_op jit(solution)/shard_map/ppermute | solution.py:511
  52.0 1.3 collective-permute-start.1
  53.3 4.4 %shard_map.86 = (f32[32,32,128]{2,1,0:T(8,128)S(1)}, f32[8,32,32,128]{3,2,1,0:T(8,128)S(1)}, f32[32,16,128]{2,1,0:T(8,128)S(1)}, f32[16,128]{1,0:T(8,128)S(1)}) custom-call(f32[768,128]{1,0:T(8,128)S(1)} %bitcast.12, f32[3,32,128]{2,1,0:T(8,128)S(1)} %shard_map.83.fields_ref), custom_call_target="tpu_custom_call" | custom-call | tf_op jit(solution)/shard_map/pallas_call | solution.py:513
  57.7 3.7 %shard_map.87 = (f32[20,128]{1,0:T(8,128)S(1)}, f32[32,8,128]{2,1,0:T(8,128)S(1)}, f32[32,8,128]{2,1,0:T(8,128)S(1)}, f32[3,48,128]{2,1,0:T(8,128)S(1)}) custom-call(f32[216,128]{1,0:T(8,128)S(1)} %collective-permute-done.low_ref, f32[216,128]{1,0:T(8,128)S(1)} %collective-permute-done.1.high_ref, f32[3,32,128]{2,1,0:T(8,128)S(1)} %shard_map.83.fields_ref, ...), custom_call_target="tpu_custom_call" | custom-call | tf_op jit(solution)/shard_map/pallas_call | solution.py:533
  61.5 19.0 %all_to_all.30 = f32[32,5,2,128]{3,2,1,0:T(2,128)S(1)} all-to-all(f32[32,5,2,128]{3,2,1,0:T(2,128)S(1)} %bitcast.18), channel_id=1, replica_groups=mesh['z'=16,'yl'=2,'core'=2,'yh'=2,'x'=4] {'yl','core','yh','x'}, dimensions={0} | all-to-all | bytes 327680 | tf_op jit(solution)/shard_map/all_to_all | solution.py:473
  80.6 14.3 %all_to_all.31 = f32[16,5,2,128]{3,2,1,0:T(2,128)S(1)} all-to-all(f32[16,5,2,128]{3,2,1,0:T(2,128)S(1)} %broadcast_in_dim.16), channel_id=1, replica_groups=mesh['z'=16,'yl'=2,'core'=2,'yh'=2,'x'=4] {'z'}, dimensions={0} | all-to-all | bytes 163840 | tf_op jit(solution)/shard_map/all_to_all | solution.py:473
  94.9 4.2 %collective-permute-start.2 = (f32[10,128]{1,0:T(8,128)S(1)}, f32[10,128]{1,0:T(8,128)S(1)}, u32[]{:S(2)}, u32[]{:S(2)}) collective-permute-start(f32[10,128]{1,0:T(8,128)S(1)} %reshape.52.own_ref), channel_id=1, source_target_pairs={{0,8},{8,0},{1,9},{9,1},{2,10},{10,2},{3,11},{11,3},{4,12},{12,4},... | collective-permute-start | bytes 15368 | tf_op jit(solution)/shard_map/ppermute | solution.py:481
  99.1 0.8 collective-permute-done.2.other_ref
  99.9 7.2 %shard_map.88 = (f32[20,128]{1,0:T(8,128)S(1)}, f32[64,128]{1,0:T(8,128)S(1)}) custom-call(s32[1]{0:T(128)} %bitcast.core_ref, f32[10,128]{1,0:T(8,128)S(1)} %reshape.52.own_ref, f32[10,128]{1,0:T(8,128)S(1)} %collective-permute-done.2.other_ref, f32[32,8,128]{2,1,0:T(8,128)S(1)} %get-tuple-element.29.south_ref, ...), custom_call_target="tpu_custom_call" | custom-call | tf_op jit(solution)/shard_map/pallas_call | solution.py:539
  107.3 11.5 %all_to_all.32 = f32[32,5,2,128]{3,2,1,0:T(2,128)S(1)} all-to-all(f32[32,5,2,128]{3,2,1,0:T(2,128)S(1)} %bitcast.19), channel_id=1, replica_groups=mesh['z'=16,'yl'=2,'core'=2,'yh'=2,'x'=4] {'yl','core','yh','x'}, dimensions={0} | all-to-all | bytes 327680 | tf_op jit(solution)/shard_map/all_to_all | solution.py:473
  118.9 14.8 %all_to_all.33 = f32[16,5,2,128]{3,2,1,0:T(2,128)S(1)} all-to-all(f32[16,5,2,128]{3,2,1,0:T(2,128)S(1)} %broadcast_in_dim.37), channel_id=1, replica_groups=mesh['z'=16,'yl'=2,'core'=2,'yh'=2,'x'=4] {'z'}, dimensions={0} | all-to-all | bytes 163840 | tf_op jit(solution)/shard_map/all_to_all | solution.py:473
  133.7 4.2 %collective-permute-start.3 = (f32[10,128]{1,0:T(8,128)S(1)}, f32[10,128]{1,0:T(8,128)S(1)}, u32[]{:S(2)}, u32[]{:S(2)}) collective-permute-start(f32[10,128]{1,0:T(8,128)S(1)} %reshape.54.own_ref), channel_id=1, source_target_pairs={{0,8},{8,0},{1,9},{9,1},{2,10},{10,2},{3,11},{11,3},{4,12},{12,4},... | collective-permute-start | bytes 15368 | tf_op jit(solution)/shard_map/ppermute | solution.py:481
  138.7 2.5 %shard_map.89 = f32[8,128]{1,0:T(8,128)S(1)} custom-call(s32[1]{0:T(128)} %bitcast.core_ref, f32[10,128]{1,0:T(8,128)S(1)} %reshape.54.own_ref, f32[10,128]{1,0:T(8,128)S(1)} %collective-permute-done.3.other_ref, f32[64,128]{1,0:T(8,128)S(1)} %get-tuple-element.34.weights_ref, f32[32,32,128]{2,1,0:T(8,128)S(1)} %get-tuple-element.30.mid_ref), custom_call_target="tpu_custom_call" | custom-call | tf_op jit(solution)/shard_map/pallas_call | solution.py:545
  141.2 18.2 %all_to_all.34.own_ref = f32[32,8,128]{2,1,0:T(8,128)S(1)} all-to-all(f32[32,8,128]{2,1,0:T(8,128)S(1)} %broadcast_in_dim.38), channel_id=1, replica_groups=mesh['z'=16,'yl'=2,'core'=2,'yh'=2,'x'=4] {'z','yl'}, dimensions={0} | all-to-all | bytes 262144 | tf_op jit(solution)/shard_map/all_to_all | solution.py:473
  159.5 4.0 %collective-permute-start.4 = (f32[32,8,128]{2,1,0:T(8,128)S(1)}, f32[32,8,128]{2,1,0:T(8,128)S(1)}, u32[]{:S(2)}, u32[]{:S(2)}) collective-permute-start(f32[32,8,128]{2,1,0:T(8,128)S(1)} %all_to_all.34.own_ref), channel_id=1, source_target_pairs={{0,8},{8,0},{1,9},{9,1},{2,10},{10,2},{3,11},{11,3},{4,12},{12,4},... | collective-permute-start | bytes 393224 | tf_op jit(solution)/shard_map/ppermute | solution.py:481
  163.5 1.0 collective-permute-done.4.other_ref
  164.5 1.0 shard_map.90
  (31 shorter events, 5.2 us)
Async XLA Ops:
  0.0 0.9 copy-start.3
  2.6 46.1 %all-to-all-start = ((f32[64,3,4,128]{3,2,1,0:T(4,128)}), f32[64,3,4,128]{3,2,1,0:T(4,128)S(1)}, u32[]{:S(2)}, u32[]{:S(2)}) async-start(f32[64,3,4,128]{3,2,1,0:T(4,128)} %bitcast.2), calls=%async_computation | async-start | bytes 786432 | tf_op jit(solution)/shard_map/all_to_all | solution.py:473
  20.7 1.0 copy-start
  21.7 0.9 copy-start.1
  22.6 0.9 copy-start.2
  23.8 0.7 copy-start.4
  24.5 0.7 copy-start.5
  25.2 0.7 copy-start.6
  25.9 0.7 copy-start.7
  48.9 8.8 %collective-permute-start = (f32[216,128]{1,0:T(8,128)S(1)}, f32[216,128]{1,0:T(8,128)S(1)}, u32[]{:S(2)}, u32[]{:S(2)}) collective-permute-start(f32[216,128]{1,0:T(8,128)S(1)} %get-tuple-element.22), channel_id=1, source_target_pairs={{0,1},{1,2},{2,3},{3,4},{4,5},{5,6},{6,7},{8,9},{9,10},{10,11},{11... | collective-permute-start | bytes 331784 | tf_op jit(solution)/shard_map/ppermute | solution.py:511
  52.0 5.7 %collective-permute-start.1 = (f32[216,128]{1,0:T(8,128)S(1)}, f32[216,128]{1,0:T(8,128)S(1)}, u32[]{:S(2)}, u32[]{:S(2)}) collective-permute-start(f32[216,128]{1,0:T(8,128)S(1)} %get-tuple-element.23), channel_id=1, source_target_pairs={{1,0},{2,1},{3,2},{4,3},{5,4},{6,5},{7,6},{9,8},{10,9},{11,10},{12... | collective-permute-start | bytes 331784 | tf_op jit(solution)/shard_map/ppermute | solution.py:512
  94.9 5.0 %collective-permute-start.2 = (f32[10,128]{1,0:T(8,128)S(1)}, f32[10,128]{1,0:T(8,128)S(1)}, u32[]{:S(2)}, u32[]{:S(2)}) collective-permute-start(f32[10,128]{1,0:T(8,128)S(1)} %reshape.52.own_ref), channel_id=1, source_target_pairs={{0,8},{8,0},{1,9},{9,1},{2,10},{10,2},{3,11},{11,3},{4,12},{12,4},... | collective-permute-start | bytes 15368 | tf_op jit(solution)/shard_map/ppermute | solution.py:481
  133.7 5.0 %collective-permute-start.3 = (f32[10,128]{1,0:T(8,128)S(1)}, f32[10,128]{1,0:T(8,128)S(1)}, u32[]{:S(2)}, u32[]{:S(2)}) collective-permute-start(f32[10,128]{1,0:T(8,128)S(1)} %reshape.54.own_ref), channel_id=1, source_target_pairs={{0,8},{8,0},{1,9},{9,1},{2,10},{10,2},{3,11},{11,3},{4,12},{12,4},... | collective-permute-start | bytes 15368 | tf_op jit(solution)/shard_map/ppermute | solution.py:481
  159.5 5.0 %collective-permute-start.4 = (f32[32,8,128]{2,1,0:T(8,128)S(1)}, f32[32,8,128]{2,1,0:T(8,128)S(1)}, u32[]{:S(2)}, u32[]{:S(2)}) collective-permute-start(f32[32,8,128]{2,1,0:T(8,128)S(1)} %all_to_all.34.own_ref), channel_id=1, source_target_pairs={{0,8},{8,0},{1,9},{9,1},{2,10},{10,2},{3,11},{11,3},{4,12},{12,4},... | collective-permute-start | bytes 393224 | tf_op jit(solution)/shard_map/ppermute | solution.py:481

commit v5 on v4

--- a/solution.py
+++ b/solution.py
@@ -74,10 +74,10 @@
         for b in range(8):
             for k in range(4):
                 at = 12 * (32 * lev + 4 * b + k)
-                pieces_ref[at : at + 8] = gather(b, k)
+                pieces_ref[at + 4 : at + 12] = gather(b, k)
                 rest = gather(b, k + 1) if k < 3 else gather((b + 1) % 8, 0)
                 other = pltpu.roll(rest, 16, axis=1)
-                pieces_ref[at + 8 : at + 12] = jnp.where(
+                pieces_ref[at : at + 4] = jnp.where(
                     lane[0:4] % 32 < 16, rest[0:4], other[4:8]
                 )
 
@@ -100,18 +100,20 @@
 
 
 def edges_body(x_ref, fields_ref, low_ref, high_ref):
-    lane = lane_of((12, LANES))
     for u in range(MEMBERS // 4):
-        low, high = None, None
-        for i in range(4):
-            at = 12 * (4 * u + i)
-            piece = x_ref[at : at + 12]
-            first = pltpu.roll(piece, 32 * i, axis=1) if i else piece
-            last = pltpu.roll(piece, (32 * i + 32) % LANES, axis=1) if i < 3 else piece
-            low = first if i == 0 else jnp.where(lane >= 32 * i, first, low)
-            high = last if i == 0 else jnp.where(lane >= 32 * i, last, high)
-        low_ref[12 * u : 12 * u + 12] = low
-        high_ref[12 * u : 12 * u + 12] = high
+        for row, count in ((0, 4), (4, 8)):
+            lane = lane_of((count, LANES))
+            low, high = None, None
+            for i in range(4):
+                at = 12 * (4 * u + i) + row
+                piece = x_ref[at : at + count]
+                first = pltpu.roll(piece, 32 * i, axis=1) if i else piece
+                last = pltpu.roll(piece, (32 * i + 32) % LANES, axis=1) if i < 3 else piece
+                low = first if i == 0 else jnp.where(lane >= 32 * i, first, low)
+                high = last if i == 0 else jnp.where(lane >= 32 * i, last, high)
+            at = 12 * u + row
+            low_ref[at : at + count] = low
+            high_ref[at : at + count] = high
     for index in range(3):
         at = EDGE - 3 * HALO + HALO * index
         low_ref[at : at + HALO] = fields_ref[index, 0:HALO]
@@ -121,9 +123,9 @@
 def halves(ref, first, second):
     parts = []
     for at in (first, second):
-        rest = ref[pl.ds(at + 8, 4)]
+        rest = ref[pl.ds(at, 4)]
         rest = jnp.concatenate([rest, pltpu.roll(rest, LANES - 16, axis=1)], axis=0)
-        parts.append((ref[pl.ds(at, 8)], rest))
+        parts.append((ref[pl.ds(at + 4, 8)], rest))
     return parts
 
 
@@ -365,12 +367,12 @@
     normal_terms(rows_of, sum_ref[...], cells_ref, gram_ref, *rest)
 
 
-def solve(core, own, other, weights):
+def solve(packed, weights):
     shape = (MEMBERS, LANES)
     wide = lane_of(shape)
     sub = lax.broadcasted_iota(jnp.int32, shape, 0)
     left = MEMBERS - 1.0
-    low, high = jnp.where(core == 0, own, other), jnp.where(core == 0, other, own)
+    low, high = packed[0], packed[1]
     packed = jnp.concatenate([low[0:8], high[0:8]], axis=0)
     ends = jnp.broadcast_to(low[8:9], shape)
     square = jnp.concatenate([packed, pltpu.roll(packed, 64, axis=1)], axis=0)
@@ -420,14 +422,12 @@
 
 
 def second_body(
-    core_ref, own_ref, other_ref, south_ref, mid_ref, north_ref, full_ref, cells_ref,
+    sums_ref, south_ref, mid_ref, north_ref, full_ref, cells_ref,
     gram_ref, weights_ref, pair_ref, buf_ref, sum_ref, obs_ref, *scratch
 ):
     coefs, rest = scratch[:5], scratch[5:]
     fill_coefs(full_ref[1], full_ref[2], coefs)
-    weights = solve(
-        core_ref[0], own_ref[...], other_ref[...], jnp.zeros((MEMBERS, LANES), jnp.float32)
-    )
+    weights = solve(sums_ref[...], jnp.zeros((MEMBERS, LANES), jnp.float32))
     weights_ref[...] = weights
     pair_ref[...] = by_pair(weights)
     anoms = (south_ref, mid_ref, north_ref)
@@ -443,24 +443,17 @@
     )
 
 
-def last_body(core_ref, own_ref, other_ref, weights_ref, mid_ref, out_ref, pair_ref):
-    weights = solve(core_ref[0], own_ref[...], other_ref[...], weights_ref[...])
+def last_body(sums_ref, weights_ref, mid_ref, out_ref, pair_ref):
+    weights = solve(sums_ref[...], weights_ref[...])
     pair_ref[...] = by_pair(weights)
     out_ref[...] = inner(blocks(mix(pair_ref, mid_ref)), 0)
 
 
-def spread_body(core_ref, own_ref, other_ref, out_ref):
+def spread_body(pieces_ref, out_ref):
     lane = lane_of((8, LANES))
-    first = core_ref[0] == 0
     for lev in range(LEV):
         for b in range(8):
-            pieces = []
-            for k in range(4):
-                at = 16 * lev + 2 * b + k // 2
-                own, other = own_ref[at], other_ref[at]
-                if k % 2:
-                    own, other = other, own
-                pieces.append(jnp.where(first, own, other))
+            pieces = [pieces_ref[k % 2, 16 * lev + 2 * b + k // 2] for k in range(4)]
             for q in range(4):
                 out = None
                 for k in range(4):
@@ -477,8 +470,8 @@
     return exchange(jnp.broadcast_to(array[None], (count, *array.shape)), axes)
 
 
-def swap_cores(array):
-    return lax.ppermute(array, "core", [(0, 1), (1, 0)])
+def both_cores(array):
+    return lax.all_gather(array, "core")
 
 
 def sum_everywhere(packed):
@@ -486,14 +479,13 @@
     halves = jnp.broadcast_to(packed.reshape(1, 2, 1, *shape), (2, 2, 8, *shape))
     part = jnp.sum(exchange(halves.reshape(32, *shape), PLANE), axis=0)
     part = jnp.sum(to_all(part, "z", 16), axis=0).reshape(10, LANES)
-    return part, swap_cores(part)
+    return both_cores(part)
 
 
 def local(
     background, anomalies, courant_lon, courant_lat, obs_value, obs_weight, obs_column, obs_level
 ):
     chunk = lax.axis_index(MEM).astype(jnp.int32).reshape(1)
-    core = lax.axis_index("core").astype(jnp.int32).reshape(1)
     pieces = call(pack_body, f32(MEMBERS * 12, LANES), in_specs=[VMEM])(anomalies[0])
     pieces = exchange(pieces.reshape(MEMBERS, 3, 4, LANES), MEM).reshape(MEMBERS * 12, LANES)
     nobs = obs_value.shape[0]
@@ -540,15 +532,13 @@
         second_body,
         (f32(PACKED, LANES), f32(MEMBERS, LANES)),
         [pair, pltpu.VMEM((2, GROUP, ROWS + 2 * HALO, LANES), jnp.float32), *rest],
-        in_specs=[SMEM] + [VMEM] * 7,
-    )(core, *sum_everywhere(gram), south, mid, north, full, cells)
-    part = call(last_body, f32(8, LANES), [pair], in_specs=[SMEM] + [VMEM] * 4)(
-        core, *sum_everywhere(gram), weights, mid
-    )
-    parts = to_all(part, ("z", "yl"), 32)
-    return call(spread_body, f32(LEV, CY, NX), in_specs=[SMEM] + [VMEM] * 2)(
-        core, parts, swap_cores(parts)
-    )
+        in_specs=[VMEM] * 6,
+    )(sum_everywhere(gram), south, mid, north, full, cells)
+    part = call(last_body, f32(8, LANES), [pair], in_specs=[VMEM] * 3)(
+        sum_everywhere(gram), weights, mid
+    )
+    parts = both_cores(to_all(part, ("z", "yl"), 32))
+    return call(spread_body, f32(LEV, CY, NX), in_specs=[VMEM])(parts)
 
 
 def solution(mesh):

time: 166 us -> 163 us (0.982)
  starting transfers between devices: 35 us -> 22.6 us
  blocking collectives: 77.8 us -> 89.2 us
  waiting for transfers between devices: 23.9 us -> 21.3 us
    ppermute x3 -> x0, starting transfers between devices: 12.5 us -> none  [swap_cores(): return lax.ppermute(array, 'core', [(0, 1), (1, 0)])]
    all_gather x0 -> x3, blocking collectives: none -> 11.4 us  [both_cores(): return lax.all_gather(array, 'core')]
    ppermute x3 -> x0, waiting for transfers between devices: 2.58 us -> none  [swap_cores(): return lax.ppermute(array, 'core', [(0, 1), (1, 0)])]
  transfers between devices with their start and end apart: 6 -> 3, of which waited for: 4 -> 1; matrix products, arithmetic and copies ran while one was open for 0% -> 0% of each run, Pallas kernels for 3% -> 3%
where the time goes in v5:
time: 163 us; the launch traced here: 162 us
  blocking collectives  89.2 us (55%)
  starting transfers between devices  22.6 us (14%)
  Pallas kernels  21.5 us (13%)
  waiting for transfers between devices  21.3 us (13%)
  local copies, waits for them, and re-layouts  6.86 us (4%)
    all_to_all x5, blocking collectives, exchange(): return lax.all_to_all(array, axes, 0, 0, tiled=True)  77.8 us
    all_to_all x1, waiting for transfers between devices, exchange(): return lax.all_to_all(array, axes, 0, 0, tiled=True)  21.3 us
    all_to_all x1, starting transfers between devices, exchange(): return lax.all_to_all(array, axes, 0, 0, tiled=True)  18.2 us
    all_gather x3, blocking collectives, both_cores(): return lax.all_gather(array, 'core')  11.4 us
    pallas_call x1, Pallas kernels, local(): call(second_body, (f32(PACKED, LANES), f32(MEMBERS, LANES)), [pair, pltpu...  7.25 us
    unnamed x16, local copies, waits for them, and re-layouts  6.66 us
    pallas_call x1, Pallas kernels, local(): call(inside_body, (f32(PAIRS, CY, LANES), f32(NSTEP, PAIRS, CY, LANES), f...  4.39 us
    pallas_call x1, Pallas kernels, local(): call(first_body, (f32(PACKED, LANES), *[f32(PAIRS, HALO, LANES)] * 2, f32...  3.65 us
  transfers between devices with their start and end apart: 3, of which 1 were waited for; matrix products, arithmetic and copies ran while one was open for 0% of the time, Pallas kernels for 3%

profile of v5, /device:TPU:1, one launch (start us, length us, event | category | flops | bytes accessed | tf_op | source)
XLA Modules:
  0.0 161.7 jit_solution(9170323759879349563)
XLA Ops:
  0.0 0.9 copy-done.3
  1.0 1.6 shard_map.82
  2.6 18.2 %all-to-all-start = ((f32[64,3,4,128]{3,2,1,0:T(4,128)}), f32[64,3,4,128]{3,2,1,0:T(4,128)S(1)}, u32[]{:S(2)}, u32[]{:S(2)}) async-start(f32[64,3,4,128]{3,2,1,0:T(4,128)} %bitcast.1), calls=%async_computation | async-start | bytes 786432 | tf_op jit(solution)/shard_map/all_to_all | solution.py:466
  20.8 0.9 copy-done
  21.7 0.9 copy-done.1
  22.6 0.9 copy-done.2
  24.5 0.7 copy-done.5
  25.2 0.7 copy-done.6
  27.3 21.3 %all-to-all-done = f32[64,3,4,128]{3,2,1,0:T(4,128)S(1)} async-done(((f32[64,3,4,128]{3,2,1,0:T(4,128)}), f32[64,3,4,128]{3,2,1,0:T(4,128)S(1)}, u32[]{:S(2)}, u32[]{:S(2)}) %all-to-all-start) | async-done | bytes 393248 | tf_op jit(solution)/shard_map/all_to_all | solution.py:466
  48.9 3.1 %collective-permute-start = (f32[216,128]{1,0:T(8,128)S(1)}, f32[216,128]{1,0:T(8,128)S(1)}, u32[]{:S(2)}, u32[]{:S(2)}) collective-permute-start(f32[216,128]{1,0:T(8,128)S(1)} %get-tuple-element.22), channel_id=1, source_target_pairs={{0,1},{1,2},{2,3},{3,4},{4,5},{5,6},{6,7},{8,9},{9,10},{10,11},{11... | collective-permute-start | bytes 331784 | tf_op jit(solution)/shard_map/ppermute | solution.py:503
  52.0 1.3 collective-permute-start.1
  53.3 4.4 %shard_map.86 = (f32[32,32,128]{2,1,0:T(8,128)S(1)}, f32[8,32,32,128]{3,2,1,0:T(8,128)S(1)}, f32[32,16,128]{2,1,0:T(8,128)S(1)}, f32[16,128]{1,0:T(8,128)S(1)}) custom-call(f32[768,128]{1,0:T(8,128)S(1)} %bitcast.12, f32[3,32,128]{2,1,0:T(8,128)S(1)} %shard_map.83.fields_ref), custom_call_target="tpu_custom_call" | custom-call | tf_op jit(solution)/shard_map/pallas_call | solution.py:505
  57.7 3.7 %shard_map.87 = (f32[20,128]{1,0:T(8,128)S(1)}, f32[32,8,128]{2,1,0:T(8,128)S(1)}, f32[32,8,128]{2,1,0:T(8,128)S(1)}, f32[3,48,128]{2,1,0:T(8,128)S(1)}) custom-call(f32[216,128]{1,0:T(8,128)S(1)} %collective-permute-done.low_ref, f32[216,128]{1,0:T(8,128)S(1)} %collective-permute-done.1.high_ref, f32[3,32,128]{2,1,0:T(8,128)S(1)} %shard_map.83.fields_ref, ...), custom_call_target="tpu_custom_call" | custom-call | tf_op jit(solution)/shard_map/pallas_call | solution.py:525
  61.5 19.0 %all_to_all.30 = f32[32,5,2,128]{3,2,1,0:T(2,128)S(1)} all-to-all(f32[32,5,2,128]{3,2,1,0:T(2,128)S(1)} %bitcast.19), channel_id=1, replica_groups=mesh['z'=16,'yl'=2,'core'=2,'yh'=2,'x'=4] {'yl','core','yh','x'}, dimensions={0} | all-to-all | bytes 327680 | tf_op jit(solution)/shard_map/all_to_all | solution.py:466
  80.6 14.3 %all_to_all.31 = f32[16,5,2,128]{3,2,1,0:T(2,128)S(1)} all-to-all(f32[16,5,2,128]{3,2,1,0:T(2,128)S(1)} %broadcast_in_dim.16), channel_id=1, replica_groups=mesh['z'=16,'yl'=2,'core'=2,'yh'=2,'x'=4] {'z'}, dimensions={0} | all-to-all | bytes 163840 | tf_op jit(solution)/shard_map/all_to_all | solution.py:466
  94.9 3.8 %all_gather.12.sums_ref = f32[2,10,128]{2,1,0:T(8,128)S(1)} all-gather(f32[1,10,128]{2,1,0:T(8,128)S(1)} %all_gather_reshape.6), channel_id=1, replica_groups=mesh['z'=16,'yl'=2,'core'=2,'yh'=2,'x'=4] {'core'}, dimensions={0}, use_global_device_ids=true | all-gather | bytes 15360 | tf_op jit(solution)/shard_map/all_gather | solution.py:474
  98.7 7.2 %shard_map.88 = (f32[20,128]{1,0:T(8,128)S(1)}, f32[64,128]{1,0:T(8,128)S(1)}) custom-call(f32[2,10,128]{2,1,0:T(8,128)S(1)} %all_gather.12.sums_ref, f32[32,8,128]{2,1,0:T(8,128)S(1)} %get-tuple-element.29.south_ref, f32[32,32,128]{2,1,0:T(8,128)S(1)} %get-tuple-element.30.mid_ref, f32[32,8,128]{2,1,0:T(8,128)S(1)} %get-tuple-element.31.north_ref, ...), custom_call_target="tpu_custom_call" | custom-call | tf_op jit(solution)/shard_map/pallas_call | solution.py:531
  106.0 11.5 %all_to_all.32 = f32[32,5,2,128]{3,2,1,0:T(2,128)S(1)} all-to-all(f32[32,5,2,128]{3,2,1,0:T(2,128)S(1)} %bitcast.20), channel_id=1, replica_groups=mesh['z'=16,'yl'=2,'core'=2,'yh'=2,'x'=4] {'yl','core','yh','x'}, dimensions={0} | all-to-all | bytes 327680 | tf_op jit(solution)/shard_map/all_to_all | solution.py:466
  117.7 14.8 %all_to_all.33 = f32[16,5,2,128]{3,2,1,0:T(2,128)S(1)} all-to-all(f32[16,5,2,128]{3,2,1,0:T(2,128)S(1)} %broadcast_in_dim.37), channel_id=1, replica_groups=mesh['z'=16,'yl'=2,'core'=2,'yh'=2,'x'=4] {'z'}, dimensions={0} | all-to-all | bytes 163840 | tf_op jit(solution)/shard_map/all_to_all | solution.py:466
  132.5 3.8 %all_gather.13.sums_ref = f32[2,10,128]{2,1,0:T(8,128)S(1)} all-gather(f32[1,10,128]{2,1,0:T(8,128)S(1)} %all_gather_reshape.7), channel_id=1, replica_groups=mesh['z'=16,'yl'=2,'core'=2,'yh'=2,'x'=4] {'core'}, dimensions={0}, use_global_device_ids=true | all-gather | bytes 15360 | tf_op jit(solution)/shard_map/all_gather | solution.py:474
  136.2 2.5 %shard_map.89 = f32[8,128]{1,0:T(8,128)S(1)} custom-call(f32[2,10,128]{2,1,0:T(8,128)S(1)} %all_gather.13.sums_ref, f32[64,128]{1,0:T(8,128)S(1)} %get-tuple-element.34.weights_ref, f32[32,32,128]{2,1,0:T(8,128)S(1)} %get-tuple-element.30.mid_ref), custom_call_target="tpu_custom_call" | custom-call | tf_op jit(solution)/shard_map/pallas_call | solution.py:537
  138.8 18.2 %all_to_all.34 = f32[32,8,128]{2,1,0:T(8,128)S(1)} all-to-all(f32[32,8,128]{2,1,0:T(8,128)S(1)} %broadcast_in_dim.38), channel_id=1, replica_groups=mesh['z'=16,'yl'=2,'core'=2,'yh'=2,'x'=4] {'z','yl'}, dimensions={0} | all-to-all | bytes 262144 | tf_op jit(solution)/shard_map/all_to_all | solution.py:466
  157.0 3.8 %all-gather = f32[64,8,128]{2,1,0:T(8,128)S(1)} all-gather(f32[32,8,128]{2,1,0:T(8,128)S(1)} %all_to_all.34), channel_id=2, replica_groups=mesh['z'=16,'yl'=2,'core'=2,'yh'=2,'x'=4] {'core'}, dimensions={0}, use_global_device_ids=true | all-gather | bytes 393216 | tf_op jit(solution)/shard_map/all_gather | solution.py:474
  160.8 1.0 shard_map.90
  (28 shorter events, 3.0 us)
Async XLA Ops:
  0.0 0.9 copy-start.3
  2.6 46.1 %all-to-all-start = ((f32[64,3,4,128]{3,2,1,0:T(4,128)}), f32[64,3,4,128]{3,2,1,0:T(4,128)S(1)}, u32[]{:S(2)}, u32[]{:S(2)}) async-start(f32[64,3,4,128]{3,2,1,0:T(4,128)} %bitcast.1), calls=%async_computation | async-start | bytes 786432 | tf_op jit(solution)/shard_map/all_to_all | solution.py:466
  20.7 1.0 copy-start
  21.7 0.9 copy-start.1
  22.6 0.9 copy-start.2
  23.8 0.7 copy-start.4
  24.5 0.7 copy-start.5
  25.2 0.7 copy-start.6
  25.9 0.7 copy-start.7
  48.9 8.8 %collective-permute-start = (f32[216,128]{1,0:T(8,128)S(1)}, f32[216,128]{1,0:T(8,128)S(1)}, u32[]{:S(2)}, u32[]{:S(2)}) collective-permute-start(f32[216,128]{1,0:T(8,128)S(1)} %get-tuple-element.22), channel_id=1, source_target_pairs={{0,1},{1,2},{2,3},{3,4},{4,5},{5,6},{6,7},{8,9},{9,10},{10,11},{11... | collective-permute-start | bytes 331784 | tf_op jit(solution)/shard_map/ppermute | solution.py:503
  52.0 5.7 %collective-permute-start.1 = (f32[216,128]{1,0:T(8,128)S(1)}, f32[216,128]{1,0:T(8,128)S(1)}, u32[]{:S(2)}, u32[]{:S(2)}) collective-permute-start(f32[216,128]{1,0:T(8,128)S(1)} %get-tuple-element.23), channel_id=1, source_target_pairs={{1,0},{2,1},{3,2},{4,3},{5,4},{6,5},{7,6},{9,8},{10,9},{11,10},{12... | collective-permute-start | bytes 331784 | tf_op jit(solution)/shard_map/ppermute | solution.py:504

commit v6 on v5

--- a/solution.py
+++ b/solution.py
@@ -10,7 +10,7 @@
 NSTEP = 8
 MEMBERS = 64
 PAIRS = 32
-GROUP = 8
+GROUP = 16
 LEV = 2
 CY = 32
 NX = 1024
@@ -65,21 +65,23 @@
                 ]
             )
 
-        def gather(b, k):
-            out = turned[0][b][(-k) % 4]
-            for q in range(1, 4):
-                out = jnp.where(lane >= 32 * q, turned[q][b][(q - k) % 4], out)
-            return out
-
         for b in range(8):
             for k in range(4):
                 at = 12 * (32 * lev + 4 * b + k)
-                pieces_ref[at + 4 : at + 12] = gather(b, k)
-                rest = gather(b, k + 1) if k < 3 else gather((b + 1) % 8, 0)
+                near = [turned[q][b][(q - k) % 4] for q in range(4)]
+                after = near if k < 3 else [turned[q][(b + 1) % 8][(q - k) % 4] for q in range(4)]
+                pieces_ref[at + 4 : at + 12] = in_groups(near)
+                rest = in_groups(after[3:] + after[:3])
                 other = pltpu.roll(rest, 16, axis=1)
-                pieces_ref[at : at + 4] = jnp.where(
-                    lane[0:4] % 32 < 16, rest[0:4], other[4:8]
-                )
+                pieces_ref[at : at + 4] = jnp.where(lane[0:4] % 32 < 16, rest[0:4], other[4:8])
+
+
+def in_groups(parts):
+    group = lane_of(parts[0].shape) // 32
+    out = parts[0]
+    for q in range(1, 4):
+        out = jnp.where(group == q, parts[q], out)
+    return out
 
 
 def fields_body(chunk_ref, bg_ref, lon_ref, lat_ref, fields_ref):
@@ -99,46 +101,46 @@
         fields_ref[index] = jnp.where(wide < 64, mid, pltpu.roll(mid, 64, axis=1))
 
 
-def edges_body(x_ref, fields_ref, low_ref, high_ref):
+def edges_body(even_ref, x_ref, fields_ref, near_ref, far_ref):
+    even = even_ref[0] == 1
+
+    def put(at, count, low, high):
+        near_ref[at : at + count] = jnp.where(even, high, low)
+        far_ref[at : at + count] = jnp.where(even, low, high)
+
     for u in range(MEMBERS // 4):
         for row, count in ((0, 4), (4, 8)):
-            lane = lane_of((count, LANES))
-            low, high = None, None
+            lows, highs = [], []
             for i in range(4):
                 at = 12 * (4 * u + i) + row
                 piece = x_ref[at : at + count]
-                first = pltpu.roll(piece, 32 * i, axis=1) if i else piece
-                last = pltpu.roll(piece, (32 * i + 32) % LANES, axis=1) if i < 3 else piece
-                low = first if i == 0 else jnp.where(lane >= 32 * i, first, low)
-                high = last if i == 0 else jnp.where(lane >= 32 * i, last, high)
-            at = 12 * u + row
-            low_ref[at : at + count] = low
-            high_ref[at : at + count] = high
+                lows.append(pltpu.roll(piece, 32 * i, axis=1) if i else piece)
+                highs.append(pltpu.roll(piece, 32 * i + 32, axis=1) if i < 3 else piece)
+            if row == 0:
+                lows, highs = lows[3:] + lows[:3], highs[3:] + highs[:3]
+            put(12 * u + row, count, in_groups(lows), in_groups(highs))
     for index in range(3):
         at = EDGE - 3 * HALO + HALO * index
-        low_ref[at : at + HALO] = fields_ref[index, 0:HALO]
-        high_ref[at : at + HALO] = fields_ref[index, CY - HALO : CY]
-
-
-def halves(ref, first, second):
-    parts = []
-    for at in (first, second):
+        put(at, HALO, fields_ref[index, 0:HALO], fields_ref[index, CY - HALO : CY])
+
+
+def unpacked(ref, first, second):
+    lane = lane_of((8, LANES))
+    place = lane % 64
+    mains, rests = [], []
+    for at, turn in ((first, 0), (second, 64)):
         rest = ref[pl.ds(at, 4)]
         rest = jnp.concatenate([rest, pltpu.roll(rest, LANES - 16, axis=1)], axis=0)
-        parts.append((ref[pl.ds(at + 4, 8)], rest))
-    return parts
-
-
-def unpacked(parts, q):
-    lane = lane_of((8, LANES))
-    place = lane % 64
-    out = None
-    for half, (main, rest) in enumerate(parts):
-        moved = pltpu.roll(main, (64 * half - 32 * q) % LANES, axis=1)
-        tail = pltpu.roll(rest, (64 * half + 32 - 32 * q) % LANES, axis=1)
-        moved = jnp.where(place < 32, moved, tail)
-        out = moved if out is None else jnp.where(lane < 64, out, moved)
-    return jnp.where(place < CHUNK + 2 * HALO, out, 0.0)
+        main = ref[pl.ds(at + 4, 8)]
+        mains.append(pltpu.roll(main, turn, axis=1) if turn else main)
+        rests.append(pltpu.roll(rest, turn, axis=1) if turn else rest)
+    sources = [mains[0], rests[0], mains[1], rests[1]]
+    out = []
+    for q in range(4):
+        whole = in_groups([sources[(group - q) % 4] for group in range(4)])
+        whole = pltpu.roll(whole, LANES - 32 * q, axis=1) if q else whole
+        out.append(jnp.where(place < CHUNK + 2 * HALO, whole, 0.0))
+    return out
 
 
 def advance(state, south, north, coefs, at):
@@ -155,26 +157,29 @@
     fill_coefs(fields_ref[1], fields_ref[2], coefs)
     total_ref[...] = jnp.zeros((CY - 2 * HALO, LANES), jnp.float32)
 
+    edge = jnp.zeros((HALO, LANES), jnp.float32)
+
     def one(index, carry):
         pairs = [index * GROUP + p for p in range(GROUP)]
         for p in pairs:
-            parts = halves(x_ref, 12 * p, 12 * (p + PAIRS))
-            for q in range(4):
+            for step in range(NSTEP):
+                steps_ref[step, p, 0:HALO] = edge
+                steps_ref[step, p, HALO + CY : ROWS] = edge
+            for q, out in enumerate(unpacked(x_ref, 12 * p, 12 * (p + PAIRS))):
                 rows = slice(8 * q, 8 * q + 8)
-                out = unpacked(parts, q)
                 mid_ref[p, rows] = out
-                steps_ref[0, p, rows] = fields_ref[0, rows] + 0.5 * out
+                steps_ref[0, p, HALO + 8 * q : HALO + 8 * q + 8] = fields_ref[0, rows] + 0.5 * out
         for step in range(NSTEP):
             for q in range(4) if step < NSTEP - 1 else (1, 2):
                 at = 8 * q
                 for p in pairs:
                     now = steps_ref.at[step, p]
-                    state = now[at : at + 8]
-                    south = now[at - 1 : at + 7] if q else pltpu.roll(state, 1, axis=0)
-                    north = now[at + 1 : at + 9] if q < 3 else pltpu.roll(state, 7, axis=0)
-                    state = advance(state, south, north, coefs, at)
+                    put = HALO + at
+                    state = advance(
+                        now[put : put + 8], now[put - 1 : put + 7], now[put + 1 : put + 9], coefs, at
+                    )
                     if step < NSTEP - 1:
-                        steps_ref[step + 1, p, at : at + 8] = state
+                        steps_ref[step + 1, p, put : put + 8] = state
                     else:
                         seen = state + 0.25 * state * state
                         seen_ref[p, at - 8 : at] = seen
@@ -243,9 +248,9 @@
     for step in range(NSTEP):
         for edge in range(2):
             inside, put, at, low = (
-                (step, step + 8, step + 1, step + 1)
+                (HALO + step, step + 8, step + 1, step + 1)
                 if edge == 0
-                else (CY - 8 - step, 8 - step, 15 - step, 39 - step)
+                else (CY - step, 8 - step, 15 - step, 39 - step)
             )
             for p in range(PAIRS):
                 now = buf_ref.at[edge, p]
@@ -338,9 +343,13 @@
 
 
 def first_body(
-    low_ref, high_ref, fields_ref, steps_ref, seen_ref, total_ref, cells_ref,
-    gram_ref, south_ref, north_ref, full_ref, buf_ref, sum_ref, obs_ref, *scratch
+    even_ref, far_ref, near_ref, fields_ref, steps_ref, seen_ref, total_ref, cells_ref,
+    gram_ref, south_ref, north_ref, full_ref, low_ref, high_ref, buf_ref, sum_ref, obs_ref, *scratch
 ):
+    even = even_ref[0] == 1
+    near, far = near_ref[...], far_ref[...]
+    low_ref[...] = jnp.where(even, far, near)
+    high_ref[...] = jnp.where(even, near, far)
     coefs, rest = scratch[:5], scratch[5:]
     for index in range(3):
         at = EDGE - 3 * HALO + HALO * index
@@ -356,9 +365,8 @@
 
     for ref, out_ref in ((low_ref, south_ref), (high_ref, north_ref)):
         for u in range(PAIRS // 4):
-            parts = halves(ref, 12 * u, 12 * (u + PAIRS // 4))
-            for i in range(4):
-                out_ref[4 * u + i] = unpacked(parts, i)
+            for i, rows in enumerate(unpacked(ref, 12 * u, 12 * (u + PAIRS // 4))):
+                out_ref[4 * u + i] = rows
     edge_transport(base, south_ref, north_ref, coefs, steps_ref, buf_ref, use)
 
     def rows_of(p):
@@ -495,18 +503,17 @@
         chunk, background, courant_lon, courant_lat
     )
     pieces, fields, cells = lax.optimization_barrier((pieces, fields, cells))
-    low_edge, high_edge = call(
-        edges_body, (f32(EDGE, LANES), f32(EDGE, LANES)), in_specs=[VMEM] * 2
-    )(pieces, fields)
-    forward = [(i, i + 1) for i in range(7)]
-    backward = [(i + 1, i) for i in range(7)]
-    low = lax.ppermute(high_edge, TILE, forward)
-    high = lax.ppermute(low_edge, TILE, backward)
+    even = (1 - lax.axis_index("x") % 2).astype(jnp.int32).reshape(1)
+    near_edge, far_edge = call(
+        edges_body, (f32(EDGE, LANES), f32(EDGE, LANES)), in_specs=[SMEM] + [VMEM] * 2
+    )(even, pieces, fields)
+    far = lax.ppermute(far_edge, TILE, [(t, t + 1 if t % 2 else t - 1) for t in range(1, 7)])
+    near = lax.ppermute(near_edge, TILE, [(t, t - 1 if t % 2 else t + 1) for t in range(8)])
     mid, steps, seen, total = call(
         inside_body,
         (
             f32(PAIRS, CY, LANES),
-            f32(NSTEP, PAIRS, CY, LANES),
+            f32(NSTEP, PAIRS, ROWS, LANES),
             f32(PAIRS, CY - 2 * HALO, LANES),
             f32(CY - 2 * HALO, LANES),
         ),
@@ -525,9 +532,13 @@
     gram, south, north, full = call(
         first_body,
         (f32(PACKED, LANES), *[f32(PAIRS, HALO, LANES)] * 2, f32(3, ROWS, LANES)),
-        [pltpu.VMEM((2, PAIRS, 3 * HALO, LANES), jnp.float32), *rest],
-        in_specs=[VMEM] * 7,
-    )(low, high, fields, steps, seen, total, cells)
+        [
+            *[pltpu.VMEM((EDGE, LANES), jnp.float32)] * 2,
+            pltpu.VMEM((2, PAIRS, 3 * HALO, LANES), jnp.float32),
+            *rest,
+        ],
+        in_specs=[SMEM] + [VMEM] * 7,
+    )(even, far, near, fields, steps, seen, total, cells)
     gram, weights = call(
         second_body,
         (f32(PACKED, LANES), f32(MEMBERS, LANES)),

time: 163 us -> 158 us (0.969)
  blocking collectives: 89.2 us -> 85.8 us
  Pallas kernels: 21.5 us -> 18.8 us
  starting transfers between devices: 22.6 us -> 24.4 us
    all_to_all x5, blocking collectives: 77.8 us -> 74.4 us  [exchange(): return lax.all_to_all(array, axes, 0, 0, tiled=True)]
    ppermute x2, starting transfers between devices: 4.41 us -> 6.24 us  [the longest x1 5.57 us: local(): lax.ppermute(near_edge, TILE, [(t, t - 1 if t % 2 else t + 1) for t in ra...]
  transfers between devices with their start and end apart: 3 -> 3, of which waited for: 1 -> 1; matrix products, arithmetic and copies ran while one was open for 0% -> 0% of each run, Pallas kernels for 3% -> 2%
where the time goes in v6:
time: 158 us
  blocking collectives  85.8 us (54%)
  starting transfers between devices  24.4 us (15%)
  waiting for transfers between devices  21.3 us (13%)
  Pallas kernels  18.8 us (12%)
  local copies, waits for them, and re-layouts  6.86 us (4%)
    all_to_all x5, blocking collectives, exchange(): return lax.all_to_all(array, axes, 0, 0, tiled=True)  74.4 us
    all_to_all x1, waiting for transfers between devices, exchange(): return lax.all_to_all(array, axes, 0, 0, tiled=True)  21.3 us
    all_to_all x1, starting transfers between devices, exchange(): return lax.all_to_all(array, axes, 0, 0, tiled=True)  18.2 us
    all_gather x3, blocking collectives, both_cores(): return lax.all_gather(array, 'core')  11.4 us
    pallas_call x1, Pallas kernels, local(): call(second_body, (f32(PACKED, LANES), f32(MEMBERS, LANES)), [pair, pltpu...  7.02 us
    unnamed x16, local copies, waits for them, and re-layouts  6.66 us
    ppermute x1, starting transfers between devices, local(): lax.ppermute(near_edge, TILE, [(t, t - 1 if t % 2 else t + 1) for t in ra...  5.57 us
  transfers between devices with their start and end apart: 3, of which 1 were waited for; matrix products, arithmetic and copies ran while one was open for 0% of the time, Pallas kernels for 2%

profile of v6, /device:TPU:1, one launch (start us, length us, event | category | flops | bytes accessed | tf_op | source)
XLA Modules:
  0.0 157.5 jit_solution(17298852812079616728)
XLA Ops:
  0.0 0.9 copy-done.3
  1.0 1.6 %shard_map.82 = f32[768,128]{1,0:T(8,128)} custom-call(f32[2,32,1024]{2,1,0:T(8,128)S(1)} %bitcast.15), custom_call_target="tpu_custom_call" | custom-call | tf_op jit(solution)/shard_map/pallas_call | solution.py:497
  2.6 18.2 %all-to-all-start = ((f32[64,3,4,128]{3,2,1,0:T(4,128)}), f32[64,3,4,128]{3,2,1,0:T(4,128)S(1)}, u32[]{:S(2)}, u32[]{:S(2)}) async-start(f32[64,3,4,128]{3,2,1,0:T(4,128)} %bitcast.2), calls=%async_computation | async-start | bytes 786432 | tf_op jit(solution)/shard_map/all_to_all | solution.py:474
  20.8 0.9 copy-done
  21.7 0.9 copy-done.1
  22.7 0.9 copy-done.2
  24.5 0.7 copy-done.5
  25.2 0.7 copy-done.6
  25.9 0.7 copy-done.7
  27.3 21.3 %all-to-all-done = f32[64,3,4,128]{3,2,1,0:T(4,128)S(1)} async-done(((f32[64,3,4,128]{3,2,1,0:T(4,128)}), f32[64,3,4,128]{3,2,1,0:T(4,128)S(1)}, u32[]{:S(2)}, u32[]{:S(2)}) %all-to-all-start) | async-done | bytes 393248 | tf_op jit(solution)/shard_map/all_to_all | solution.py:474
  49.6 5.6 %collective-permute-start.1 = (f32[216,128]{1,0:T(8,128)S(1)}, f32[216,128]{1,0:T(8,128)S(1)}, u32[]{:S(2)}, u32[]{:S(2)}) collective-permute-start(f32[216,128]{1,0:T(8,128)S(1)} %get-tuple-element.23), channel_id=1, source_target_pairs={{0,1},{1,0},{2,3},{3,2},{4,5},{5,4},{6,7},{7,6},{8,9},{9,8},{10,11... | collective-permute-start | bytes 331784 | tf_op jit(solution)/shard_map/ppermute | solution.py:511
  55.2 2.8 %shard_map.86 = (f32[32,32,128]{2,1,0:T(8,128)S(1)}, f32[8,32,48,128]{3,2,1,0:T(8,128)S(1)}, f32[32,16,128]{2,1,0:T(8,128)S(1)}, f32[16,128]{1,0:T(8,128)S(1)}) custom-call(f32[768,128]{1,0:T(8,128)S(1)} %bitcast.13, f32[3,32,128]{2,1,0:T(8,128)S(1)} %shard_map.83.fields_ref), custom_call_target="tpu_custom_call" | custom-call | tf_op jit(solution)/shard_map/pallas_call | solution.py:512
  58.0 2.8 %shard_map.87 = (f32[20,128]{1,0:T(8,128)S(1)}, f32[32,8,128]{2,1,0:T(8,128)S(1)}, f32[32,8,128]{2,1,0:T(8,128)S(1)}, f32[3,48,128]{2,1,0:T(8,128)S(1)}) custom-call(s32[1]{0:T(128)} %bitcast.even_ref, f32[216,128]{1,0:T(8,128)S(1)} %collective-permute-done.far_ref, f32[216,128]{1,0:T(8,128)S(1)} %collective-permute-done.1.near_ref, ...), custom_call_target="tpu_custom_call" | custom-call | tf_op jit(solution)/shard_map/pallas_call | solution.py:532
  60.9 15.6 %all_to_all.30 = f32[32,5,2,128]{3,2,1,0:T(2,128)S(1)} all-to-all(f32[32,5,2,128]{3,2,1,0:T(2,128)S(1)} %bitcast.20), channel_id=1, replica_groups=mesh['z'=16,'yl'=2,'core'=2,'yh'=2,'x'=4] {'yl','core','yh','x'}, dimensions={0} | all-to-all | bytes 327680 | tf_op jit(solution)/shard_map/all_to_all | solution.py:474
  76.6 14.3 %all_to_all.31 = f32[16,5,2,128]{3,2,1,0:T(2,128)S(1)} all-to-all(f32[16,5,2,128]{3,2,1,0:T(2,128)S(1)} %broadcast_in_dim.16), channel_id=1, replica_groups=mesh['z'=16,'yl'=2,'core'=2,'yh'=2,'x'=4] {'z'}, dimensions={0} | all-to-all | bytes 163840 | tf_op jit(solution)/shard_map/all_to_all | solution.py:474
  90.9 3.8 %all_gather.12.sums_ref = f32[2,10,128]{2,1,0:T(8,128)S(1)} all-gather(f32[1,10,128]{2,1,0:T(8,128)S(1)} %all_gather_reshape.6), channel_id=1, replica_groups=mesh['z'=16,'yl'=2,'core'=2,'yh'=2,'x'=4] {'core'}, dimensions={0}, use_global_device_ids=true | all-gather | bytes 15360 | tf_op jit(solution)/shard_map/all_gather | solution.py:482
  94.7 7.0 %shard_map.88 = (f32[20,128]{1,0:T(8,128)S(1)}, f32[64,128]{1,0:T(8,128)S(1)}) custom-call(f32[2,10,128]{2,1,0:T(8,128)S(1)} %all_gather.12.sums_ref, f32[32,8,128]{2,1,0:T(8,128)S(1)} %get-tuple-element.29.south_ref, f32[32,32,128]{2,1,0:T(8,128)S(1)} %get-tuple-element.30.mid_ref, f32[32,8,128]{2,1,0:T(8,128)S(1)} %get-tuple-element.31.north_ref, ...), custom_call_target="tpu_custom_call" | custom-call | tf_op jit(solution)/shard_map/pallas_call | solution.py:542
  101.8 11.5 %all_to_all.32 = f32[32,5,2,128]{3,2,1,0:T(2,128)S(1)} all-to-all(f32[32,5,2,128]{3,2,1,0:T(2,128)S(1)} %bitcast.21), channel_id=1, replica_groups=mesh['z'=16,'yl'=2,'core'=2,'yh'=2,'x'=4] {'yl','core','yh','x'}, dimensions={0} | all-to-all | bytes 327680 | tf_op jit(solution)/shard_map/all_to_all | solution.py:474
  113.5 14.8 %all_to_all.33 = f32[16,5,2,128]{3,2,1,0:T(2,128)S(1)} all-to-all(f32[16,5,2,128]{3,2,1,0:T(2,128)S(1)} %broadcast_in_dim.37), channel_id=1, replica_groups=mesh['z'=16,'yl'=2,'core'=2,'yh'=2,'x'=4] {'z'}, dimensions={0} | all-to-all | bytes 163840 | tf_op jit(solution)/shard_map/all_to_all | solution.py:474
  128.3 3.8 %all_gather.13.sums_ref = f32[2,10,128]{2,1,0:T(8,128)S(1)} all-gather(f32[1,10,128]{2,1,0:T(8,128)S(1)} %all_gather_reshape.7), channel_id=1, replica_groups=mesh['z'=16,'yl'=2,'core'=2,'yh'=2,'x'=4] {'core'}, dimensions={0}, use_global_device_ids=true | all-gather | bytes 15360 | tf_op jit(solution)/shard_map/all_gather | solution.py:482
  132.0 2.5 %shard_map.89 = f32[8,128]{1,0:T(8,128)S(1)} custom-call(f32[2,10,128]{2,1,0:T(8,128)S(1)} %all_gather.13.sums_ref, f32[64,128]{1,0:T(8,128)S(1)} %get-tuple-element.34.weights_ref, f32[32,32,128]{2,1,0:T(8,128)S(1)} %get-tuple-element.30.mid_ref), custom_call_target="tpu_custom_call" | custom-call | tf_op jit(solution)/shard_map/pallas_call | solution.py:548
  134.6 18.2 %all_to_all.34 = f32[32,8,128]{2,1,0:T(8,128)S(1)} all-to-all(f32[32,8,128]{2,1,0:T(8,128)S(1)} %broadcast_in_dim.38), channel_id=1, replica_groups=mesh['z'=16,'yl'=2,'core'=2,'yh'=2,'x'=4] {'z','yl'}, dimensions={0} | all-to-all | bytes 262144 | tf_op jit(solution)/shard_map/all_to_all | solution.py:474
  152.8 3.8 %all-gather = f32[64,8,128]{2,1,0:T(8,128)S(1)} all-gather(f32[32,8,128]{2,1,0:T(8,128)S(1)} %all_to_all.34), channel_id=2, replica_groups=mesh['z'=16,'yl'=2,'core'=2,'yh'=2,'x'=4] {'core'}, dimensions={0}, use_global_device_ids=true | all-gather | bytes 393216 | tf_op jit(solution)/shard_map/all_gather | solution.py:482
  156.6 1.0 shard_map.90
  (28 shorter events, 2.9 us)
Async XLA Ops:
  0.0 0.9 copy-start.3
  2.6 46.1 %all-to-all-start = ((f32[64,3,4,128]{3,2,1,0:T(4,128)}), f32[64,3,4,128]{3,2,1,0:T(4,128)S(1)}, u32[]{:S(2)}, u32[]{:S(2)}) async-start(f32[64,3,4,128]{3,2,1,0:T(4,128)} %bitcast.2), calls=%async_computation | async-start | bytes 786432 | tf_op jit(solution)/shard_map/all_to_all | solution.py:474
  20.8 1.0 copy-start
  21.7 0.9 copy-start.1
  22.7 0.9 copy-start.2
  23.8 0.7 copy-start.4
  24.5 0.7 copy-start.5
  25.2 0.7 copy-start.6
  25.9 0.7 copy-start.7
  48.9 9.1 %collective-permute-start = (f32[216,128]{1,0:T(8,128)S(1)}, f32[216,128]{1,0:T(8,128)S(1)}, u32[]{:S(2)}, u32[]{:S(2)}) collective-permute-start(f32[216,128]{1,0:T(8,128)S(1)} %get-tuple-element.22), channel_id=1, source_target_pairs={{1,2},{2,1},{3,4},{4,3},{5,6},{6,5},{9,10},{10,9},{11,12},{12,11},... | collective-permute-start | bytes 331784 | tf_op jit(solution)/shard_map/ppermute | solution.py:510
  49.6 8.4 %collective-permute-start.1 = (f32[216,128]{1,0:T(8,128)S(1)}, f32[216,128]{1,0:T(8,128)S(1)}, u32[]{:S(2)}, u32[]{:S(2)}) collective-permute-start(f32[216,128]{1,0:T(8,128)S(1)} %get-tuple-element.23), channel_id=1, source_target_pairs={{0,1},{1,0},{2,3},{3,2},{4,5},{5,4},{6,7},{7,6},{8,9},{9,8},{10,11... | collective-permute-start | bytes 331784 | tf_op jit(solution)/shard_map/ppermute | solution.py:511

commit v7 on v6

--- a/solution.py
+++ b/solution.py
@@ -17,10 +17,9 @@
 CHUNK = 32
 HALO = 8
 ROWS = CY + 2 * HALO
-EDGE = 12 * MEMBERS // 4 + 3 * HALO
+EDGE = 12 * MEMBERS // 4
 LANES = 128
 PACKED = 20
-HIGHEST = lax.Precision.HIGHEST
 
 MEM = ("z", "yl", "core")
 TILE = ("yh", "x")
@@ -84,8 +83,8 @@
     return out
 
 
-def fields_body(chunk_ref, bg_ref, lon_ref, lat_ref, fields_ref):
-    chunk = chunk_ref[0]
+def fields_body(chunk_ref, even_ref, bg_ref, lon_ref, lat_ref, fields_ref, near_ref, far_ref):
+    chunk, even = chunk_ref[0], even_ref[0] == 1
     lev, b, k = chunk // 32, chunk % 32 // 4, chunk % 4
     wide = lane_of((CY, LANES))
 
@@ -98,10 +97,13 @@
         mid = jnp.where((wide < HALO) & (k == 3), block(ref, (b + 1) % 8), mid)
         mid = pltpu.roll(mid, (HALO - CHUNK * k + LANES) % LANES, axis=1)
         mid = jnp.where(wide < CHUNK + 2 * HALO, mid, 0.0)
-        fields_ref[index] = jnp.where(wide < 64, mid, pltpu.roll(mid, 64, axis=1))
-
-
-def edges_body(even_ref, x_ref, fields_ref, near_ref, far_ref):
+        mid = jnp.where(wide < 64, mid, pltpu.roll(mid, 64, axis=1))
+        fields_ref[index] = mid
+        near_ref[index] = jnp.where(even, mid[CY - HALO :], mid[:HALO])
+        far_ref[index] = jnp.where(even, mid[:HALO], mid[CY - HALO :])
+
+
+def edges_body(even_ref, x_ref, near_ref, far_ref):
     even = even_ref[0] == 1
 
     def put(at, count, low, high):
@@ -119,9 +121,6 @@
             if row == 0:
                 lows, highs = lows[3:] + lows[:3], highs[3:] + highs[:3]
             put(12 * u + row, count, in_groups(lows), in_groups(highs))
-    for index in range(3):
-        at = EDGE - 3 * HALO + HALO * index
-        put(at, HALO, fields_ref[index, 0:HALO], fields_ref[index, CY - HALO : CY])
 
 
 def unpacked(ref, first, second):
@@ -294,6 +293,17 @@
     lax.fori_loop(0, PAIRS // GROUP, one, 0)
 
 
+def split(value):
+    high = value.astype(jnp.bfloat16)
+    return high, (value - high.astype(jnp.float32)).astype(jnp.bfloat16)
+
+
+def by_rows(left, right):
+    return lax.dot_general(
+        left, right, (((1,), (1,)), ((), ())), preferred_element_type=jnp.float32
+    )
+
+
 def normal_terms(rows_of, total, cells_ref, gram_ref, dev_ref, left_ref, right_ref):
     center = (total + pltpu.roll(total, 64, axis=1)) * (1.0 / MEMBERS)
     for p in range(PAIRS):
@@ -310,13 +320,9 @@
         left_ref[:, LANES * r : LANES * r + LANES] = rows
         right_ref[0:MEMBERS, LANES * r : LANES * r + LANES] = rows * weight[r : r + 1]
         right_ref[MEMBERS : MEMBERS + 1, LANES * r : LANES * r + LANES] = aim[r : r + 1]
-    gram = lax.dot_general(
-        left_ref[...],
-        right_ref[...],
-        (((1,), (1,)), ((), ())),
-        precision=HIGHEST,
-        preferred_element_type=jnp.float32,
-    )
+    (left_high, left_low), (right_high, right_low) = split(left_ref[...]), split(right_ref[...])
+    gram = by_rows(left_high, right_high)
+    gram = gram + (by_rows(left_high, right_low) + by_rows(left_low, right_high))
     wide = lane_of((MEMBERS, LANES))
     sub = lax.broadcasted_iota(jnp.int32, (MEMBERS, LANES), 0)
     column = jnp.broadcast_to(gram[:, MEMBERS : MEMBERS + 1], (MEMBERS, LANES))
@@ -343,7 +349,7 @@
 
 
 def first_body(
-    even_ref, far_ref, near_ref, fields_ref, steps_ref, seen_ref, total_ref, cells_ref,
+    even_ref, far_ref, near_ref, far_fields_ref, near_fields_ref, fields_ref, steps_ref, seen_ref, total_ref, cells_ref,
     gram_ref, south_ref, north_ref, full_ref, low_ref, high_ref, buf_ref, sum_ref, obs_ref, *scratch
 ):
     even = even_ref[0] == 1
@@ -351,11 +357,10 @@
     low_ref[...] = jnp.where(even, far, near)
     high_ref[...] = jnp.where(even, near, far)
     coefs, rest = scratch[:5], scratch[5:]
-    for index in range(3):
-        at = EDGE - 3 * HALO + HALO * index
-        full_ref[index, 0:HALO] = low_ref[at : at + HALO]
-        full_ref[index, HALO : HALO + CY] = fields_ref[index]
-        full_ref[index, HALO + CY : ROWS] = high_ref[at : at + HALO]
+    near, far = near_fields_ref[...], far_fields_ref[...]
+    full_ref[:, 0:HALO] = jnp.where(even, far, near)
+    full_ref[:, HALO : HALO + CY] = fields_ref[...]
+    full_ref[:, HALO + CY : ROWS] = jnp.where(even, near, far)
     fill_coefs(full_ref[1], full_ref[2], coefs)
     sum_ref[0:HALO] = jnp.zeros((HALO, LANES), jnp.float32)
     sum_ref[HALO : CY - HALO] = total_ref[...]
@@ -499,16 +504,24 @@
     nobs = obs_value.shape[0]
     flat = [a.reshape(1, nobs) for a in (obs_value, obs_weight, obs_column, obs_level)]
     cells = call(cells_body, f32(2, CY, LANES), in_specs=[SMEM] + [VMEM] * 4)(chunk, *flat)
-    fields = call(fields_body, f32(3, CY, LANES), in_specs=[SMEM] + [VMEM] * 3)(
-        chunk, background, courant_lon, courant_lat
-    )
-    pieces, fields, cells = lax.optimization_barrier((pieces, fields, cells))
     even = (1 - lax.axis_index("x") % 2).astype(jnp.int32).reshape(1)
+    to_far = [(t, t + 1 if t % 2 else t - 1) for t in range(1, 7)]
+    to_near = [(t, t - 1 if t % 2 else t + 1) for t in range(8)]
+    fields, near_fields, far_fields = call(
+        fields_body,
+        (f32(3, CY, LANES), f32(3, HALO, LANES), f32(3, HALO, LANES)),
+        in_specs=[SMEM] * 2 + [VMEM] * 3,
+    )(chunk, even, background, courant_lon, courant_lat)
+    far_fields = lax.ppermute(far_fields, TILE, to_far)
+    near_fields = lax.ppermute(near_fields, TILE, to_near)
+    pieces, fields, cells, far_fields, near_fields = lax.optimization_barrier(
+        (pieces, fields, cells, far_fields, near_fields)
+    )
     near_edge, far_edge = call(
-        edges_body, (f32(EDGE, LANES), f32(EDGE, LANES)), in_specs=[SMEM] + [VMEM] * 2
-    )(even, pieces, fields)
-    far = lax.ppermute(far_edge, TILE, [(t, t + 1 if t % 2 else t - 1) for t in range(1, 7)])
-    near = lax.ppermute(near_edge, TILE, [(t, t - 1 if t % 2 else t + 1) for t in range(8)])
+        edges_body, (f32(EDGE, LANES), f32(EDGE, LANES)), in_specs=[SMEM, VMEM]
+    )(even, pieces)
+    far = lax.ppermute(far_edge, TILE, to_far)
+    near = lax.ppermute(near_edge, TILE, to_near)
     mid, steps, seen, total = call(
         inside_body,
         (
@@ -537,8 +550,8 @@
             pltpu.VMEM((2, PAIRS, 3 * HALO, LANES), jnp.float32),
             *rest,
         ],
-        in_specs=[SMEM] + [VMEM] * 7,
-    )(even, far, near, fields, steps, seen, total, cells)
+        in_specs=[SMEM] + [VMEM] * 9,
+    )(even, far, near, far_fields, near_fields, fields, steps, seen, total, cells)
     gram, weights = call(
         second_body,
         (f32(PACKED, LANES), f32(MEMBERS, LANES)),

time: 158 us -> 158 us (level)
  starting transfers between devices: 24.4 us -> 30.6 us
  waiting for transfers between devices: 21.3 us -> 15.1 us
    all_to_all x1, waiting for transfers between devices: 21.3 us -> 15 us  [exchange(): return lax.all_to_all(array, axes, 0, 0, tiled=True)]
    ppermute x2 -> x4, starting transfers between devices: 6.24 us -> 12.5 us  [the longest x1 5.58 us: local(): near_fields = lax.ppermute(near_fields, TILE, to_near)]
  transfers between devices with their start and end apart: 3 -> 5, of which waited for: 1 -> 1; matrix products, arithmetic and copies ran while one was open for 0% -> 0% of each run, Pallas kernels for 2% -> 2%
where the time goes in v7:
time: 158 us; the launch traced here: 157 us
  blocking collectives  85.6 us (54%)
  starting transfers between devices  30.6 us (19%)
  Pallas kernels  18.3 us (12%)
  waiting for transfers between devices  15.1 us (10%)
  local copies, waits for them, and re-layouts  6.86 us (4%)
    all_to_all x5, blocking collectives, exchange(): return lax.all_to_all(array, axes, 0, 0, tiled=True)  74.3 us
    all_to_all x1, starting transfers between devices, exchange(): return lax.all_to_all(array, axes, 0, 0, tiled=True)  18.2 us
    all_to_all x1, waiting for transfers between devices, exchange(): return lax.all_to_all(array, axes, 0, 0, tiled=True)  15 us
    all_gather x3, blocking collectives, both_cores(): return lax.all_gather(array, 'core')  11.4 us
    pallas_call x1, Pallas kernels, local(): call(second_body, (f32(PACKED, LANES), f32(MEMBERS, LANES)), [pair, pltpu...  6.76 us
    unnamed x16, local copies, waits for them, and re-layouts  6.66 us
    ppermute x1, starting transfers between devices, local(): near_fields = lax.ppermute(near_fields, TILE, to_near)  5.58 us
    ppermute x1, starting transfers between devices, local(): near = lax.ppermute(near_edge, TILE, to_near)  5.57 us
  transfers between devices with their start and end apart: 5, of which 1 were waited for; matrix products, arithmetic and copies ran while one was open for 0% of the time, Pallas kernels for 2%

profile of v7, /device:TPU:1, one launch (start us, length us, event | category | flops | bytes accessed | tf_op | source)
XLA Modules:
  0.0 156.9 jit_solution(2632574890682291792)
XLA Ops:
  0.0 0.9 copy-done
  1.0 1.6 %shard_map.82 = f32[768,128]{1,0:T(8,128)} custom-call(f32[2,32,1024]{2,1,0:T(8,128)S(1)} %bitcast.15), custom_call_target="tpu_custom_call" | custom-call | tf_op jit(solution)/shard_map/pallas_call | solution.py:502
  2.6 18.2 %all-to-all-start = ((f32[64,3,4,128]{3,2,1,0:T(4,128)}), f32[64,3,4,128]{3,2,1,0:T(4,128)S(1)}, u32[]{:S(2)}, u32[]{:S(2)}) async-start(f32[64,3,4,128]{3,2,1,0:T(4,128)} %bitcast.2), calls=%async_computation | async-start | bytes 786432 | tf_op jit(solution)/shard_map/all_to_all | solution.py:479
  20.8 0.9 copy-done.1
  21.7 0.9 copy-done.2
  22.7 0.9 copy-done.3
  24.4 5.6 %collective-permute-start.1 = (f32[3,8,128]{2,1,0:T(8,128)S(1)}, f32[3,8,128]{2,1,0:T(8,128)S(1)}, u32[]{:S(2)}, u32[]{:S(2)}) collective-permute-start(f32[3,8,128]{2,1,0:T(8,128)S(1)} %get-tuple-element.27), channel_id=1, source_target_pairs={{0,1},{1,0},{2,3},{3,2},{4,5},{5,4},{6,7},{7,6},{8,9},{9,8},{10,11... | collective-permute-start | bytes 36872 | tf_op jit(solution)/shard_map/ppermute | solution.py:516
  30.7 0.7 copy-done.5
  32.2 0.7 copy-done.7
  33.6 15.0 %all-to-all-done = f32[64,3,4,128]{3,2,1,0:T(4,128)S(1)} async-done(((f32[64,3,4,128]{3,2,1,0:T(4,128)}), f32[64,3,4,128]{3,2,1,0:T(4,128)S(1)}, u32[]{:S(2)}, u32[]{:S(2)}) %all-to-all-start) | async-done | bytes 393248 | tf_op jit(solution)/shard_map/all_to_all | solution.py:479
  49.6 5.6 %collective-permute-start.3 = (f32[192,128]{1,0:T(8,128)S(1)}, f32[192,128]{1,0:T(8,128)S(1)}, u32[]{:S(2)}, u32[]{:S(2)}) collective-permute-start(f32[192,128]{1,0:T(8,128)S(1)} %get-tuple-element.30), channel_id=1, source_target_pairs={{0,1},{1,0},{2,3},{3,2},{4,5},{5,4},{6,7},{7,6},{8,9},{9,8},{10,11... | collective-permute-start | bytes 294920 | tf_op jit(solution)/shard_map/ppermute | solution.py:524
  55.2 2.8 %shard_map.86 = (f32[32,32,128]{2,1,0:T(8,128)S(1)}, f32[8,32,48,128]{3,2,1,0:T(8,128)S(1)}, f32[32,16,128]{2,1,0:T(8,128)S(1)}, f32[16,128]{1,0:T(8,128)S(1)}) custom-call(f32[768,128]{1,0:T(8,128)S(1)} %bitcast.13, f32[3,32,128]{2,1,0:T(8,128)S(1)} %get-tuple-element.33.fields_ref), custom_call_target="tpu_custom_call" | custom-call | tf_op jit(solution)/shard_map/pallas_call | solution.py:525
  58.0 2.5 %shard_map.87 = (f32[20,128]{1,0:T(8,128)S(1)}, f32[32,8,128]{2,1,0:T(8,128)S(1)}, f32[32,8,128]{2,1,0:T(8,128)S(1)}, f32[3,48,128]{2,1,0:T(8,128)S(1)}) custom-call(s32[1]{0:T(128)} %bitcast.even_ref, f32[192,128]{1,0:T(8,128)S(1)} %collective-permute-done.2.far_ref, f32[192,128]{1,0:T(8,128)S(1)} %collective-permute-done.3.near_ref, ...), custom_call_target="tpu_custom_call" | custom-call | tf_op jit(solution)/shard_map/pallas_call | solution.py:545
  60.6 15.5 %all_to_all.30 = f32[32,5,2,128]{3,2,1,0:T(2,128)S(1)} all-to-all(f32[32,5,2,128]{3,2,1,0:T(2,128)S(1)} %bitcast.20), channel_id=1, replica_groups=mesh['z'=16,'yl'=2,'core'=2,'yh'=2,'x'=4] {'yl','core','yh','x'}, dimensions={0} | all-to-all | bytes 327680 | tf_op jit(solution)/shard_map/all_to_all | solution.py:479
  76.2 14.3 %all_to_all.31 = f32[16,5,2,128]{3,2,1,0:T(2,128)S(1)} all-to-all(f32[16,5,2,128]{3,2,1,0:T(2,128)S(1)} %broadcast_in_dim.16), channel_id=1, replica_groups=mesh['z'=16,'yl'=2,'core'=2,'yh'=2,'x'=4] {'z'}, dimensions={0} | all-to-all | bytes 163840 | tf_op jit(solution)/shard_map/all_to_all | solution.py:479
  90.5 3.8 %all_gather.12.sums_ref = f32[2,10,128]{2,1,0:T(8,128)S(1)} all-gather(f32[1,10,128]{2,1,0:T(8,128)S(1)} %all_gather_reshape.6), channel_id=1, replica_groups=mesh['z'=16,'yl'=2,'core'=2,'yh'=2,'x'=4] {'core'}, dimensions={0}, use_global_device_ids=true | all-gather | bytes 15360 | tf_op jit(solution)/shard_map/all_gather | solution.py:487
  94.3 6.8 %shard_map.88 = (f32[20,128]{1,0:T(8,128)S(1)}, f32[64,128]{1,0:T(8,128)S(1)}) custom-call(f32[2,10,128]{2,1,0:T(8,128)S(1)} %all_gather.12.sums_ref, f32[32,8,128]{2,1,0:T(8,128)S(1)} %get-tuple-element.39.south_ref, f32[32,32,128]{2,1,0:T(8,128)S(1)} %get-tuple-element.40.mid_ref, f32[32,8,128]{2,1,0:T(8,128)S(1)} %get-tuple-element.41.north_ref, ...), custom_call_target="tpu_custom_call" | custom-call | tf_op jit(solution)/shard_map/pallas_call | solution.py:555
  101.1 11.5 %all_to_all.32 = f32[32,5,2,128]{3,2,1,0:T(2,128)S(1)} all-to-all(f32[32,5,2,128]{3,2,1,0:T(2,128)S(1)} %bitcast.21), channel_id=1, replica_groups=mesh['z'=16,'yl'=2,'core'=2,'yh'=2,'x'=4] {'yl','core','yh','x'}, dimensions={0} | all-to-all | bytes 327680 | tf_op jit(solution)/shard_map/all_to_all | solution.py:479
  112.8 14.8 %all_to_all.33 = f32[16,5,2,128]{3,2,1,0:T(2,128)S(1)} all-to-all(f32[16,5,2,128]{3,2,1,0:T(2,128)S(1)} %broadcast_in_dim.37), channel_id=1, replica_groups=mesh['z'=16,'yl'=2,'core'=2,'yh'=2,'x'=4] {'z'}, dimensions={0} | all-to-all | bytes 163840 | tf_op jit(solution)/shard_map/all_to_all | solution.py:479
  127.6 3.8 %all_gather.13.sums_ref = f32[2,10,128]{2,1,0:T(8,128)S(1)} all-gather(f32[1,10,128]{2,1,0:T(8,128)S(1)} %all_gather_reshape.7), channel_id=1, replica_groups=mesh['z'=16,'yl'=2,'core'=2,'yh'=2,'x'=4] {'core'}, dimensions={0}, use_global_device_ids=true | all-gather | bytes 15360 | tf_op jit(solution)/shard_map/all_gather | solution.py:487
  131.4 2.5 %shard_map.89 = f32[8,128]{1,0:T(8,128)S(1)} custom-call(f32[2,10,128]{2,1,0:T(8,128)S(1)} %all_gather.13.sums_ref, f32[64,128]{1,0:T(8,128)S(1)} %get-tuple-element.44.weights_ref, f32[32,32,128]{2,1,0:T(8,128)S(1)} %get-tuple-element.40.mid_ref), custom_call_target="tpu_custom_call" | custom-call | tf_op jit(solution)/shard_map/pallas_call | solution.py:561
  133.9 18.2 %all_to_all.34 = f32[32,8,128]{2,1,0:T(8,128)S(1)} all-to-all(f32[32,8,128]{2,1,0:T(8,128)S(1)} %broadcast_in_dim.38), channel_id=1, replica_groups=mesh['z'=16,'yl'=2,'core'=2,'yh'=2,'x'=4] {'z','yl'}, dimensions={0} | all-to-all | bytes 262144 | tf_op jit(solution)/shard_map/all_to_all | solution.py:479
  152.1 3.8 %all-gather = f32[64,8,128]{2,1,0:T(8,128)S(1)} all-gather(f32[32,8,128]{2,1,0:T(8,128)S(1)} %all_to_all.34), channel_id=2, replica_groups=mesh['z'=16,'yl'=2,'core'=2,'yh'=2,'x'=4] {'core'}, dimensions={0}, use_global_device_ids=true | all-gather | bytes 393216 | tf_op jit(solution)/shard_map/all_gather | solution.py:487
  155.9 1.0 shard_map.90
  (32 shorter events, 4.3 us)
Async XLA Ops:
  0.0 0.9 copy-start
  2.6 46.1 %all-to-all-start = ((f32[64,3,4,128]{3,2,1,0:T(4,128)}), f32[64,3,4,128]{3,2,1,0:T(4,128)S(1)}, u32[]{:S(2)}, u32[]{:S(2)}) async-start(f32[64,3,4,128]{3,2,1,0:T(4,128)} %bitcast.2), calls=%async_computation | async-start | bytes 786432 | tf_op jit(solution)/shard_map/all_to_all | solution.py:479
  20.8 1.0 copy-start.1
  21.7 0.9 copy-start.2
  22.7 0.9 copy-start.3
  23.8 9.8 %collective-permute-start = (f32[3,8,128]{2,1,0:T(8,128)S(1)}, f32[3,8,128]{2,1,0:T(8,128)S(1)}, u32[]{:S(2)}, u32[]{:S(2)}) collective-permute-start(f32[3,8,128]{2,1,0:T(8,128)S(1)} %get-tuple-element.26), channel_id=1, source_target_pairs={{1,2},{2,1},{3,4},{4,3},{5,6},{6,5},{9,10},{10,9},{11,12},{12,11},... | collective-permute-start | bytes 36872 | tf_op jit(solution)/shard_map/ppermute | solution.py:515
  24.4 9.1 %collective-permute-start.1 = (f32[3,8,128]{2,1,0:T(8,128)S(1)}, f32[3,8,128]{2,1,0:T(8,128)S(1)}, u32[]{:S(2)}, u32[]{:S(2)}) collective-permute-start(f32[3,8,128]{2,1,0:T(8,128)S(1)} %get-tuple-element.27), channel_id=1, source_target_pairs={{0,1},{1,0},{2,3},{3,2},{4,5},{5,4},{6,7},{7,6},{8,9},{9,8},{10,11... | collective-permute-start | bytes 36872 | tf_op jit(solution)/shard_map/ppermute | solution.py:516
  30.0 0.7 copy-start.4
  30.7 0.7 copy-start.5
  31.5 0.7 copy-start.6
  32.2 0.7 copy-start.7
  48.9 9.1 %collective-permute-start.2 = (f32[192,128]{1,0:T(8,128)S(1)}, f32[192,128]{1,0:T(8,128)S(1)}, u32[]{:S(2)}, u32[]{:S(2)}) collective-permute-start(f32[192,128]{1,0:T(8,128)S(1)} %get-tuple-element.29), channel_id=1, source_target_pairs={{1,2},{2,1},{3,4},{4,3},{5,6},{6,5},{9,10},{10,9},{11,12},{12,11},... | collective-permute-start | bytes 294920 | tf_op jit(solution)/shard_map/ppermute | solution.py:523
  49.6 8.4 %collective-permute-start.3 = (f32[192,128]{1,0:T(8,128)S(1)}, f32[192,128]{1,0:T(8,128)S(1)}, u32[]{:S(2)}, u32[]{:S(2)}) collective-permute-start(f32[192,128]{1,0:T(8,128)S(1)} %get-tuple-element.30), channel_id=1, source_target_pairs={{0,1},{1,0},{2,3},{3,2},{4,5},{5,4},{6,7},{7,6},{8,9},{9,8},{10,11... | collective-permute-start | bytes 294920 | tf_op jit(solution)/shard_map/ppermute | solution.py:524

commit v8 on v7

--- a/solution.py
+++ b/solution.py
@@ -20,6 +20,7 @@
 EDGE = 12 * MEMBERS // 4
 LANES = 128
 PACKED = 20
+WHOLE = 24
 
 MEM = ("z", "yl", "core")
 TILE = ("yh", "x")
@@ -333,7 +334,7 @@
     square = jnp.where(lane - 32 >= sub, pltpu.roll(top, 32, axis=1), bottom)
     square = jnp.where(lane < 32, pltpu.roll(top, LANES - 32, axis=1), square)
     packed = jnp.where(lane[0:16] < 64, square[0:16], pltpu.roll(square[16:32], 64, axis=1))
-    gram_ref[...] = jnp.zeros((PACKED, LANES), jnp.float32)
+    gram_ref[...] = jnp.zeros((WHOLE, LANES), jnp.float32)
     gram_ref[0:8] = packed[0:8]
     gram_ref[8:9] = jnp.where(lane[0:1] < 64, project, pltpu.roll(diagonal, 32, axis=1))
     gram_ref[10:18] = packed[8:16]
@@ -429,8 +430,9 @@
 
 def mix(pair_ref, anoms_ref):
     total = jnp.zeros(anoms_ref.shape[1:], jnp.float32)
+    weights = pair_ref[...]
     for p in range(PAIRS):
-        total = total + pair_ref[p : p + 1] * anoms_ref[p]
+        total = total + weights[p : p + 1] * anoms_ref[p]
     return total + pltpu.roll(total, 64, axis=1)
 
 
@@ -489,10 +491,10 @@
 
 def sum_everywhere(packed):
     shape = (5, 2, LANES)
-    halves = jnp.broadcast_to(packed.reshape(1, 2, 1, *shape), (2, 2, 8, *shape))
+    halves = jnp.broadcast_to(packed[:PACKED].reshape(1, 2, 1, *shape), (2, 2, 8, *shape))
     part = jnp.sum(exchange(halves.reshape(32, *shape), PLANE), axis=0)
     part = jnp.sum(to_all(part, "z", 16), axis=0).reshape(10, LANES)
-    return both_cores(part)
+    return both_cores(jnp.pad(part, ((0, 6), (0, 0))))
 
 
 def local(
@@ -544,7 +546,7 @@
     pair = pltpu.VMEM((PAIRS, LANES), jnp.float32)
     gram, south, north, full = call(
         first_body,
-        (f32(PACKED, LANES), *[f32(PAIRS, HALO, LANES)] * 2, f32(3, ROWS, LANES)),
+        (f32(WHOLE, LANES), *[f32(PAIRS, HALO, LANES)] * 2, f32(3, ROWS, LANES)),
         [
             *[pltpu.VMEM((EDGE, LANES), jnp.float32)] * 2,
             pltpu.VMEM((2, PAIRS, 3 * HALO, LANES), jnp.float32),
@@ -554,7 +556,7 @@
     )(even, far, near, far_fields, near_fields, fields, steps, seen, total, cells)
     gram, weights = call(
         second_body,
-        (f32(PACKED, LANES), f32(MEMBERS, LANES)),
+        (f32(WHOLE, LANES), f32(MEMBERS, LANES)),
         [pair, pltpu.VMEM((2, GROUP, ROWS + 2 * HALO, LANES), jnp.float32), *rest],
         in_specs=[VMEM] * 6,
     )(sum_everywhere(gram), south, mid, north, full, cells)

time: 158 us -> 158 us (level)
  no operation moved by 1% of the time
where the time goes in v8:
time: 158 us; the launch traced here: 157 us
  blocking collectives  85.6 us (54%)
  starting transfers between devices  30.6 us (19%)
  Pallas kernels  18.3 us (12%)
  waiting for transfers between devices  15.1 us (10%)
  local copies, waits for them, and re-layouts  6.88 us (4%)
    all_to_all x5, blocking collectives, exchange(): return lax.all_to_all(array, axes, 0, 0, tiled=True)  74.3 us
    all_to_all x1, starting transfers between devices, exchange(): return lax.all_to_all(array, axes, 0, 0, tiled=True)  18.2 us
    all_to_all x1, waiting for transfers between devices, exchange(): return lax.all_to_all(array, axes, 0, 0, tiled=True)  15 us
    all_gather x3, blocking collectives, both_cores(): return lax.all_gather(array, 'core')  11.4 us
    pallas_call x1, Pallas kernels, local(): call(second_body, (f32(WHOLE, LANES), f32(MEMBERS, LANES)), [pair, pltpu....  6.7 us
    unnamed x16, local copies, waits for them, and re-layouts  6.66 us
    ppermute x1, starting transfers between devices, local(): near_fields = lax.ppermute(near_fields, TILE, to_near)  5.58 us
    ppermute x1, starting transfers between devices, local(): near = lax.ppermute(near_edge, TILE, to_near)  5.57 us
  transfers between devices with their start and end apart: 5, of which 1 were waited for; matrix products, arithmetic and copies ran while one was open for 0% of the time, Pallas kernels for 2%

profile of v8, /device:TPU:1, one launch (start us, length us, event | category | flops | bytes accessed | tf_op | source)
XLA Modules:
  0.0 156.9 jit_solution(16745391050946181224)
XLA Ops:
  0.0 0.9 copy-done
  1.0 1.6 %shard_map.82 = f32[768,128]{1,0:T(8,128)} custom-call(f32[2,32,1024]{2,1,0:T(8,128)S(1)} %bitcast.19), custom_call_target="tpu_custom_call" | custom-call | tf_op jit(solution)/shard_map/pallas_call | solution.py:504
  2.6 18.2 %all-to-all-start = ((f32[64,3,4,128]{3,2,1,0:T(4,128)}), f32[64,3,4,128]{3,2,1,0:T(4,128)S(1)}, u32[]{:S(2)}, u32[]{:S(2)}) async-start(f32[64,3,4,128]{3,2,1,0:T(4,128)} %bitcast.2), calls=%async_computation | async-start | bytes 786432 | tf_op jit(solution)/shard_map/all_to_all | solution.py:481
  20.8 0.9 copy-done.1
  21.7 0.9 copy-done.2
  22.7 0.9 copy-done.3
  24.4 5.6 %collective-permute-start.1 = (f32[3,8,128]{2,1,0:T(8,128)S(1)}, f32[3,8,128]{2,1,0:T(8,128)S(1)}, u32[]{:S(2)}, u32[]{:S(2)}) collective-permute-start(f32[3,8,128]{2,1,0:T(8,128)S(1)} %get-tuple-element.27), channel_id=1, source_target_pairs={{0,1},{1,0},{2,3},{3,2},{4,5},{5,4},{6,7},{7,6},{8,9},{9,8},{10,11... | collective-permute-start | bytes 36872 | tf_op jit(solution)/shard_map/ppermute | solution.py:518
  30.7 0.7 copy-done.5
  32.2 0.7 copy-done.7
  33.6 15.0 %all-to-all-done = f32[64,3,4,128]{3,2,1,0:T(4,128)S(1)} async-done(((f32[64,3,4,128]{3,2,1,0:T(4,128)}), f32[64,3,4,128]{3,2,1,0:T(4,128)S(1)}, u32[]{:S(2)}, u32[]{:S(2)}) %all-to-all-start) | async-done | bytes 393248 | tf_op jit(solution)/shard_map/all_to_all | solution.py:481
  49.6 5.6 %collective-permute-start.3 = (f32[192,128]{1,0:T(8,128)S(1)}, f32[192,128]{1,0:T(8,128)S(1)}, u32[]{:S(2)}, u32[]{:S(2)}) collective-permute-start(f32[192,128]{1,0:T(8,128)S(1)} %get-tuple-element.30), channel_id=1, source_target_pairs={{0,1},{1,0},{2,3},{3,2},{4,5},{5,4},{6,7},{7,6},{8,9},{9,8},{10,11... | collective-permute-start | bytes 294920 | tf_op jit(solution)/shard_map/ppermute | solution.py:526
  55.2 2.8 %shard_map.86 = (f32[32,32,128]{2,1,0:T(8,128)S(1)}, f32[8,32,48,128]{3,2,1,0:T(8,128)S(1)}, f32[32,16,128]{2,1,0:T(8,128)S(1)}, f32[16,128]{1,0:T(8,128)S(1)}) custom-call(f32[768,128]{1,0:T(8,128)S(1)} %bitcast.17, f32[3,32,128]{2,1,0:T(8,128)S(1)} %get-tuple-element.33.fields_ref), custom_call_target="tpu_custom_call" | custom-call | tf_op jit(solution)/shard_map/pallas_call | solution.py:527
  58.0 2.5 %shard_map.87 = (f32[24,128]{1,0:T(8,128)S(1)}, f32[32,8,128]{2,1,0:T(8,128)S(1)}, f32[32,8,128]{2,1,0:T(8,128)S(1)}, f32[3,48,128]{2,1,0:T(8,128)S(1)}) custom-call(s32[1]{0:T(128)} %bitcast.even_ref, f32[192,128]{1,0:T(8,128)S(1)} %collective-permute-done.2.far_ref, f32[192,128]{1,0:T(8,128)S(1)} %collective-permute-done.3.near_ref, ...), custom_call_target="tpu_custom_call" | custom-call | tf_op jit(solution)/shard_map/pallas_call | solution.py:547
  60.6 15.5 %all_to_all.30 = f32[32,5,2,128]{3,2,1,0:T(2,128)S(1)} all-to-all(f32[32,5,2,128]{3,2,1,0:T(2,128)S(1)} %bitcast.28), channel_id=1, replica_groups=mesh['z'=16,'yl'=2,'core'=2,'yh'=2,'x'=4] {'yl','core','yh','x'}, dimensions={0} | all-to-all | bytes 327680 | tf_op jit(solution)/shard_map/all_to_all | solution.py:481
  76.2 14.3 %all_to_all.31 = f32[16,5,2,128]{3,2,1,0:T(2,128)S(1)} all-to-all(f32[16,5,2,128]{3,2,1,0:T(2,128)S(1)} %broadcast_in_dim.16), channel_id=1, replica_groups=mesh['z'=16,'yl'=2,'core'=2,'yh'=2,'x'=4] {'z'}, dimensions={0} | all-to-all | bytes 163840 | tf_op jit(solution)/shard_map/all_to_all | solution.py:481
  90.5 3.8 %all-gather = f32[32,128]{1,0:T(8,128)S(1)} all-gather(f32[16,128]{1,0:T(8,128)S(1)} %pad.7), channel_id=2, replica_groups=mesh['z'=16,'yl'=2,'core'=2,'yh'=2,'x'=4] {'core'}, dimensions={0}, use_global_device_ids=true | all-gather | bytes 24576 | tf_op jit(solution)/shard_map/all_gather | solution.py:489
  94.3 6.7 %shard_map.88 = (f32[24,128]{1,0:T(8,128)S(1)}, f32[64,128]{1,0:T(8,128)S(1)}) custom-call(f32[2,16,128]{2,1,0:T(8,128)S(1)} %bitcast.20, f32[32,8,128]{2,1,0:T(8,128)S(1)} %get-tuple-element.39.south_ref, f32[32,32,128]{2,1,0:T(8,128)S(1)} %get-tuple-element.40.mid_ref, f32[32,8,128]{2,1,0:T(8,128)S(1)} %get-tuple-element.41.north_ref, ...), custom_call_target="tpu_custom_call" | custom-call | tf_op jit(solution)/shard_map/pallas_call | solution.py:557
  101.1 11.5 %all_to_all.32 = f32[32,5,2,128]{3,2,1,0:T(2,128)S(1)} all-to-all(f32[32,5,2,128]{3,2,1,0:T(2,128)S(1)} %bitcast.29), channel_id=1, replica_groups=mesh['z'=16,'yl'=2,'core'=2,'yh'=2,'x'=4] {'yl','core','yh','x'}, dimensions={0} | all-to-all | bytes 327680 | tf_op jit(solution)/shard_map/all_to_all | solution.py:481
  112.7 14.8 %all_to_all.33 = f32[16,5,2,128]{3,2,1,0:T(2,128)S(1)} all-to-all(f32[16,5,2,128]{3,2,1,0:T(2,128)S(1)} %broadcast_in_dim.37), channel_id=1, replica_groups=mesh['z'=16,'yl'=2,'core'=2,'yh'=2,'x'=4] {'z'}, dimensions={0} | all-to-all | bytes 163840 | tf_op jit(solution)/shard_map/all_to_all | solution.py:481
  127.5 3.8 %all-gather.1 = f32[32,128]{1,0:T(8,128)S(1)} all-gather(f32[16,128]{1,0:T(8,128)S(1)} %pad.8), channel_id=3, replica_groups=mesh['z'=16,'yl'=2,'core'=2,'yh'=2,'x'=4] {'core'}, dimensions={0}, use_global_device_ids=true | all-gather | bytes 24576 | tf_op jit(solution)/shard_map/all_gather | solution.py:489
  131.3 2.6 %shard_map.89 = f32[8,128]{1,0:T(8,128)S(1)} custom-call(f32[2,16,128]{2,1,0:T(8,128)S(1)} %bitcast.21, f32[64,128]{1,0:T(8,128)S(1)} %get-tuple-element.44.weights_ref, f32[32,32,128]{2,1,0:T(8,128)S(1)} %get-tuple-element.40.mid_ref), custom_call_target="tpu_custom_call" | custom-call | tf_op jit(solution)/shard_map/pallas_call | solution.py:563
  134.0 18.2 %all_to_all.34 = f32[32,8,128]{2,1,0:T(8,128)S(1)} all-to-all(f32[32,8,128]{2,1,0:T(8,128)S(1)} %broadcast_in_dim.38), channel_id=1, replica_groups=mesh['z'=16,'yl'=2,'core'=2,'yh'=2,'x'=4] {'z','yl'}, dimensions={0} | all-to-all | bytes 262144 | tf_op jit(solution)/shard_map/all_to_all | solution.py:481
  152.2 3.8 %all-gather.2 = f32[64,8,128]{2,1,0:T(8,128)S(1)} all-gather(f32[32,8,128]{2,1,0:T(8,128)S(1)} %all_to_all.34), channel_id=4, replica_groups=mesh['z'=16,'yl'=2,'core'=2,'yh'=2,'x'=4] {'core'}, dimensions={0}, use_global_device_ids=true | all-gather | bytes 393216 | tf_op jit(solution)/shard_map/all_gather | solution.py:489
  156.0 1.0 shard_map.90
  (34 shorter events, 4.3 us)
Async XLA Ops:
  0.0 0.9 copy-start
  2.6 46.1 %all-to-all-start = ((f32[64,3,4,128]{3,2,1,0:T(4,128)}), f32[64,3,4,128]{3,2,1,0:T(4,128)S(1)}, u32[]{:S(2)}, u32[]{:S(2)}) async-start(f32[64,3,4,128]{3,2,1,0:T(4,128)} %bitcast.2), calls=%async_computation | async-start | bytes 786432 | tf_op jit(solution)/shard_map/all_to_all | solution.py:481
  20.8 1.0 copy-start.1
  21.7 0.9 copy-start.2
  22.7 0.9 copy-start.3
  23.8 9.8 %collective-permute-start = (f32[3,8,128]{2,1,0:T(8,128)S(1)}, f32[3,8,128]{2,1,0:T(8,128)S(1)}, u32[]{:S(2)}, u32[]{:S(2)}) collective-permute-start(f32[3,8,128]{2,1,0:T(8,128)S(1)} %get-tuple-element.26), channel_id=1, source_target_pairs={{1,2},{2,1},{3,4},{4,3},{5,6},{6,5},{9,10},{10,9},{11,12},{12,11},... | collective-permute-start | bytes 36872 | tf_op jit(solution)/shard_map/ppermute | solution.py:517
  24.4 9.1 %collective-permute-start.1 = (f32[3,8,128]{2,1,0:T(8,128)S(1)}, f32[3,8,128]{2,1,0:T(8,128)S(1)}, u32[]{:S(2)}, u32[]{:S(2)}) collective-permute-start(f32[3,8,128]{2,1,0:T(8,128)S(1)} %get-tuple-element.27), channel_id=1, source_target_pairs={{0,1},{1,0},{2,3},{3,2},{4,5},{5,4},{6,7},{7,6},{8,9},{9,8},{10,11... | collective-permute-start | bytes 36872 | tf_op jit(solution)/shard_map/ppermute | solution.py:518
  30.0 0.7 copy-start.4
  30.7 0.7 copy-start.5
  31.5 0.7 copy-start.6
  32.2 0.7 copy-start.7
  48.9 9.1 %collective-permute-start.2 = (f32[192,128]{1,0:T(8,128)S(1)}, f32[192,128]{1,0:T(8,128)S(1)}, u32[]{:S(2)}, u32[]{:S(2)}) collective-permute-start(f32[192,128]{1,0:T(8,128)S(1)} %get-tuple-element.29), channel_id=1, source_target_pairs={{1,2},{2,1},{3,4},{4,3},{5,6},{6,5},{9,10},{10,9},{11,12},{12,11},... | collective-permute-start | bytes 294920 | tf_op jit(solution)/shard_map/ppermute | solution.py:525
  49.6 8.4 %collective-permute-start.3 = (f32[192,128]{1,0:T(8,128)S(1)}, f32[192,128]{1,0:T(8,128)S(1)}, u32[]{:S(2)}, u32[]{:S(2)}) collective-permute-start(f32[192,128]{1,0:T(8,128)S(1)} %get-tuple-element.30), channel_id=1, source_target_pairs={{0,1},{1,0},{2,3},{3,2},{4,5},{5,4},{6,7},{7,6},{8,9},{9,8},{10,11... | collective-permute-start | bytes 294920 | tf_op jit(solution)/shard_map/ppermute | solution.py:526
